TPU v7x, 32 devices: a whole 2x2x4 slice. The times are simulated.
32 devices in a mesh: dp: 16 (over z, y, x), opt: 2 (over core).
Axes of the slice: x: 2, y: 2, z: 4, core: 2. Of those that a mesh axis runs over, the one named last changes fastest.
Arguments:
- enc_in: bfloat16 [49152, 768], P(('dp', 'opt')), may hold values from -6 to 6
- enc_cot: bfloat16 [49152, 768], P(('dp', 'opt')), may hold values from -0.59765625 to 0.59765625
- dec_in: bfloat16 [640, 768], P(('dp', 'opt')), may hold values from -6 to 6
- dec_cot: bfloat16 [640, 768], P(('dp', 'opt')), may hold values from -6 to 6
- passage_lengths: int32 [96], P(('dp', 'opt')), may hold values from 250 to 500, as said below
- passage_example: int32 [96], P(('dp', 'opt')), may hold values from 0 to 31, as said below
- answer_tokens: int32 [32, 20], P(('dp', 'opt')), may hold values from 0 to 32127, as said below
- owner_slot: int32 [1008], replicated, may hold values from 0 to 1023, as said below
- master: float32 [1024, 128, 128], P(('dp', 'opt'))
- kron_stats: float32 [1024, 2, 128, 128], P(('dp', 'opt'))
- inverse_roots: float32 [1024, 2, 128, 128], P(('dp', 'opt'))
- small_params: float32 [5376], P(('dp', 'opt'))
- small_moment: float32 [5376], P(('dp', 'opt')), may hold values from -9.797959 to 9.797959
Outputs:
- dec_out: bfloat16 [640, 768], P(('dp', 'opt'))
- encodings: bfloat16 [49152, 768], P(('dp', 'opt'))
- enc_in_grad: float32 [49152, 768], P(('dp', 'opt'))
- dec_in_grad: float32 [640, 768], P(('dp', 'opt'))
- block_grads: float32 [1024, 128, 128], P(('dp', 'opt'))
- new_stats: float32 [1024, 2, 128, 128], P(('dp', 'opt'))
- new_master: float32 [1024, 128, 128], P(('dp', 'opt'))
- small_grads: float32 [5376], P(('dp', 'opt'))
- new_moment: float32 [5376], P(('dp', 'opt'))
- new_small: float32 [5376], P(('dp', 'opt'))
Inputs may be any that keep to these rules, and one draw needn't show every extreme that they name: `passage_lengths`: each length is 250 or 500; the first passage has 500 tokens and the second 250. `passage_example`: devices are numbered dp-major (index dp times the opt size plus opt); example e belongs to device e. A passage on device (a, o) belongs to an example of device (b, o) with k = (a - b) mod the dp size below 3; every example has exactly one passage with each k, and its passages are ordered by k. `answer_tokens`: ids of 1 to 32127, then 0 to the end of the row; every answer has one token or more, the first one 20. `owner_slot`: distinct slots; slot s belongs to device s // 32, devices numbered dp-major.
All inputs are finite; a program needn't handle non-finite values.
Results may differ from a plain program's by a relative error of at most 0.018.
Values may be sent and summed in bfloat16 or wider, within the bound.
A program may use at most 448 MiB of HBM per device.

v0:
```python
import jax
import jax.numpy as jnp
import numpy as np
from jax import lax
from jax.sharding import PartitionSpec as P

D = 768
H = 12
HD = 64
FF = 3072
NB = 32
MAXD = 128
BLK = 128
PASS_SLOT = 512
PASS_EX = 3
ALEN = 20
EX_DEV = 1


exact_prec = lax.Precision.HIGHEST
neg_fill = -1000000000.0
stat_decay = 0.95
block_rate = 0.5
moment_decay = 0.9
small_rate = 0.002


def passed_along(shard, axis, by):
    size = lax.axis_size(axis)
    return lax.ppermute(shard, axis, [(i, (i + by) % size) for i in range(size)])


def to_low(values):
    return values.astype(jnp.bfloat16)


def matmul(left, right):
    return jnp.dot(left, right, preferred_element_type=jnp.float32)


def weight_grad(rows_in, grads):
    return lax.dot_general(
        rows_in, grads, (((0,), (0,)), ((), ())), preferred_element_type=jnp.float32
    )


def rows_grad(grads, weight):
    return lax.dot_general(
        grads, weight, (((1,), (1,)), ((), ())), preferred_element_type=jnp.float32
    )


def bucket_index(length, both_sides):
    offsets = np.arange(-(length - 1), length)
    if both_sides:
        halves = NB // 2
        bucket_base = (offsets > 0) * halves
        distance = np.abs(offsets)
    else:
        halves = NB
        bucket_base = offsets * 0
        distance = np.maximum(-offsets, 0)
    exact_count = halves // 2
    widened = np.maximum(distance, 1) * 1.0
    far_bucket = exact_count + np.floor(
        np.log(widened / exact_count) / np.log(MAXD / exact_count) * (halves - exact_count)
    ).astype(np.int32)
    far_bucket = np.minimum(far_bucket, halves - 1)
    return (bucket_base + np.where(distance < exact_count, distance, far_bucket)).astype(np.int32)


def bucket_onehot(length, both_sides):
    return jnp.asarray(
        (bucket_index(length, both_sides)[:, None] == np.arange(NB)[None, :]).astype(np.float32)
    )


def bias_offsets(bias_table, length, both_sides):
    return jnp.dot(
        bias_table.T,
        bucket_onehot(length, both_sides).T,
        precision=exact_prec,
        preferred_element_type=jnp.float32,
    )


def spread_offsets(offset_bias, length):
    head_count = offset_bias.shape[0]
    tiled_rows = jnp.broadcast_to(offset_bias[:, None, :], (head_count, length, 2 * length - 1))
    flattened = tiled_rows.reshape(head_count, length * (2 * length - 1))
    flattened = jnp.concatenate([flattened, jnp.zeros((head_count, length), jnp.float32)], axis=1)
    return flattened.reshape(head_count, length, 2 * length)[:, ::-1, :length]


def collapse_offsets(bias_total, length):
    head_count = bias_total.shape[0]
    flipped = bias_total[:, ::-1, :]
    padded = jnp.concatenate(
        [flipped, jnp.zeros((head_count, length, length), jnp.float32)], axis=2
    ).reshape(head_count, 2 * length * length)
    trimmed = padded[:, : length * (2 * length - 1)].reshape(head_count, length, 2 * length - 1)
    return jnp.sum(trimmed, axis=1)


def table_grad(bias_total, length, both_sides):
    return jnp.dot(
        bucket_onehot(length, both_sides).T,
        collapse_offsets(bias_total, length).T,
        precision=exact_prec,
        preferred_element_type=jnp.float32,
    )


def rms_scale(values, norm_gain):
    return values * lax.rsqrt(jnp.mean(values * values, axis=-1, keepdims=True) + 1e-06) * norm_gain


def smooth_gate(inner_act):
    return jax.nn.gelu(inner_act, approximate=True)


def norm_back(values, norm_gain, upstream):
    result, pullback = jax.vjp(rms_scale, values, norm_gain)
    return pullback(upstream)


def gate_back(inner_act, upstream):
    result, pullback = jax.vjp(smooth_gate, inner_act)
    return pullback(upstream)[0]


def matrix_shapes():
    square = (D, D)
    return [
        square,
        square,
        square,
        square,
        (D, FF),
        (FF, D),
        square,
        square,
        square,
        square,
        square,
        square,
        square,
        square,
        (D, FF),
        (FF, D),
    ]


def assemble(ordered):
    matrices = []
    first_block = 0
    for rows_in, cols_out in matrix_shapes():
        block_count = rows_in // BLK * (cols_out // BLK)
        block_grid = ordered[first_block : first_block + block_count].reshape(
            rows_in // BLK, cols_out // BLK, BLK, BLK
        )
        matrices.append(block_grid.transpose(0, 2, 1, 3).reshape(rows_in, cols_out))
        first_block = first_block + block_count
    return matrices


def to_blocks(matrices):
    pieces = []
    for matrix in matrices:
        rows_in, cols_out = matrix.shape
        block_grid = matrix.reshape(rows_in // BLK, BLK, cols_out // BLK, BLK).transpose(0, 2, 1, 3)
        pieces.append(block_grid.reshape(-1, BLK, BLK))
    return jnp.concatenate(pieces, axis=0)


def attend_forward(queries, key_rows, value_rows, score_bias, pair_valid):
    scores = (
        jnp.einsum("rhe,che->hrc", queries, key_rows, preferred_element_type=jnp.float32)
        + score_bias
    )
    scores = jnp.where(pair_valid[None], scores, neg_fill)
    peak = jnp.max(scores, axis=-1, keepdims=True)
    expos = jnp.exp(scores - peak)
    totals = jnp.sum(expos, axis=-1, keepdims=True)
    weights = to_low(expos / totals)
    mixed_heads = jnp.einsum(
        "hrc,che->rhe", weights, value_rows, preferred_element_type=jnp.float32
    )
    return (to_low(mixed_heads), peak + jnp.log(totals))


def attend_back(queries, key_rows, value_rows, score_bias, pair_valid, log_total, mixed_grad):
    scores = (
        jnp.einsum("rhe,che->hrc", queries, key_rows, preferred_element_type=jnp.float32)
        + score_bias
    )
    scores = jnp.where(pair_valid[None], scores, neg_fill)
    probs = jnp.exp(scores - log_total)
    prob_grad = jnp.einsum(
        "rhe,che->hrc", mixed_grad, value_rows, preferred_element_type=jnp.float32
    )
    score_grad = to_low(probs * (prob_grad - jnp.sum(probs * prob_grad, axis=-1, keepdims=True)))
    value_grad = to_low(
        jnp.einsum("hrc,rhe->che", to_low(probs), mixed_grad, preferred_element_type=jnp.float32)
    )
    query_grad = to_low(
        jnp.einsum("hrc,che->rhe", score_grad, key_rows, preferred_element_type=jnp.float32)
    )
    key_grad = to_low(
        jnp.einsum("hrc,rhe->che", score_grad, queries, preferred_element_type=jnp.float32)
    )
    return (query_grad, key_grad, value_grad, score_grad)


def encode(matrices, norm_gains, score_bias, enc_rows, key_valid):
    passages, slot_rows = key_valid.shape
    heads_shape = (passages, slot_rows, H, HD)
    inputs = enc_rows.astype(jnp.float32)
    normed = to_low(rms_scale(inputs, norm_gains[0]))
    queries = to_low(matmul(normed, matrices[0]))
    key_rows = to_low(matmul(normed, matrices[1]))
    value_rows = to_low(matmul(normed, matrices[2]))

    def one_passage(operands):
        pair_valid = jnp.broadcast_to(operands[3][None, :], (slot_rows, slot_rows))
        return attend_forward(operands[0], operands[1], operands[2], score_bias, pair_valid)

    mixed_heads, log_total = lax.map(
        one_passage,
        (
            queries.reshape(heads_shape),
            key_rows.reshape(heads_shape),
            value_rows.reshape(heads_shape),
            key_valid,
        ),
    )
    mixed_heads = mixed_heads.reshape(passages * slot_rows, D)
    hidden = inputs + matmul(mixed_heads, matrices[3])
    normed_two = to_low(rms_scale(hidden, norm_gains[1]))
    inner_act = matmul(normed_two, matrices[4])
    gated_act = to_low(smooth_gate(inner_act))
    output = hidden + matmul(gated_act, matrices[5])
    encoded = to_low(rms_scale(output, norm_gains[2]))
    return (
        encoded,
        (
            inputs,
            normed,
            queries,
            key_rows,
            value_rows,
            mixed_heads,
            log_total,
            hidden,
            normed_two,
            inner_act,
            gated_act,
            output,
        ),
    )


def encode_back(matrices, norm_gains, score_bias, key_valid, saved, encoded_grad):
    (
        inputs,
        normed,
        queries,
        key_rows,
        value_rows,
        mixed_heads,
        log_total,
        hidden,
        normed_two,
        inner_act,
        gated_act,
        output,
    ) = saved
    passages, slot_rows = key_valid.shape
    heads_shape = (passages, slot_rows, H, HD)
    output_grad, final_gain = norm_back(output, norm_gains[2], encoded_grad)
    branch_grad = to_low(output_grad)
    grad_down = weight_grad(gated_act, branch_grad)
    inner_grad = to_low(gate_back(inner_act, rows_grad(branch_grad, matrices[5])))
    grad_up = weight_grad(normed_two, inner_grad)
    hidden_part, second_gain = norm_back(hidden, norm_gains[1], rows_grad(inner_grad, matrices[4]))
    hidden_grad = output_grad + hidden_part
    attn_grad = to_low(hidden_grad)
    grad_out = weight_grad(mixed_heads, attn_grad)
    mixed_grad = to_low(rows_grad(attn_grad, matrices[3]))

    def one_passage(bias_total, operands):
        pair_valid = jnp.broadcast_to(operands[3][None, :], (slot_rows, slot_rows))
        query_grad, key_grad, value_grad, score_grad = attend_back(
            operands[0], operands[1], operands[2], score_bias, pair_valid, operands[4], operands[5]
        )
        return (bias_total + score_grad.astype(jnp.float32), (query_grad, key_grad, value_grad))

    bias_total, grads = lax.scan(
        one_passage,
        jnp.zeros((H, slot_rows, slot_rows), jnp.float32),
        (
            queries.reshape(heads_shape),
            key_rows.reshape(heads_shape),
            value_rows.reshape(heads_shape),
            key_valid,
            log_total,
            mixed_grad.reshape(heads_shape),
        ),
    )
    query_grad = grads[0].reshape(passages * slot_rows, D)
    key_grad = grads[1].reshape(passages * slot_rows, D)
    value_grad = grads[2].reshape(passages * slot_rows, D)
    grad_query = weight_grad(normed, query_grad)
    grad_key = weight_grad(normed, key_grad)
    grad_value = weight_grad(normed, value_grad)
    normed_grad = (
        rows_grad(query_grad, matrices[0])
        + rows_grad(key_grad, matrices[1])
        + rows_grad(value_grad, matrices[2])
    )
    input_part, first_gain = norm_back(inputs, norm_gains[0], normed_grad)
    return (
        hidden_grad + input_part,
        [grad_query, grad_key, grad_value, grad_out, grad_up, grad_down],
        [first_gain, second_gain, final_gain],
        bias_total,
    )


def decode(matrices, norm_gains, score_bias, dec_rows, memory, memory_valid):
    examples, memory_len = memory_valid.shape
    self_shape = (examples, ALEN, H, HD)
    memory_shape = (examples, memory_len, H, HD)
    inputs = dec_rows.astype(jnp.float32)
    normed = to_low(rms_scale(inputs, norm_gains[3]))
    queries = to_low(matmul(normed, matrices[6])).reshape(self_shape)
    key_rows = to_low(matmul(normed, matrices[7])).reshape(self_shape)
    value_rows = to_low(matmul(normed, matrices[8])).reshape(self_shape)
    causal = jnp.arange(ALEN)[:, None] >= jnp.arange(ALEN)[None, :]
    mixed_heads, self_total = jax.vmap(attend_forward, in_axes=(0, 0, 0, None, None))(
        queries, key_rows, value_rows, score_bias, causal
    )
    mixed_heads = mixed_heads.reshape(examples * ALEN, D)
    first = inputs + matmul(mixed_heads, matrices[9])
    normed_two = to_low(rms_scale(first, norm_gains[4]))
    cross_queries = to_low(matmul(normed_two, matrices[10])).reshape(self_shape)
    memory_rows = memory.reshape(examples * memory_len, D)
    cross_keys = to_low(matmul(memory_rows, matrices[11])).reshape(memory_shape)
    cross_values = to_low(matmul(memory_rows, matrices[12])).reshape(memory_shape)
    cross_valid = jnp.broadcast_to(memory_valid[:, None, :], (examples, ALEN, memory_len))
    cross_heads, cross_total = jax.vmap(attend_forward, in_axes=(0, 0, 0, None, 0))(
        cross_queries, cross_keys, cross_values, 0.0, cross_valid
    )
    cross_heads = cross_heads.reshape(examples * ALEN, D)
    second = first + matmul(cross_heads, matrices[13])
    normed_three = to_low(rms_scale(second, norm_gains[5]))
    inner_act = matmul(normed_three, matrices[14])
    gated_act = to_low(smooth_gate(inner_act))
    output = second + matmul(gated_act, matrices[15])
    return (
        output,
        (
            inputs,
            normed,
            queries,
            key_rows,
            value_rows,
            self_total,
            mixed_heads,
            first,
            normed_two,
            cross_queries,
            memory_rows,
            cross_keys,
            cross_values,
            cross_valid,
            cross_total,
            cross_heads,
            second,
            normed_three,
            inner_act,
            gated_act,
        ),
    )


def decode_back(matrices, norm_gains, score_bias, saved, output_grad):
    (
        inputs,
        normed,
        queries,
        key_rows,
        value_rows,
        self_total,
        mixed_heads,
        first,
        normed_two,
        cross_queries,
        memory_rows,
        cross_keys,
        cross_values,
        cross_valid,
        cross_total,
        cross_heads,
        second,
        normed_three,
        inner_act,
        gated_act,
    ) = saved
    examples, memory_len = (cross_keys.shape[0], cross_keys.shape[1])
    self_shape = (examples, ALEN, H, HD)
    causal = jnp.arange(ALEN)[:, None] >= jnp.arange(ALEN)[None, :]
    branch_grad = to_low(output_grad)
    grad_down = weight_grad(gated_act, branch_grad)
    inner_grad = to_low(gate_back(inner_act, rows_grad(branch_grad, matrices[15])))
    grad_up = weight_grad(normed_three, inner_grad)
    second_part, third_gain = norm_back(second, norm_gains[5], rows_grad(inner_grad, matrices[14]))
    second_grad = output_grad + second_part
    cross_out = to_low(second_grad)
    grad_cross_out = weight_grad(cross_heads, cross_out)
    cross_mixed = to_low(rows_grad(cross_out, matrices[13])).reshape(self_shape)
    cross_query_grad, cross_key_grad, cross_value_grad, unused = jax.vmap(
        attend_back, in_axes=(0, 0, 0, None, 0, 0, 0)
    )(cross_queries, cross_keys, cross_values, 0.0, cross_valid, cross_total, cross_mixed)
    cross_query_grad = cross_query_grad.reshape(examples * ALEN, D)
    cross_key_grad = cross_key_grad.reshape(examples * memory_len, D)
    cross_value_grad = cross_value_grad.reshape(examples * memory_len, D)
    grad_cross_query = weight_grad(normed_two, cross_query_grad)
    grad_cross_key = weight_grad(memory_rows, cross_key_grad)
    grad_cross_value = weight_grad(memory_rows, cross_value_grad)
    memory_grad = to_low(
        rows_grad(cross_key_grad, matrices[11]) + rows_grad(cross_value_grad, matrices[12])
    )
    first_part, second_gain = norm_back(
        first, norm_gains[4], rows_grad(cross_query_grad, matrices[10])
    )
    first_grad = second_grad + first_part
    self_out = to_low(first_grad)
    grad_self_out = weight_grad(mixed_heads, self_out)
    self_mixed = to_low(rows_grad(self_out, matrices[9])).reshape(self_shape)
    query_grad, key_grad, value_grad, self_scores = jax.vmap(
        attend_back, in_axes=(0, 0, 0, None, None, 0, 0)
    )(queries, key_rows, value_rows, score_bias, causal, self_total, self_mixed)
    bias_total = jnp.sum(self_scores.astype(jnp.float32), axis=0)
    query_grad = query_grad.reshape(examples * ALEN, D)
    key_grad = key_grad.reshape(examples * ALEN, D)
    value_grad = value_grad.reshape(examples * ALEN, D)
    grad_query = weight_grad(normed, query_grad)
    grad_key = weight_grad(normed, key_grad)
    grad_value = weight_grad(normed, value_grad)
    normed_grad = (
        rows_grad(query_grad, matrices[6])
        + rows_grad(key_grad, matrices[7])
        + rows_grad(value_grad, matrices[8])
    )
    input_part, first_gain = norm_back(inputs, norm_gains[3], normed_grad)
    weight_list = [
        grad_query,
        grad_key,
        grad_value,
        grad_self_out,
        grad_cross_query,
        grad_cross_key,
        grad_cross_value,
        grad_cross_out,
        grad_up,
        grad_down,
    ]
    return (
        first_grad + input_part,
        weight_list,
        [first_gain, second_gain, third_gain],
        bias_total,
        memory_grad,
    )


def per_device(
    enc_in,
    enc_cot,
    dec_in,
    dec_cot,
    passage_lengths,
    passage_example,
    answer_tokens,
    owner_slot,
    master,
    kron_stats,
    inverse_roots,
    small_params,
    small_moment,
):
    dp_count = lax.axis_size("dp")
    pair_count = lax.axis_size("opt")
    slot_dev = master.shape[0]
    slot_total = dp_count * pair_count * slot_dev
    gathered, small_all = (
        lax.all_gather(to_low(master), ("dp", "opt"), axis=0, tiled=True),
        lax.all_gather(to_low(small_params), ("dp", "opt"), axis=0, tiled=True),
    )
    matrices = assemble(gathered[owner_slot])
    small_float = small_all.astype(jnp.float32)
    norm_gains = [small_float[gain_index * D : (gain_index + 1) * D] for gain_index in range(6)]
    table_size = NB * H
    enc_bias = spread_offsets(
        bias_offsets(small_float[6 * D : 6 * D + table_size].reshape(NB, H), PASS_SLOT, True),
        PASS_SLOT,
    )
    dec_bias = spread_offsets(
        bias_offsets(small_float[6 * D + table_size :].reshape(NB, H), ALEN, False), ALEN
    )
    passages = passage_lengths.shape[0]
    key_valid = jnp.arange(PASS_SLOT)[None, :] < passage_lengths[:, None]
    encoded, saved = encode(matrices, norm_gains, enc_bias, enc_in, key_valid)
    owner_dp = passage_example // EX_DEV // pair_count
    target = (lax.axis_index("dp") - owner_dp) % dp_count * EX_DEV + passage_example % EX_DEV
    chooser = (target[None, :] == jnp.arange(passages)[:, None]).astype(jnp.bfloat16)
    send_rows = to_low(matmul(chooser, encoded.reshape(passages, PASS_SLOT * D)))
    send_valid = to_low(matmul(chooser, key_valid.astype(jnp.bfloat16)))
    memory_parts = [send_rows[0:EX_DEV]]
    valid_parts = [send_valid[0:EX_DEV]]
    for offset in range(1, PASS_EX):
        moved_rows, moved_valid = passed_along(
            (
                send_rows[offset * EX_DEV : (offset + 1) * EX_DEV],
                send_valid[offset * EX_DEV : (offset + 1) * EX_DEV],
            ),
            "dp",
            -offset,
        )
        memory_parts.append(moved_rows)
        valid_parts.append(moved_valid)
    memory = jnp.stack(memory_parts, axis=1).reshape(EX_DEV, PASS_EX * PASS_SLOT, D)
    memory_valid = jnp.stack(valid_parts, axis=1).reshape(EX_DEV, PASS_EX * PASS_SLOT) > 0.5
    dec_out, dec_saved = decode(matrices, norm_gains, dec_bias, dec_in, memory, memory_valid)
    answer_valid = (answer_tokens != 0).reshape(-1, 1).astype(jnp.float32)
    dec_in_grad, dec_grads, dec_gains, dec_bias_total, memory_grad = decode_back(
        matrices, norm_gains, dec_bias, dec_saved, dec_cot.astype(jnp.float32) * answer_valid
    )
    memory_grad = memory_grad.reshape(EX_DEV, PASS_EX, PASS_SLOT * D)
    back_parts = [memory_grad[:, 0]]
    for offset in range(1, PASS_EX):
        back_parts.append(passed_along(memory_grad[:, offset], "dp", offset))
    returned = jnp.concatenate(back_parts, axis=0)
    cross_grad = lax.dot_general(
        chooser, returned, (((0,), (0,)), ((), ())), preferred_element_type=jnp.float32
    )
    row_valid = key_valid.reshape(-1, 1).astype(jnp.float32)
    encoded_grad = (
        cross_grad.reshape(passages * PASS_SLOT, D) + enc_cot.astype(jnp.float32) * row_valid
    )
    enc_in_grad, enc_grads, enc_gains, enc_bias_total = encode_back(
        matrices, norm_gains, enc_bias, key_valid, saved, encoded_grad
    )
    block_terms = to_blocks(enc_grads + dec_grads)
    small_terms = jnp.concatenate(
        enc_gains
        + dec_gains
        + [
            table_grad(enc_bias_total, PASS_SLOT, True).reshape(-1),
            table_grad(dec_bias_total, ALEN, False).reshape(-1),
        ]
    )
    grad_slots = jnp.zeros((slot_total, BLK, BLK), jnp.float32).at[owner_slot].set(block_terms)
    block_sum, small_grads = (
        lax.psum_scatter(grad_slots, ("dp", "opt"), scatter_dimension=0, tiled=True),
        lax.psum_scatter(small_terms, ("dp", "opt"), scatter_dimension=0, tiled=True),
    )
    left_gram = jnp.einsum("sij,skj->sik", block_sum, block_sum, precision=exact_prec)
    right_gram = jnp.einsum("sji,sjk->sik", block_sum, block_sum, precision=exact_prec)
    new_stats = stat_decay * kron_stats + (1.0 - stat_decay) * jnp.stack(
        [left_gram, right_gram], axis=1
    )
    shaped = jnp.einsum("sij,sjk->sik", inverse_roots[:, 0], block_sum, precision=exact_prec)
    shaped = jnp.einsum("sij,sjk->sik", shaped, inverse_roots[:, 1], precision=exact_prec)
    shaped_rms = jnp.sqrt(jnp.mean(shaped * shaped, axis=(1, 2), keepdims=True) + 1e-06)
    weight_rms = jnp.sqrt(jnp.mean(master * master, axis=(1, 2), keepdims=True) + 1e-06)
    new_master = master - block_rate * weight_rms * shaped / shaped_rms
    new_moment = moment_decay * small_moment + small_grads
    new_small = small_params - small_rate * new_moment
    return (
        dec_out.astype(jnp.bfloat16),
        encoded,
        enc_in_grad,
        dec_in_grad,
        block_sum,
        new_stats,
        new_master,
        small_grads,
        new_moment,
        new_small,
    )


def solution(mesh):
    placed = (
        P(("dp", "opt"), None),
        P(("dp", "opt"), None),
        P(("dp", "opt"), None),
        P(("dp", "opt"), None),
        P(("dp", "opt")),
        P(("dp", "opt")),
        P(("dp", "opt"), None),
        P(),
        P(("dp", "opt"), None, None),
        P(("dp", "opt"), None, None, None),
        P(("dp", "opt"), None, None, None),
        P(("dp", "opt")),
        P(("dp", "opt")),
    )
    return jax.shard_map(
        per_device,
        mesh=mesh,
        in_specs=placed,
        out_specs=(
            P(("dp", "opt"), None),
            P(("dp", "opt"), None),
            P(("dp", "opt"), None),
            P(("dp", "opt"), None),
            P(("dp", "opt"), None, None),
            P(("dp", "opt"), None, None, None),
            P(("dp", "opt"), None, None),
            P(("dp", "opt")),
            P(("dp", "opt")),
            P(("dp", "opt")),
        ),
        check_vma=False,
    )
```

profile of v0, /device:TPU:0, one launch (start us, length us, event | category | flops | bytes accessed | tf_op | source)
XLA Modules:
  0.0 2063.2 jit_solution(14917181217994221228)
XLA Ops:
  19.5 38.9 %all-reduce.4 = bf16[5376]{0:T(1024)(128)(2,1)S(1)} all-reduce(bf16[5376]{0:T(1024)(128)(2,1)S(1)} %dynamic-update-slice), channel_id=1, replica_groups=mesh['dp'=16,'opt'=2] {'dp','opt'}, use_global_device_ids=true, to_apply=%add.4 | all-reduce | flops 5376 | bytes 21504
  83.9 38.4 %reshape.742 = f32[12,523776]{1,0:T(8,128)} reshape(f32[12,512,1023]{2,1,0:T(8,128)} %broadcast_in_dim.100) | data formatting | bytes 50282496 | tf_op jit(solution)/shard_map/reshape | solution.py:90
  134.4 36.1 %copy.416 = f32[2,8,512,1024]{3,2,1,0:T(8,128)} copy(f32[2,8,512,1024]{3,1,2,0:T(8,128)S(1)} %bitcast.637) | data formatting | bytes 67108864
  182.0 96.1 %rev.13 = f32[12,512,512]{2,1,0:T(8,128)} reverse(f32[12,512,512]{2,1,0:T(8,128)} %slice.186), dimensions={1} | reverse | bytes 25165824 | tf_op jit(solution)/shard_map/rev | solution.py:92
  291.4 36.4 %gather_fusion = bf16[1008,128,128]{2,1,0:T(8,128)(2,1)} fusion(bf16[1024,128,128]{2,1,0:T(8,128)(2,1)} %all-gather.2.cloned.1.call-done, s32[1024]{0:T(1024)S(1)} %pad_clamp_fusion), kind=kCustom, calls=%fused_computation | custom fusion | bytes 66064320 | tf_op jit(solution)/shard_map/gather | solution.py:501
  337.6 15.8 fusion.308
  444.8 39.3 %while.29 = (s32[]{:T(128)}, bf16[3,512,12,64]{1,3,2,0:T(8,128)(2,1)}, f32[3,12,512,1]{2,1,3,0:T(8,128)}, bf16[3,512,12,64]{1,3,2,0:T(8,128)(2,1)}, pred[3,512]{...) while((s32[]{:T(128)}, ...), condition=%wide.region_7.8_spmd, body=%wide.region_4.7_spmd.sunk | while | flops 830859264 | bytes 53685868 | solution.py:228
  506.4 13.9 multiply_reduce_fusion.5
  573.4 30.8 %collective-permute-done = bf16[1,393216]{1,0:T(2,128)(2,1)} collective-permute-done((bf16[1,393216]{1,0:T(2,128)(2,1)S(1)}, bf16[1,393216]{1,0:T(2,128)(2,1)}, u32[]{:S(2)}, u32[]{:S(2)}) %collective-permute-start) | collective-permute-done | bytes 786464 | tf_op jit(solution)/shard_map/ppermute | solution.py:30
  748.2 17.2 collective-permute-done.5
  805.4 24.7 %fusion.54 = bf16[1536,3072]{1,0:T(8,128)(2,1)} fusion(f32[1536,3072]{1,0:T(8,128)} %fusion.79, bf16[96,8,24,128]{3,2,1,0:T(8,128)(2,1)S(1)} %bitcast.715, f32[1536,768]{0,1:T(8,128)S(1)} %add_add_fusion.2), kind=kOutput, calls=%fused_computation.66 | convolution fusion | flops 7343308800 | bytes 37748736 | tf_op jit(solution)/shard_map/dot_general | solution.py:48
  841.6 15.6 multiply_reduce_fusion.2
  927.5 135.8 %while.30 = (s32[]{:T(128)}, f32[12,512,512]{1,2,0:T(8,128)}, bf16[3,512,12,64]{1,3,2,0:T(8,128)(2,1)}, bf16[3,512,12,64]{1,3,2,0:T(8,128)(2,1)}, bf16[3,512,12,...) while((s32[]{:T(128)}, f32[12,512,512]{1,2,0:T(8,128)}, ...), condition=%wide.region_20.21_spmd.clone, body=%wide.region_18.20_spmd.clone.sunk | while | flops 2052188160 | bytes 158989024 | solution.py:298
  993.3 15.9 select_add_fusion.2
  1039.4 15.9 select_add_fusion.2
  1129.7 21.2 %broadcast_in_dim.114 = f32[1024,128,128]{2,1,0:T(8,128)} broadcast(f32[]{:T(128)} %constant.142.clone.1), dimensions={} | broadcast | bytes 67108864 | tf_op jit(solution)/shard_map/broadcast_in_dim | solution.py:564
  1151.0 182.3 %scatter_fusion = f32[1024,128,128]{2,1,0:T(8,128)} fusion(f32[1024,128,128]{2,1,0:T(8,128)} %broadcast_in_dim.114, s32[1008]{0:T(1024)S(1)} %copy-done.133, f32[1008,128,128]{2,1,0:T(8,128)} %constant_dynamic-update-slice_fusion), kind=kCustom, calls=%fused_computation.1 | custom fusion | bytes 198184896 | tf_op jit(solution)/shard_map/scatter | solution.py:564
  1357.4 101.0 %rev.14 = f32[12,512,512]{1,2,0:T(8,128)} reverse(f32[12,512,512]{1,2,0:T(8,128)} %get-tuple-element.123), dimensions={1} | reverse | bytes 25165824 | tf_op jit(solution)/shard_map/rev | solution.py:97
  1471.0 14.5 concatenate.25.clone
  1496.7 39.8 %copy.434 = f32[2,8,512,1024]{3,1,2,0:T(8,128)} copy(f32[2,8,512,1024]{3,2,1,0:T(8,128)S(1)} %bitcast.638) | data formatting | bytes 67108864
  1536.5 22.8 %slice.209 = f32[12,523776]{1,0:T(8,128)} slice(f32[12,524288]{1,0:T(8,128)} %bitcast.639), slice={[0:12], [0:523776]} | slice | bytes 50282496 | tf_op jit(solution)/shard_map/slice | solution.py:101
  1559.2 42.2 %reshape.803 = f32[12,512,1023]{2,1,0:T(8,128)} reshape(f32[12,523776]{1,0:T(8,128)} %slice.209) | data formatting | bytes 50282496 | tf_op jit(solution)/shard_map/reshape | solution.py:101
  1612.0 43.4 %all-reduce.5 = f32[5376]{0:T(1024)S(1)} all-reduce(f32[5376]{0:T(1024)S(1)} %constant_dynamic-update-slice_fusion.17), channel_id=3, replica_groups=mesh['dp'=16,'opt'=2] {'dp','opt'}, use_global_device_ids=true, to_apply=%region_37.38.clone | all-reduce | flops 5376 | bytes 43008
  1656.1 379.5 %reduce-scatter.2.cloned.1.call-done = f32[32,128,128]{2,1,0:T(8,128)} async-done(((f32[1024,128,128]{2,1,0:T(8,128)}), f32[32,128,128]{2,1,0:T(8,128)}) %reduce-scatter.2.cloned.1.call-update) | async-done | bytes 2097168 | tf_op jit(solution)/shard_map/reduce_scatter | solution.py:566
  (714 shorter events, 803.6 us)
Async XLA Ops:
  7.2 284.2 %all-gather.2.cloned.1.call-start = ((), (), s32[]{:S(2)}) async-start(), calls=%async_computation.1 | async-start | bytes 34603008 | tf_op jit(solution)/shard_map/all_gather | solution.py:498
  11.4 50.2 %copy-start.151 = (s32[1008]{0:T(1024)S(1)}, s32[1008]{0:T(1024)}, u32[]{:S(2)}) copy-start(s32[1008]{0:T(1024)} %param.28) | copy-start | bytes 12100
  11.4 50.2 %copy-start.98 = (bf16[20,768]{1,0:T(8,128)(2,1)S(1)}, bf16[20,768]{1,0:T(8,128)(2,1)}, u32[]{:S(2)}) copy-start(bf16[20,768]{1,0:T(8,128)(2,1)} %param.23) | copy-start | bytes 92164
  11.4 50.3 %copy-start.170 = (s32[1,20]{1,0:T(1,128)S(1)}, s32[1,20]{1,0:T(1,128)}, u32[]{:S(2)}) copy-start(s32[1,20]{1,0:T(1,128)} %param.27) | copy-start | bytes 244
  11.4 2024.2 %reduce-scatter.2.cloned.1.call-start = ((), (), s32[]{:S(2)}) async-start(), calls=%async_computation.2 | async-start | bytes 69206016 | tf_op jit(solution)/shard_map/reduce_scatter | solution.py:566
  11.7 279.0 %collective-permute-start.3 = (bf16[1,512]{1,0:T(2,128)(2,1)S(1)}, bf16[1,512]{1,0:T(2,128)(2,1)S(1)}, u32[]{:S(2)}, u32[]{:S(2)}) collective-permute-start(bf16[1,512]{1,0:T(2,128)(2,1)S(1)} %get-tuple-element.386), channel_id=1, source_target_pairs={{0,28},{2,30},{4,0},{6,2},{8,4},{10,6},{12,8},{14,10},{16,12},{18,... | collective-permute-start | bytes 3080 | tf_op jit(solution)/shard_map/ppermute | solution.py:30
  17.8 273.0 %collective-permute-start.2 = (bf16[1,512]{1,0:T(2,128)(2,1)S(1)}, bf16[1,512]{1,0:T(2,128)(2,1)S(1)}, u32[]{:S(2)}, u32[]{:S(2)}) collective-permute-start(bf16[1,512]{1,0:T(2,128)(2,1)S(1)} %get-tuple-element.387), channel_id=1, source_target_pairs={{0,30},{2,0},{4,2},{6,4},{8,6},{10,8},{12,10},{14,12},{16,14},{18,... | collective-permute-start | bytes 3080 | tf_op jit(solution)/shard_map/ppermute | solution.py:30
  62.5 315.1 %copy-start.154 = (f32[20]{0:T(128)}, f32[20]{0:T(128)S(1)}, u32[]{:S(2)}) copy-start(f32[20]{0:T(128)S(1)} %fusion.293) | copy-start | bytes 244
  64.3 313.3 %copy-start.130 = (f32[768]{0:T(1024)}, f32[768]{0:T(1024)S(1)}, u32[]{:S(2)}) copy-start(f32[768]{0:T(1024)S(1)} %get-tuple-element.382) | copy-start | bytes 9220
  506.4 16.0 copy-start.125
  534.2 39.2 %collective-permute-start.1 = (bf16[1,393216]{1,0:T(2,128)(2,1)}, bf16[1,393216]{1,0:T(2,128)(2,1)}, u32[]{:S(2)}, u32[]{:S(2)}) collective-permute-start(bf16[1,393216]{1,0:T(2,128)(2,1)} %get-tuple-element.370), channel_id=1, source_target_pairs={{0,28},{2,30},{4,0},{6,2},{8,4},{10,6},{12,8},{14,10},{16,12},{18,... | collective-permute-start | bytes 2359304 | tf_op jit(solution)/shard_map/ppermute | solution.py:30
  538.2 66.0 %collective-permute-start = (bf16[1,393216]{1,0:T(2,128)(2,1)S(1)}, bf16[1,393216]{1,0:T(2,128)(2,1)}, u32[]{:S(2)}, u32[]{:S(2)}) collective-permute-start(bf16[1,393216]{1,0:T(2,128)(2,1)S(1)} %get-tuple-element.371), channel_id=1, source_target_pairs={{0,30},{2,0},{4,2},{6,4},{8,6},{10,8},{12,10},{14,12},{16,14},{18,... | collective-permute-start | bytes 2359304 | tf_op jit(solution)/shard_map/ppermute | solution.py:30
  540.6 12.8 copy-start.161
  540.6 85.3 %copy-start.71 = (f32[20,768]{1,0:T(8,128)}, f32[20,768]{1,0:T(8,128)S(1)}, u32[]{:S(2)}) copy-start(f32[20,768]{1,0:T(8,128)S(1)} %get-tuple-element.397) | copy-start | bytes 184324
  553.9 68.5 %copy-start.96 = (bf16[20,12,64]{2,1,0:T(8,128)(2,1)}, bf16[20,12,64]{2,1,0:T(8,128)(2,1)S(1)}, u32[]{:S(2)}) copy-start(bf16[20,12,64]{2,1,0:T(8,128)(2,1)S(1)} %reshape.757) | copy-start | bytes 92164
  700.0 65.3 %collective-permute-start.5 = (bf16[1,393216]{1,0:T(2,128)(2,1)}, bf16[1,393216]{1,0:T(2,128)(2,1)}, u32[]{:S(2)}, u32[]{:S(2)}) collective-permute-start(bf16[1,393216]{1,0:T(2,128)(2,1)} %get-tuple-element.367), channel_id=1, source_target_pairs={{0,4},{2,6},{4,8},{6,10},{8,12},{10,14},{12,16},{14,18},{16,20},{1... | collective-permute-start | bytes 2359304 | tf_op jit(solution)/shard_map/ppermute | solution.py:30
  700.0 72.0 %collective-permute-start.4 = (bf16[1,393216]{1,0:T(2,128)(2,1)}, bf16[1,393216]{1,0:T(2,128)(2,1)}, u32[]{:S(2)}, u32[]{:S(2)}) collective-permute-start(bf16[1,393216]{1,0:T(2,128)(2,1)} %get-tuple-element.368), channel_id=1, source_target_pairs={{0,2},{2,4},{4,6},{6,8},{8,10},{10,12},{12,14},{14,16},{16,18},{18... | collective-permute-start | bytes 2359304 | tf_op jit(solution)/shard_map/ppermute | solution.py:30
  744.8 27.2 %copy-start.75 = (bf16[1,393216]{1,0:T(2,128)(2,1)S(1)}, bf16[1,393216]{1,0:T(2,128)(2,1)}, u32[]{:S(2)}) copy-start(bf16[1,393216]{1,0:T(2,128)(2,1)} %get-tuple-element.366) | copy-start | bytes 2359300
  744.8 27.2 %copy-start.168 = (s32[3]{0:T(128)S(1)}, s32[3]{0:T(128)}, u32[]{:S(2)}) copy-start(s32[3]{0:T(128)} %copy-done.166) | copy-start | bytes 40
  805.3 24.7 %copy-start.8 = (f32[1536,768]{0,1:T(8,128)}, f32[1536,768]{0,1:T(8,128)S(1)}, u32[]{:S(2)}) copy-start(f32[1536,768]{0,1:T(8,128)S(1)} %add_add_fusion.2) | copy-start | bytes 14155780
  841.6 15.7 copy-start.171
  1129.7 21.3 %copy-start.133 = (s32[1008]{0:T(1024)S(1)}, s32[1008]{0:T(1024)}, u32[]{:S(2)}) copy-start(s32[1008]{0:T(1024)} %copy-done.132) | copy-start | bytes 12100
  1601.5 53.9 %copy-start.159 = (f32[168]{0:T(256)S(1)}, f32[168]{0:T(256)}, u32[]{:S(2)}) copy-start(f32[168]{0:T(256)} %param.32) | copy-start | bytes 2020
  1601.5 53.9 %copy-start.160 = (f32[168]{0:T(256)S(1)}, f32[168]{0:T(256)}, u32[]{:S(2)}) copy-start(f32[168]{0:T(256)} %param.33) | copy-start | bytes 2020
  (182 other events, 879.2 us)
Sparse Core Ops, SparseCore 0:
  11.6 198.6 all-gather.1
  1333.5 702.0 reduce-scatter.1
where the time goes:
time: 2090 us; the launch traced here: 2060 us
  local copies, waits for them, and re-layouts  1050 us (50%)
  waiting for transfers between devices  447 us (21%)
  matrix products  341 us (16%)
  other arithmetic  109 us (5%)
  blocking collectives  82.3 us (4%)
    reduce_scatter x1, waiting for transfers between devices, per_device(): lax.psum_scatter(grad_slots, ('dp', 'opt'), scatter_dimension=0, tiled=True)  380 us
    unnamed x427, local copies, waits for them, and re-layouts  213 us
    scatter x1, local copies, waits for them, and re-layouts, per_device(): jnp.zeros((slot_total, BLK, BLK), jnp.float32).at[owner_slot]  182 us
    rev x2, local copies, waits for them, and re-layouts, collapse_offsets(): flipped = bias_total[:, ::-1, :]  101 us
    rev x2, local copies, waits for them, and re-layouts, spread_offsets(): return flattened.reshape(head_count, length, 2 * length)[:, ::-1, :length]  96.1 us
    unnamed x2, blocking collectives  82.3 us
    dot_general x16, matrix products, rows_grad(): lax.dot_general(grads, weight, (((1,), (1,)), ((), ())), preferred_elemen...  68.6 us
    ppermute x6, waiting for transfers between devices, passed_along(): lax.ppermute(shard, axis, [(i, (i + by) % size) for i in range(size)])  67.1 us
  transfers between devices with their start and end apart: 8, of which 5 were waited for; matrix products, arithmetic and copies ran while one was open for 28% of the time, Pallas kernels for 0%

commit v1 on v0

v1 whole, which is shorter than its diff:
```python
import functools

import jax
import jax.numpy as jnp
import numpy as np
from jax import lax
from jax.experimental import pallas as pl
from jax.experimental.pallas import tpu as pltpu
from jax.sharding import PartitionSpec as P

D = 768
H = 12
HD = 64
FF = 3072
NB = 32
MAXD = 128
BLK = 128
PASS_SLOT = 512
PASS_EX = 3
ALEN = 20
EX_DEV = 1
AROWS = 32
PAIRS = H // 2
STRIP = 7 * BLK
EXTRA = 16

exact_prec = lax.Precision.HIGHEST
neg_fill = -1000000000.0
stat_decay = 0.95
block_rate = 0.5
moment_decay = 0.9
small_rate = 0.002
MESH = pl.DeviceIdType.MESH
VMEM_CAP = 60 << 20
f32 = jnp.float32
bf16 = jnp.bfloat16

ENC_QKV, ENC_OUT, ENC_UP, ENC_DOWN = 0, 108, 144, 288
DEC_QKV, DEC_OUT, CROSS_Q, CROSS_KV, CROSS_OUT, DEC_UP, DEC_DOWN = 432, 540, 576, 612, 684, 720, 864


def dot(left, right):
    return jnp.dot(left, right, preferred_element_type=f32)


def dot_nt(left, right):
    return lax.dot_general(left, right, (((1,), (1,)), ((), ())), preferred_element_type=f32)


def dot_tn(left, right):
    return lax.dot_general(left, right, (((0,), (0,)), ((), ())), preferred_element_type=f32)


def to_low(values):
    return values.astype(bf16)


def rms_factor(values):
    return lax.rsqrt(jnp.mean(values * values, axis=-1, keepdims=True) + 1e-06)


def rms_scale(values, gain):
    return values * rms_factor(values) * gain


def norm_back(values, gain, upstream):
    factor = rms_factor(values)
    scaled = values * factor
    lifted = upstream * gain
    inner = jnp.mean(lifted * scaled, axis=-1, keepdims=True)
    rows = factor * (lifted - scaled * inner)
    return rows, jnp.sum(upstream * scaled, axis=0, keepdims=True)


GATE_A = float(np.sqrt(2.0 / np.pi))
GATE_B = 0.044715


def gate(values):
    return 0.5 * values * (1.0 + jnp.tanh(GATE_A * (values + GATE_B * values * values * values)))


def gate_both(values):
    square = values * values
    bend = jnp.tanh(GATE_A * values * (1.0 + GATE_B * square))
    half = 0.5 * (1.0 + bend)
    slope = half + 0.5 * values * (1.0 - bend * bend) * (GATE_A * (1.0 + 3.0 * GATE_B * square))
    return values * half, slope


def bucket_of(offsets, both_sides):
    if both_sides:
        halves = NB // 2
        bucket_base = (offsets > 0) * halves
        distance = np.abs(offsets)
    else:
        halves = NB
        bucket_base = offsets * 0
        distance = np.maximum(-offsets, 0)
    exact_count = halves // 2
    widened = np.maximum(distance, 1) * 1.0
    far_bucket = exact_count + np.floor(
        np.log(widened / exact_count) / np.log(MAXD / exact_count) * (halves - exact_count)
    ).astype(np.int32)
    far_bucket = np.minimum(far_bucket, halves - 1)
    return (bucket_base + np.where(distance < exact_count, distance, far_bucket)).astype(np.int32)


def strip_buckets():
    rho = np.arange(2 * BLK, 5 * BLK)[:, None]
    return bucket_of(rho - 3 * BLK - np.arange(BLK)[None, :], True)


def start_blocks(rows_ref, gathered, first, rows, cols, dest, sem):
    across = cols // BLK

    def body(b, carry):
        i = b // across
        j = b - i * across
        source = pl.multiple_of(rows_ref[first + b], 16)
        pltpu.make_async_copy(
            gathered.at[pl.ds(source, BLK)],
            dest.at[pl.ds(pl.multiple_of(i * BLK, BLK), BLK), pl.ds(pl.multiple_of(j * BLK, BLK), BLK)],
            sem,
        ).start()
        return carry

    lax.fori_loop(0, rows // BLK * across, body, 0)


def wait_whole(dest, sem):
    pltpu.make_async_copy(dest, dest, sem).wait()


def head_lanes(rows, head):
    lane = lax.broadcasted_iota(jnp.int32, (rows, BLK), 1)
    return (lane < HD) if head == 0 else (lane >= HD)


def chunk_plan(rows, nbits):
    if nbits != 4:
        return [(0, rows, list(range(nbits - 1, -1, -1)))]
    A = [3, 2, 0, 1]; B = [3, 2, 1, 0]; C = [0, 1, 3, 2]; D = [1, 0, 3, 2]
    orders = [A, B, C, D, A, B]
    unit = rows // 16
    sizes = [768, 768, 512, 512, 768]
    sizes.append(rows - sum(sizes))
    out = []; s = 0
    for z, o in zip(sizes, orders):
        out.append((s, z, o)); s += z
    return out

def tree_info(order):
    n = len(order)
    stage = {b: t for t, b in enumerate(order)}
    def last(m):
        return max([stage[b] for b in range(n) if m >> b & 1], default=-1)
    return stage, last

def gather_kernel(plan, nbits, rows, x_ref, out_ref, ssem, rsem, ssib, rsib, lsem):
    me = lax.axis_index("dp"); core = lax.axis_index("opt")
    bar = pltpu.get_barrier_semaphore()
    for b in range(nbits):
        pl.semaphore_signal(bar, inc=1, device_id=(me ^ (1 << b), core), device_id_type=MESH)
    pl.semaphore_signal(bar, inc=1, device_id=(me, 1 - core), device_id_type=MESH)
    pl.semaphore_wait(bar, nbits + 1)
    nm = 1 << nbits
    def region(c, m, o=None):
        s, z, _ = plan[c]
        dev = (me ^ m) * 2 + (core if o is None else o)
        return out_ref.at[pl.ds(pl.multiple_of(dev * rows + s, 16), z)]
    def own(c):
        s, z, _ = plan[c]
        return x_ref.at[pl.ds(s, z)]
    waits = []
    events = []
    for c, (s, z, order) in enumerate(plan):
        stage, last = tree_info(order)
        for m in range(nm):
            events.append((last(m) * 2 + (c if last(m) >= 0 else 0), c, m))
    events.sort()
    idx = {c: 0 for c in range(len(plan))}
    local = []
    for _, c, m in events:
        s, z, order = plan[c]
        stage, last = tree_info(order)
        if m:
            b = order[last(m)]
            pltpu.make_async_remote_copy(region(c, m), region(c, m), ssem.at[c, 0], rsem.at[c, m], device_id=(me ^ (1 << b), core), device_id_type=MESH).wait_recv()
        src = region(c, m) if m else own(c)
        for t in range(last(m) + 1, nbits):
            b = order[t]
            cp = pltpu.make_async_remote_copy(src, region(c, m), ssem.at[c, idx[c]], rsem.at[c, m | (1 << b)], device_id=(me ^ (1 << b), core), device_id_type=MESH)
            cp.start(); waits.append(cp); idx[c] += 1
        cp = pltpu.make_async_remote_copy(src, region(c, m), ssib.at[c, m], rsib.at[c, m], device_id=(me, 1 - core), device_id_type=MESH)
        cp.start(); waits.append(cp)
        if m == 0:
            cp = pltpu.make_async_copy(src, region(c, 0), lsem.at[c]); cp.start(); local.append(cp)
    for c in range(len(plan)):
        for m in range(nm):
            r = region(c, m, 1 - core)
            pltpu.make_async_remote_copy(r, r, ssib.at[c, m], rsib.at[c, m], device_id=(me, 1 - core), device_id_type=MESH).wait_recv()
    for cp in waits: cp.wait_send()
    for cp in local: cp.wait()

def gather_rows(x, dp_count, cid):
    rows = x.shape[0]
    nbits = dp_count.bit_length() - 1
    plan = chunk_plan(rows, nbits)
    nm = 1 << nbits; nc = len(plan)
    return pl.pallas_call(functools.partial(gather_kernel, plan, nbits, rows),
        out_shape=jax.ShapeDtypeStruct((dp_count * 2 * rows, 128), x.dtype),
        in_specs=[pl.BlockSpec(memory_space=pl.ANY)], out_specs=pl.BlockSpec(memory_space=pl.ANY),
        scratch_shapes=[pltpu.SemaphoreType.DMA((nc, nm)), pltpu.SemaphoreType.DMA((nc, nm)), pltpu.SemaphoreType.DMA((nc, nm)), pltpu.SemaphoreType.DMA((nc, nm)), pltpu.SemaphoreType.DMA((nc,))],
        name="gather_rows",
        compiler_params=pltpu.CompilerParams(collective_id=cid, has_side_effects=True))(x)

def scatter_kernel(plan, nbits, rows, s_ref, out_ref, own, sib, land, ssem, rsem, ssib, rsib, lsem):
    me = lax.axis_index("dp"); core = lax.axis_index("opt")
    bar = pltpu.get_barrier_semaphore()
    for b in range(nbits):
        pl.semaphore_signal(bar, inc=1, device_id=(me ^ (1 << b), core), device_id_type=MESH)
    pl.semaphore_signal(bar, inc=1, device_id=(me, 1 - core), device_id_type=MESH)
    nm = 1 << nbits
    def src(c, m, o):
        s, z, _ = plan[c]
        dev = (me ^ m) * 2 + o
        return s_ref.at[pl.ds(pl.multiple_of(dev * rows + s, 16), z)]
    def send_stage(order, m):
        rev = order[::-1]
        return min([t for t in range(nbits) if m >> rev[t] & 1], default=nbits)
    events = sorted((send_stage(order, m) * 2 + c, c, m) for c, (s, z, order) in enumerate(plan) for m in range(nm))
    loads = {}
    for _, c, m in events:
        s, z, _o = plan[c]
        cp = pltpu.make_async_copy(src(c, m, core), own.at[m, pl.ds(s, z)], lsem.at[c, m]); cp.start(); loads[c, m] = cp
    pl.semaphore_wait(bar, nbits + 1)
    sends = []
    for _, c, m in events:
        s, z, _o = plan[c]
        cp = pltpu.make_async_remote_copy(src(c, m, 1 - core), sib.at[m, pl.ds(s, z)], ssib.at[c, m], rsib.at[c, m], device_id=(me, 1 - core), device_id_type=MESH)
        cp.start(); sends.append(cp)
    for _, c, m in events:
        s, z, order = plan[c]
        rev = order[::-1]
        st = send_stage(order, m)
        loads[c, m].wait()
        here = own.at[m, pl.ds(s, z)]
        pltpu.make_async_remote_copy(here, sib.at[m, pl.ds(s, z)], ssib.at[c, m], rsib.at[c, m], device_id=(me, 1 - core), device_id_type=MESH).wait_recv()
        terms = [own.at[m], sib.at[m]]
        for t in range(st):
            mm = m | (1 << rev[t])
            pltpu.make_async_remote_copy(here, land.at[mm - 1, pl.ds(s, z)], ssem.at[c, mm], rsem.at[c, mm], device_id=(me ^ (1 << rev[t]), core), device_id_type=MESH).wait_recv()
            terms.append(land.at[mm - 1])
        step = 128
        def add(i, k):
            r = pl.ds(pl.multiple_of(s + i * step, 16), k)
            total = terms[0][r, :].astype(jnp.float32) + terms[1][r, :].astype(jnp.float32)
            for x in terms[2:]:
                total = total + x[r, :].astype(jnp.float32)
            if m:
                own[m, r, :] = total.astype(jnp.bfloat16)
            else:
                out_ref[r, :] = total
        def body(i, carry):
            add(i, step); return carry
        lax.fori_loop(0, z // step, body, 0)
        if z % step:
            add(z // step, z % step)
        if m:
            cp = pltpu.make_async_remote_copy(here, land.at[m - 1, pl.ds(s, z)], ssem.at[c, m], rsem.at[c, m], device_id=(me ^ (1 << rev[st]), core), device_id_type=MESH)
            cp.start(); sends.append(cp)
    for cp in sends: cp.wait_send()

def scatter_rows(s, dp_count, cid):
    rows = s.shape[0] // (dp_count * 2)
    nbits = dp_count.bit_length() - 1
    plan = chunk_plan(rows, nbits)
    nm = 1 << nbits; nc = len(plan)
    return pl.pallas_call(functools.partial(scatter_kernel, plan, nbits, rows),
        out_shape=jax.ShapeDtypeStruct((rows, 128), jnp.float32),
        in_specs=[pl.BlockSpec(memory_space=pl.ANY)], out_specs=pl.BlockSpec(memory_space=pltpu.VMEM),
        scratch_shapes=[pltpu.VMEM((nm, rows, 128), jnp.bfloat16), pltpu.VMEM((nm, rows, 128), jnp.bfloat16), pltpu.VMEM((nm - 1, rows, 128), jnp.bfloat16)]
          + [pltpu.SemaphoreType.DMA((nc, nm))] * 5,
        name="scatter_rows",
        compiler_params=pltpu.CompilerParams(collective_id=cid, has_side_effects=True, vmem_limit_bytes=60 << 20))(s)


def strip_kernel(table, buckets, out):
    head = pl.program_id(0)
    which = buckets[...]
    total = jnp.zeros((3 * BLK, BLK), f32)
    for b in range(NB):
        total = jnp.where(which == b, table[b * H + head], total)
    out[0, 0 : 2 * BLK, :] = jnp.full((2 * BLK, BLK), table[(NB // 2 - 1) * H + head], f32)
    out[0, 2 * BLK : 5 * BLK, :] = total
    out[0, 5 * BLK :, :] = jnp.full((2 * BLK, BLK), table[(NB - 1) * H + head], f32)


def bias_strips(table):
    return pl.pallas_call(
        strip_kernel,
        grid=(H,),
        in_specs=[
            pl.BlockSpec(memory_space=pltpu.SMEM),
            pl.BlockSpec((3 * BLK, BLK), lambda h: (0, 0)),
        ],
        out_specs=pl.BlockSpec((1, STRIP, BLK), lambda h: (h, 0, 0)),
        out_shape=jax.ShapeDtypeStruct((H, STRIP, BLK), f32),
        name="bias_strips",
    )(table, jnp.asarray(strip_buckets()))


def masked_scores(keys, queries, strip, offset, length):
    rows = keys.shape[0]
    scores = dot_nt(keys, queries)
    bias = jnp.concatenate(
        [strip[(3 - n) * BLK : (3 - n) * BLK + rows, :] for n in (offset, offset + 1)], axis=1
    )
    key_at = lax.broadcasted_iota(jnp.int32, scores.shape, 0)
    return jnp.where(key_at < length, scores + bias, neg_fill)


def attend_kernel(rows_ref, lengths, x_ref, gathered, gains, strips, qkv, lse, mixed, hidden, wqkv, wout, sems):
    step = pl.program_id(0)

    @pl.when(step == 0)
    def _():
        for m in range(3):
            start_blocks(rows_ref, gathered, ENC_QKV + 36 * m, D, D, wqkv.at[m], sems.at[m])
        start_blocks(rows_ref, gathered, ENC_OUT, D, D, wout, sems.at[3])

    values = x_ref[...].astype(f32)
    normed = to_low(rms_scale(values, gains[0:1, :]))
    for m in range(3):

        @pl.when(step == 0)
        def _(m=m):
            wait_whole(wqkv.at[m], sems.at[m])

        qkv[:, m * D : (m + 1) * D] = to_low(dot(normed, wqkv[m]))
    length = lengths[step]

    def one_pair(pair, carry):
        at = pl.multiple_of(pair * BLK, BLK)
        queries = qkv[:, pl.ds(at, BLK)]
        keys = qkv[:, pl.ds(pl.multiple_of(at + D, BLK), BLK)]
        turned = qkv[:, pl.ds(pl.multiple_of(at + 2 * D, BLK), BLK)].T
        for n in range(2):
            part = queries[n * 256 : (n + 1) * 256]
            outs = []
            for head in range(2):
                only = jnp.where(head_lanes(256, head), part, jnp.zeros_like(part))
                scores = masked_scores(keys, only, strips.at[2 * pair + head], 2 * n, length)
                peak = jnp.max(scores, axis=0, keepdims=True)
                expos = jnp.exp(scores - peak)
                total = jnp.sum(expos, axis=0, keepdims=True)
                lse[0, pl.ds(2 * pair + head, 1), n * 256 : (n + 1) * 256] = peak + jnp.log(total)
                outs.append(dot(turned, to_low(expos * (1.0 / total))))
            lane = lax.broadcasted_iota(jnp.int32, (BLK, 256), 0)
            both = jnp.where(lane < HD, outs[0], outs[1])
            mixed[n * 256 : (n + 1) * 256, pl.ds(at, BLK)] = to_low(both.T)
        return carry

    lax.fori_loop(0, PAIRS, one_pair, 0)

    @pl.when(step == 0)
    def _():
        wait_whole(wout, sems.at[3])

    hidden[...] = x_ref[...].astype(f32) + dot(mixed[...], wout[...])


def encoder_attend(rows, lengths, enc_in, gathered, gains, strips):
    count = lengths.shape[0]
    total = count * PASS_SLOT
    by_row = lambda p, *_: (p, 0)
    return pl.pallas_call(
        attend_kernel,
        grid_spec=pltpu.PrefetchScalarGridSpec(
            num_scalar_prefetch=2,
            grid=(count,),
            in_specs=[
                pl.BlockSpec((PASS_SLOT, D), by_row),
                pl.BlockSpec(memory_space=pl.ANY),
                pl.BlockSpec((8, D), lambda p, *_: (0, 0)),
                pl.BlockSpec((H, STRIP, BLK), lambda p, *_: (0, 0, 0)),
            ],
            out_specs=[
                pl.BlockSpec((PASS_SLOT, 3 * D), by_row),
                pl.BlockSpec((1, 16, PASS_SLOT), lambda p, *_: (p, 0, 0)),
                pl.BlockSpec((PASS_SLOT, D), by_row),
                pl.BlockSpec((PASS_SLOT, D), by_row),
            ],
            scratch_shapes=[
                pltpu.VMEM((3, D, D), bf16),
                pltpu.VMEM((D, D), bf16),
                pltpu.SemaphoreType.DMA((4,)),
            ],
        ),
        out_shape=[
            jax.ShapeDtypeStruct((total, 3 * D), bf16),
            jax.ShapeDtypeStruct((count, 16, PASS_SLOT), f32),
            jax.ShapeDtypeStruct((total, D), bf16),
            jax.ShapeDtypeStruct((total, D), f32),
        ],
        compiler_params=pltpu.CompilerParams(vmem_limit_bytes=VMEM_CAP),
        name="encoder_attend",
    )(rows, lengths, enc_in, gathered, gains, strips)


FCHUNK = 512


def feed_kernel(rows_ref, hidden, gathered, gains, inner, output, encoded, cross, wup, wdown, wkv, sems):
    step = pl.program_id(0)

    @pl.when(step == 0)
    def _():
        start_blocks(rows_ref, gathered, ENC_UP, D, FF, wup, sems.at[0])
        start_blocks(rows_ref, gathered, ENC_DOWN, FF, D, wdown, sems.at[1])
        for m in range(2):
            start_blocks(rows_ref, gathered, CROSS_KV + 36 * m, D, D, wkv.at[m], sems.at[2 + m])

    normed = to_low(rms_scale(hidden[...], gains[1:2, :]))

    @pl.when(step == 0)
    def _():
        wait_whole(wup, sems.at[0])
        wait_whole(wdown, sems.at[1])

    total = hidden[...]
    for c in range(FF // FCHUNK):
        cols = slice(c * FCHUNK, (c + 1) * FCHUNK)
        act = dot(normed, wup[:, cols])
        inner[:, cols] = to_low(act)
        total = total + dot(to_low(gate(act)), wdown[cols, :])
    output[...] = total
    low = to_low(rms_scale(total, gains[2:3, :]))
    encoded[...] = low
    for m in range(2):

        @pl.when(step == 0)
        def _(m=m):
            wait_whole(wkv.at[m], sems.at[2 + m])

        cross[:, m * D : (m + 1) * D] = to_low(dot(low, wkv[m]))


def encoder_feed(rows, hidden, gathered, gains):
    total = hidden.shape[0]
    tile = 256
    by_row = lambda p, *_: (p, 0)
    return pl.pallas_call(
        feed_kernel,
        grid_spec=pltpu.PrefetchScalarGridSpec(
            num_scalar_prefetch=1,
            grid=(total // tile,),
            in_specs=[
                pl.BlockSpec((tile, D), by_row),
                pl.BlockSpec(memory_space=pl.ANY),
                pl.BlockSpec((8, D), lambda p, *_: (0, 0)),
            ],
            out_specs=[
                pl.BlockSpec((tile, FF), by_row),
                pl.BlockSpec((tile, D), by_row),
                pl.BlockSpec((tile, D), by_row),
                pl.BlockSpec((tile, 2 * D), by_row),
            ],
            scratch_shapes=[
                pltpu.VMEM((D, FF), bf16),
                pltpu.VMEM((FF, D), bf16),
                pltpu.VMEM((2, D, D), bf16),
                pltpu.SemaphoreType.DMA((4,)),
            ],
        ),
        out_shape=[
            jax.ShapeDtypeStruct((total, FF), bf16),
            jax.ShapeDtypeStruct((total, D), f32),
            jax.ShapeDtypeStruct((total, D), bf16),
            jax.ShapeDtypeStruct((total, 2 * D), bf16),
        ],
        compiler_params=pltpu.CompilerParams(vmem_limit_bytes=VMEM_CAP),
        name="encoder_feed",
    )(rows, hidden, gathered, gains)


def feed_back_kernel(
    rows_ref, output, hidden, inner, upstream, gathered, gains,
    act_low, inner_grad, branch, normed, hidden_grad, attn_grad, mixed_grad, gain_sums,
    wup, wdown, wout, sems,
):
    step = pl.program_id(0)

    @pl.when(step == 0)
    def _():
        start_blocks(rows_ref, gathered, ENC_DOWN, FF, D, wdown, sems.at[0])
        start_blocks(rows_ref, gathered, ENC_UP, D, FF, wup, sems.at[1])
        start_blocks(rows_ref, gathered, ENC_OUT, D, D, wout, sems.at[2])
        gain_sums[...] = jnp.zeros_like(gain_sums)

    output_grad, final_gain = norm_back(output[...], gains[2:3, :], upstream[...])
    low = to_low(output_grad)
    branch[...] = low

    @pl.when(step == 0)
    def _():
        wait_whole(wdown, sems.at[0])
        wait_whole(wup, sems.at[1])

    total = jnp.zeros(hidden.shape, f32)
    for c in range(FF // FCHUNK):
        cols = slice(c * FCHUNK, (c + 1) * FCHUNK)
        value, slope = gate_both(inner[:, cols].astype(f32))
        act_low[:, cols] = to_low(value)
        grad = to_low(slope * dot_nt(low, wdown[cols, :]))
        inner_grad[:, cols] = grad
        total = total + dot_nt(grad, wup[:, cols])
    values = hidden[...]
    normed[...] = to_low(rms_scale(values, gains[1:2, :]))
    part, second_gain = norm_back(values, gains[1:2, :], total)
    grad = output_grad + part
    hidden_grad[...] = grad
    low = to_low(grad)
    attn_grad[...] = low

    @pl.when(step == 0)
    def _():
        wait_whole(wout, sems.at[2])

    mixed_grad[...] = to_low(dot_nt(low, wout[...]))
    gain_sums[0:1, :] += second_gain
    gain_sums[1:2, :] += final_gain


def feed_back(rows, output, hidden, inner, upstream, gathered, gains):
    total = hidden.shape[0]
    tile = 256
    by_row = lambda p, *_: (p, 0)
    fixed = lambda p, *_: (0, 0)
    row = pl.BlockSpec((tile, D), by_row)
    wide = pl.BlockSpec((tile, FF), by_row)
    return pl.pallas_call(
        feed_back_kernel,
        grid_spec=pltpu.PrefetchScalarGridSpec(
            num_scalar_prefetch=1,
            grid=(total // tile,),
            in_specs=[row, row, wide, row, pl.BlockSpec(memory_space=pl.ANY), pl.BlockSpec((8, D), fixed)],
            out_specs=[wide, wide, row, row, row, row, row, pl.BlockSpec((8, D), fixed)],
            scratch_shapes=[
                pltpu.VMEM((D, FF), bf16),
                pltpu.VMEM((FF, D), bf16),
                pltpu.VMEM((D, D), bf16),
                pltpu.SemaphoreType.DMA((3,)),
            ],
        ),
        out_shape=[
            jax.ShapeDtypeStruct((total, FF), bf16),
            jax.ShapeDtypeStruct((total, FF), bf16),
            jax.ShapeDtypeStruct((total, D), bf16),
            jax.ShapeDtypeStruct((total, D), bf16),
            jax.ShapeDtypeStruct((total, D), f32),
            jax.ShapeDtypeStruct((total, D), bf16),
            jax.ShapeDtypeStruct((total, D), bf16),
            jax.ShapeDtypeStruct((8, D), f32),
        ],
        compiler_params=pltpu.CompilerParams(vmem_limit_bytes=VMEM_CAP),
        name="feed_back",
    )(rows, output, hidden, inner, upstream, gathered, gains)


def attend_back_kernel(lengths, q_ref, k_ref, v_ref, go_ref, lse, strips, gq_ref, gk_ref, gv_ref, bias_sums):
    pair = pl.program_id(0)
    step = pl.program_id(1)

    @pl.when(step == 0)
    def _():
        bias_sums[...] = jnp.zeros_like(bias_sums)

    length = lengths[step]
    keys = k_ref[...]
    values = v_ref[...]
    turned = keys.T
    lane = lax.broadcasted_iota(jnp.int32, turned.shape, 0)
    halves = [
        jnp.where(lane < HD, turned, jnp.zeros_like(turned)),
        jnp.where(lane >= HD, turned, jnp.zeros_like(turned)),
    ]
    key_grad = jnp.zeros((PASS_SLOT, BLK), f32)
    value_grad = jnp.zeros((PASS_SLOT, BLK), f32)
    for n in range(2):
        span = slice(n * 256, (n + 1) * 256)
        query_grad = jnp.zeros((BLK, 256), f32)
        for head in range(2):
            mask = head_lanes(256, head)
            queries = jnp.where(mask, q_ref[span, :], jnp.zeros((256, BLK), bf16))
            grads = jnp.where(mask, go_ref[span, :], jnp.zeros((256, BLK), bf16))
            scores = masked_scores(keys, queries, strips.at[head], 2 * n, length)
            probs = jnp.exp(scores - lse[0, pl.ds(2 * pair + head, 1), span])
            prob_grad = dot_nt(values, grads)
            inner = jnp.sum(probs * prob_grad, axis=0, keepdims=True)
            score_grad = to_low(probs * (prob_grad - inner))
            wide = score_grad.astype(f32)
            for m in range(2):
                first = (3 - 2 * n - m) * BLK
                bias_sums[head, first : first + PASS_SLOT, :] += wide[:, m * BLK : (m + 1) * BLK]
            value_grad = value_grad + dot(to_low(probs), grads)
            key_grad = key_grad + dot(score_grad, queries)
            query_grad = query_grad + dot(halves[head], score_grad)
        gq_ref[span, :] = to_low(query_grad.T)
    gk_ref[...] = to_low(key_grad)
    gv_ref[...] = to_low(value_grad)


def attend_back(lengths, qkv, mixed_grad, lse, strips):
    count = lengths.shape[0]
    total = count * PASS_SLOT
    block = (PASS_SLOT, BLK)
    place = pl.BlockSpec(block, lambda a, p, *_: (p, a))
    return pl.pallas_call(
        attend_back_kernel,
        grid_spec=pltpu.PrefetchScalarGridSpec(
            num_scalar_prefetch=1,
            grid=(PAIRS, count),
            in_specs=[
                place,
                pl.BlockSpec(block, lambda a, p, *_: (p, a + PAIRS)),
                pl.BlockSpec(block, lambda a, p, *_: (p, a + 2 * PAIRS)),
                place,
                pl.BlockSpec((1, 16, PASS_SLOT), lambda a, p, *_: (p, 0, 0)),
                pl.BlockSpec((2, STRIP, BLK), lambda a, p, *_: (a, 0, 0)),
            ],
            out_specs=[place, place, place, pl.BlockSpec((2, STRIP, BLK), lambda a, p, *_: (a, 0, 0))],
        ),
        out_shape=[jax.ShapeDtypeStruct((total, D), bf16)] * 3
        + [jax.ShapeDtypeStruct((H, STRIP, BLK), f32)],
        compiler_params=pltpu.CompilerParams(vmem_limit_bytes=VMEM_CAP),
        name="attend_back",
    )(lengths, qkv, qkv, qkv, mixed_grad, lse, strips)


def input_back_kernel(
    rows_ref, x_ref, gq, gk, gv, hidden_grad, gathered, gains, result, normed, gain_sums, wqkv, sems
):
    step = pl.program_id(0)

    @pl.when(step == 0)
    def _():
        for m in range(3):
            start_blocks(rows_ref, gathered, ENC_QKV + 36 * m, D, D, wqkv.at[m], sems.at[m])
        gain_sums[...] = jnp.zeros_like(gain_sums)

    values = x_ref[...].astype(f32)
    normed[...] = to_low(rms_scale(values, gains[0:1, :]))
    total = jnp.zeros(values.shape, f32)
    for m, grads in enumerate((gq, gk, gv)):

        @pl.when(step == 0)
        def _(m=m):
            wait_whole(wqkv.at[m], sems.at[m])

        total = total + dot_nt(grads[...], wqkv[m])
    part, first_gain = norm_back(values, gains[0:1, :], total)
    result[...] = hidden_grad[...] + part
    gain_sums[0:1, :] += first_gain


def input_back(rows, enc_in, gq, gk, gv, hidden_grad, gathered, gains):
    total = enc_in.shape[0]
    tile = 256
    fixed = lambda p, *_: (0, 0)
    row = pl.BlockSpec((tile, D), lambda p, *_: (p, 0))
    return pl.pallas_call(
        input_back_kernel,
        grid_spec=pltpu.PrefetchScalarGridSpec(
            num_scalar_prefetch=1,
            grid=(total // tile,),
            in_specs=[row, row, row, row, row, pl.BlockSpec(memory_space=pl.ANY), pl.BlockSpec((8, D), fixed)],
            out_specs=[row, row, pl.BlockSpec((8, D), fixed)],
            scratch_shapes=[pltpu.VMEM((3, D, D), bf16), pltpu.SemaphoreType.DMA((3,))],
        ),
        out_shape=[
            jax.ShapeDtypeStruct((total, D), f32),
            jax.ShapeDtypeStruct((total, D), bf16),
            jax.ShapeDtypeStruct((8, D), f32),
        ],
        compiler_params=pltpu.CompilerParams(vmem_limit_bytes=VMEM_CAP),
        name="input_back",
    )(rows, enc_in, gq, gk, gv, hidden_grad, gathered, gains)


HROWS = H * AROWS
SIDE = D + 2 * BLK


def spread_heads(rows):
    lane = lax.broadcasted_iota(jnp.int32, rows.shape, 1)
    zero = jnp.zeros_like(rows)
    return jnp.concatenate(
        [jnp.where((lane >= h * HD) & (lane < (h + 1) * HD), rows, zero) for h in range(H)], axis=0
    )


def gather_heads(spread):
    lane = lax.broadcasted_iota(jnp.int32, (AROWS, D), 1)
    total = jnp.zeros((AROWS, D), f32)
    for h in range(H):
        total = jnp.where(
            (lane >= h * HD) & (lane < (h + 1) * HD), spread[h * AROWS : (h + 1) * AROWS], total
        )
    return total


def heads_to_lanes(column):
    lane = lax.broadcasted_iota(jnp.int32, (AROWS, BLK), 1)
    total = jnp.zeros((AROWS, BLK), f32)
    for h in range(H):
        total = jnp.where(lane == h, column[h * AROWS : (h + 1) * AROWS], total)
    return total


def lanes_to_heads(lanes):
    return jnp.concatenate([lanes[:, h : h + 1] for h in range(H)], axis=0)


def lanes_over_heads(lanes):
    lane = lax.broadcasted_iota(jnp.int32, (AROWS, D), 1)
    total = jnp.zeros((AROWS, D), f32)
    for h in range(H):
        total = jnp.where((lane >= h * HD) & (lane < (h + 1) * HD), lanes[:, h : h + 1], total)
    return total


def causal_scores(queries, keys, bias):
    scores = dot_nt(spread_heads(queries), keys) + bias
    row = lax.broadcasted_iota(jnp.int32, scores.shape, 0)
    key_at = lax.broadcasted_iota(jnp.int32, scores.shape, 1)
    return jnp.where(key_at <= row % AROWS, scores, neg_fill)


def self_kernel(rows_ref, dec_ref, gathered, gains, bias, qkv, mixed, first, normed, normed_two, cross, wqkv, wout, wcq, sems):
    for m in range(3):
        start_blocks(rows_ref, gathered, DEC_QKV + 36 * m, D, D, wqkv.at[m], sems.at[m])
    start_blocks(rows_ref, gathered, DEC_OUT, D, D, wout, sems.at[3])
    start_blocks(rows_ref, gathered, CROSS_Q, D, D, wcq, sems.at[4])
    values = dec_ref[...].astype(f32)
    low = to_low(rms_scale(values, gains[3:4, :]))
    normed[...] = low
    for m in range(3):
        wait_whole(wqkv.at[m], sems.at[m])
        qkv[:, m * D : (m + 1) * D] = to_low(dot(low, wqkv[m]))
    scores = causal_scores(qkv[:, 0:D], qkv[:, D : 2 * D], bias[...])
    peak = jnp.max(scores, axis=1, keepdims=True)
    expos = jnp.exp(scores - peak)
    probs = to_low(expos / jnp.sum(expos, axis=1, keepdims=True))
    heads = to_low(gather_heads(dot(probs, qkv[:, 2 * D : 3 * D])))
    mixed[...] = heads
    wait_whole(wout, sems.at[3])
    after = values + dot(heads, wout[...])
    first[...] = after
    low = to_low(rms_scale(after, gains[4:5, :]))
    normed_two[...] = low
    wait_whole(wcq, sems.at[4])
    cross[...] = to_low(dot(low, wcq[...]))


def whole_spec(shape):
    return pl.BlockSpec(shape, lambda *_: (0,) * len(shape))


def decoder_call(body, name, rows, ins, outs, scratch):
    specs = [pl.BlockSpec(memory_space=pl.ANY) if x.shape[0] > 65536 else whole_spec(x.shape) for x in ins]
    return pl.pallas_call(
        body,
        grid_spec=pltpu.PrefetchScalarGridSpec(
            num_scalar_prefetch=1,
            grid=(1,),
            in_specs=specs,
            out_specs=[whole_spec(shape) for shape, kind in outs],
            scratch_shapes=scratch,
        ),
        out_shape=[jax.ShapeDtypeStruct(shape, kind) for shape, kind in outs],
        compiler_params=pltpu.CompilerParams(vmem_limit_bytes=VMEM_CAP),
        name=name,
    )(rows, *ins)


def decoder_self(rows, dec_rows, gathered, gains, bias):
    low, full = ((AROWS, D), bf16), ((AROWS, D), f32)
    square = pltpu.VMEM((D, D), bf16)
    return decoder_call(
        self_kernel, "decoder_self", rows, (dec_rows, gathered, gains, bias),
        [((AROWS, 3 * D), bf16), low, full, low, low, low],
        [pltpu.VMEM((3, D, D), bf16), square, square, pltpu.SemaphoreType.DMA((5,))],
    )


def cross_kernel(lengths, offsets, queries, memory, result):
    length = lengths[pl.program_id(0)]
    scores = dot_nt(spread_heads(queries[0]), memory[:, 0:D])
    key_at = lax.broadcasted_iota(jnp.int32, scores.shape, 1)
    scores = jnp.where(key_at < length, scores, neg_fill)
    peak = jnp.max(scores, axis=1, keepdims=True)
    expos = jnp.exp(scores - peak)
    result[0, :, 0:D] = gather_heads(dot(to_low(expos), memory[:, D : 2 * D]))
    result[0, :, D : D + BLK] = heads_to_lanes(peak)
    result[0, :, D + BLK :] = heads_to_lanes(jnp.sum(expos, axis=1, keepdims=True))


def cross_attend(lengths, offsets, queries, memory):
    count = lengths.shape[0]
    at_offset = lambda p, lens, offs: (offs[p], 0, 0)
    return pl.pallas_call(
        cross_kernel,
        grid_spec=pltpu.PrefetchScalarGridSpec(
            num_scalar_prefetch=2,
            grid=(count,),
            in_specs=[
                pl.BlockSpec((1, AROWS, D), at_offset),
                pl.BlockSpec((PASS_SLOT, 2 * D), lambda p, *_: (p, 0)),
            ],
            out_specs=pl.BlockSpec((1, AROWS, SIDE), at_offset),
        ),
        out_shape=jax.ShapeDtypeStruct((count, AROWS, SIDE), f32),
        compiler_params=pltpu.CompilerParams(vmem_limit_bytes=VMEM_CAP),
        name="cross_attend",
    )(lengths, offsets, queries, memory)


def feed_decoder_kernel(
    rows_ref, parts, first, dec_cot, valid, gathered, gains,
    result, mixed, normed, act_low, inner_grad, branch, cross_grad, back, second_grad, gain_sums,
    wout, wup, wdown, sems,
):
    start_blocks(rows_ref, gathered, CROSS_OUT, D, D, wout, sems.at[0])
    start_blocks(rows_ref, gathered, DEC_UP, D, FF, wup, sems.at[1])
    start_blocks(rows_ref, gathered, DEC_DOWN, FF, D, wdown, sems.at[2])
    peaks = [parts[k, :, D : D + BLK] for k in range(PASS_EX)]
    peak = functools.reduce(jnp.maximum, peaks)
    scales = [jnp.exp(one - peak) for one in peaks]
    total = sum(parts[k, :, D + BLK :] * scales[k] for k in range(PASS_EX))
    lane = lax.broadcasted_iota(jnp.int32, total.shape, 1)
    total = jnp.where(lane < H, total, 1.0)
    heads = sum(parts[k, :, 0:D] * lanes_over_heads(scales[k] / total) for k in range(PASS_EX))
    low = to_low(heads)
    mixed[...] = low
    wait_whole(wout, sems.at[0])
    second = first[...] + dot(low, wout[...])
    low = to_low(rms_scale(second, gains[5:6, :]))
    normed[...] = low
    output_grad = dec_cot[...].astype(f32) * valid[:, 0:1]
    grad_low = to_low(output_grad)
    branch[...] = grad_low
    wait_whole(wup, sems.at[1])
    wait_whole(wdown, sems.at[2])
    after = second
    back_sum = jnp.zeros((AROWS, D), f32)
    for c in range(FF // D):
        cols = slice(c * D, (c + 1) * D)
        value, slope = gate_both(dot(low, wup[:, cols]))
        value = to_low(value)
        act_low[:, cols] = value
        after = after + dot(value, wdown[cols, :])
        grad = to_low(slope * dot_nt(grad_low, wdown[cols, :]))
        inner_grad[:, cols] = grad
        back_sum = back_sum + dot_nt(grad, wup[:, cols])
    result[...] = to_low(after)
    part, gain_grad = norm_back(second, gains[5:6, :], back_sum)
    grad = output_grad + part
    second_grad[...] = grad
    gain_sums[...] = jnp.broadcast_to(gain_grad, gain_sums.shape)
    low = to_low(grad)
    cross_grad[...] = low
    head_grad = to_low(dot_nt(low, wout[...])).astype(f32)
    back[:, 0:D] = head_grad
    back[:, D : D + BLK] = peak + jnp.log(total)
    product = head_grad * heads
    at = lax.broadcasted_iota(jnp.int32, (AROWS, D), 1)
    inner = jnp.zeros((AROWS, BLK), f32)
    for h in range(H):
        one = jnp.where((at >= h * HD) & (at < (h + 1) * HD), product, 0.0)
        inner = jnp.where(lane == h, jnp.sum(one, axis=1, keepdims=True), inner)
    back[:, D + BLK :] = inner


def decoder_feed(rows, parts, first, dec_cot, valid, gathered, gains):
    low, full, wide = ((AROWS, D), bf16), ((AROWS, D), f32), ((AROWS, FF), bf16)
    return decoder_call(
        feed_decoder_kernel, "decoder_feed", rows, (parts, first, dec_cot, valid, gathered, gains),
        [low, low, low, wide, wide, low, low, ((AROWS, SIDE), f32), full, ((8, D), f32)],
        [pltpu.VMEM((D, D), bf16), pltpu.VMEM((D, FF), bf16), pltpu.VMEM((FF, D), bf16), pltpu.SemaphoreType.DMA((3,))],
    )


def cross_back_kernel(
    rows_ref, lengths, offsets, queries, back, memory, enc_cot, gathered,
    memory_grad, query_grad, upstream, wkv, sems,
):
    step = pl.program_id(0)

    @pl.when(step == 0)
    def _():
        for m in range(2):
            start_blocks(rows_ref, gathered, CROSS_KV + 36 * m, D, D, wkv.at[m], sems.at[m])

    length = lengths[step]
    spread = spread_heads(queries[0])
    grads = spread_heads(to_low(back[0, :, 0:D]))
    keys = memory[:, 0:D]
    scores = dot_nt(spread, keys)
    key_at = lax.broadcasted_iota(jnp.int32, scores.shape, 1)
    scores = jnp.where(key_at < length, scores, neg_fill)
    probs = jnp.exp(scores - lanes_to_heads(back[0, :, D : D + BLK]))
    prob_grad = dot_nt(grads, memory[:, D : 2 * D])
    score_grad = to_low(probs * (prob_grad - lanes_to_heads(back[0, :, D + BLK :])))
    query_grad[0] = gather_heads(dot(score_grad, keys))
    key_low = to_low(dot_tn(score_grad, spread))
    value_low = to_low(dot_tn(to_low(probs), grads))
    memory_grad[:, 0:D] = key_low
    memory_grad[:, D : 2 * D] = value_low

    @pl.when(step == 0)
    def _():
        for m in range(2):
            wait_whole(wkv.at[m], sems.at[m])

    total = to_low(dot_nt(key_low, wkv[0]) + dot_nt(value_low, wkv[1])).astype(f32)
    row = lax.broadcasted_iota(jnp.int32, total.shape, 0)
    upstream[...] = total + jnp.where(row < length, enc_cot[...].astype(f32), 0.0)


def cross_back(rows, lengths, offsets, queries, back, memory, enc_cot, gathered):
    count = lengths.shape[0]
    total = count * PASS_SLOT
    at_offset = lambda p, rows, lens, offs: (offs[p], 0, 0)
    by_row = lambda p, *_: (p, 0)
    return pl.pallas_call(
        cross_back_kernel,
        grid_spec=pltpu.PrefetchScalarGridSpec(
            num_scalar_prefetch=3,
            grid=(count,),
            in_specs=[
                pl.BlockSpec((1, AROWS, D), at_offset),
                pl.BlockSpec((1, AROWS, SIDE), at_offset),
                pl.BlockSpec((PASS_SLOT, 2 * D), by_row),
                pl.BlockSpec((PASS_SLOT, D), by_row),
                pl.BlockSpec(memory_space=pl.ANY),
            ],
            out_specs=[
                pl.BlockSpec((PASS_SLOT, 2 * D), by_row),
                pl.BlockSpec((1, AROWS, D), at_offset),
                pl.BlockSpec((PASS_SLOT, D), by_row),
            ],
            scratch_shapes=[pltpu.VMEM((2, D, D), bf16), pltpu.SemaphoreType.DMA((2,))],
        ),
        out_shape=[
            jax.ShapeDtypeStruct((total, 2 * D), bf16),
            jax.ShapeDtypeStruct((count, AROWS, D), f32),
            jax.ShapeDtypeStruct((total, D), f32),
        ],
        compiler_params=pltpu.CompilerParams(vmem_limit_bytes=VMEM_CAP),
        name="cross_back",
    )(rows, lengths, offsets, queries, back, memory, enc_cot, gathered)


def self_back_kernel(
    rows_ref, parts, second_grad, first, dec_ref, qkv, gathered, gains, bias,
    result, cross_grad, out_grad, qkv_grad, score_grads, gain_sums, wqkv, wout, wcq, sems,
):
    start_blocks(rows_ref, gathered, CROSS_Q, D, D, wcq, sems.at[4])
    start_blocks(rows_ref, gathered, DEC_OUT, D, D, wout, sems.at[3])
    for m in range(3):
        start_blocks(rows_ref, gathered, DEC_QKV + 36 * m, D, D, wqkv.at[m], sems.at[m])
    low = to_low(parts[0] + parts[1] + parts[2])
    cross_grad[...] = low
    wait_whole(wcq, sems.at[4])
    part, second_gain = norm_back(first[...], gains[4:5, :], dot_nt(low, wcq[...]))
    first_grad = second_grad[...] + part
    low = to_low(first_grad)
    out_grad[...] = low
    wait_whole(wout, sems.at[3])
    heads_grad = spread_heads(to_low(dot_nt(low, wout[...])))
    queries = qkv[:, 0:D]
    keys = qkv[:, D : 2 * D]
    scores = causal_scores(queries, keys, bias[...])
    peak = jnp.max(scores, axis=1, keepdims=True)
    expos = jnp.exp(scores - peak)
    probs = expos / jnp.sum(expos, axis=1, keepdims=True)
    prob_grad = dot_nt(heads_grad, qkv[:, 2 * D : 3 * D])
    inner = jnp.sum(probs * prob_grad, axis=1, keepdims=True)
    score_grad = to_low(probs * (prob_grad - inner))
    score_grads[...] = score_grad.astype(f32)
    grads = (
        gather_heads(dot(score_grad, keys)),
        dot_tn(score_grad, spread_heads(queries)),
        dot_tn(to_low(probs), heads_grad),
    )
    total = jnp.zeros((AROWS, D), f32)
    for m in range(3):
        low = to_low(grads[m])
        qkv_grad[:, m * D : (m + 1) * D] = low
        wait_whole(wqkv.at[m], sems.at[m])
        total = total + dot_nt(low, wqkv[m])
    part, first_gain = norm_back(dec_ref[...].astype(f32), gains[3:4, :], total)
    result[...] = first_grad + part
    gain_sums[0:1, :] = first_gain
    gain_sums[1:2, :] = second_gain


def decoder_self_back(rows, parts, second_grad, first, dec_rows, qkv, gathered, gains, bias):
    low, full = ((AROWS, D), bf16), ((AROWS, D), f32)
    square = pltpu.VMEM((D, D), bf16)
    return decoder_call(
        self_back_kernel, "decoder_self_back", rows,
        (parts, second_grad, first, dec_rows, qkv, gathered, gains, bias),
        [full, low, low, ((AROWS, 3 * D), bf16), ((HROWS, AROWS), f32), ((8, D), f32)],
        [pltpu.VMEM((3, D, D), bf16), square, square, pltpu.SemaphoreType.DMA((5,))],
    )


def shift_kernel(way, one, two, got_one, got_two, ssem, rsem):
    size = lax.axis_size("dp")
    me = lax.axis_index("dp")
    core = lax.axis_index("opt")
    bar = pltpu.get_barrier_semaphore()
    for k in (1, 2):
        pl.semaphore_signal(bar, inc=1, device_id=((me - way * k + size) % size, core), device_id_type=MESH)
    pl.semaphore_wait(bar, 2)
    copies = []
    for k, source, dest in ((1, one, got_one), (2, two, got_two)):
        copies.append(
            pltpu.make_async_remote_copy(
                src_ref=source, dst_ref=dest, send_sem=ssem.at[k - 1], recv_sem=rsem.at[k - 1],
                device_id=((me + way * k + size) % size, core), device_id_type=MESH,
            )
        )
    for copy in copies:
        copy.start()
    for copy in copies:
        copy.wait()


def shifted(one, two, way, cid):
    vmem = pl.BlockSpec(memory_space=pltpu.VMEM)
    return pl.pallas_call(
        functools.partial(shift_kernel, way),
        in_specs=[vmem, vmem],
        out_specs=[vmem, vmem],
        out_shape=[jax.ShapeDtypeStruct(one.shape, one.dtype), jax.ShapeDtypeStruct(two.shape, two.dtype)],
        scratch_shapes=[pltpu.SemaphoreType.DMA((2,)), pltpu.SemaphoreType.DMA((2,))],
        compiler_params=pltpu.CompilerParams(collective_id=cid, has_side_effects=True),
        name="shift_rows",
    )(one, two)


def weight_kernel(first, tile, chunk, cols, has_into, rows_ref, *refs):
    if has_into:
        left, right, into, slots, turned, held, sems = refs
    else:
        left, right, slots, turned, held, sems = refs
    step = pl.program_id(0)
    steps = pl.num_programs(0)
    across = cols // BLK
    down = tile // BLK
    turned[...] = left[...].T
    parts = cols // chunk
    for c in range(parts):
        slot = c % 2
        buffer = held.at[slot]

        def drain():
            wait_whole(held.at[slot], sems.at[slot])

        if c >= 2:
            drain()
        else:
            pl.when(step > 0)(drain)
        held[slot] = to_low(dot(turned[...], right[:, c * chunk : (c + 1) * chunk]))
        for i in range(down):
            for j in range(chunk // BLK):
                row = pl.multiple_of(rows_ref[first + (step * down + i) * across + c * (chunk // BLK) + j], 16)
                pltpu.make_async_copy(
                    buffer.at[pl.ds(i * BLK, BLK), pl.ds(j * BLK, BLK)], slots.at[pl.ds(row, BLK)], sems.at[slot]
                ).start()

    @pl.when(step == steps - 1)
    def _():
        for slot in range(min(2, parts)):
            wait_whole(held.at[slot], sems.at[slot])


def weight_slots(rows, left, right, first, into, total_rows, chunk=D, tile=256):
    count, down = left.shape
    cols = right.shape[1]
    assert cols // chunk >= 2 or cols == chunk
    any_space = pl.BlockSpec(memory_space=pl.ANY)
    operands = (rows, left, right) + (() if into is None else (into,))
    if cols == chunk:
        chunk = cols // 2
    return pl.pallas_call(
        functools.partial(weight_kernel, first, tile, chunk, cols, into is not None),
        grid_spec=pltpu.PrefetchScalarGridSpec(
            num_scalar_prefetch=1,
            grid=(down // tile,),
            in_specs=[
                pl.BlockSpec((count, tile), lambda p, *_: (0, p)),
                pl.BlockSpec((count, cols), lambda p, *_: (0, 0)),
            ]
            + ([] if into is None else [any_space]),
            out_specs=any_space,
            scratch_shapes=[
                pltpu.VMEM((tile, count), bf16),
                pltpu.VMEM((2, tile, chunk), bf16),
                pltpu.SemaphoreType.DMA((2,)),
            ],
        ),
        out_shape=jax.ShapeDtypeStruct((total_rows, BLK), bf16),
        input_output_aliases={} if into is None else {3: 0},
        compiler_params=pltpu.CompilerParams(vmem_limit_bytes=VMEM_CAP),
        name="weight_slots",
    )(*operands)


def exact(left, right, dims):
    return lax.dot_general(left, right, (dims, ((), ())), precision=exact_prec, preferred_element_type=f32)


def update_kernel(slots, has_ref, sums, master, stats, roots, grads, new_stats, new_master):
    for s in range(slots):
        has = has_ref[pl.program_id(0) * slots + s]
        grad = sums[s * BLK : (s + 1) * BLK, :]
        grad = jnp.where(has > 0, grad, 0.0)
        grads[s] = grad
        new_stats[s, 0] = stat_decay * stats[s, 0] + (1.0 - stat_decay) * exact(grad, grad, ((1,), (1,)))
        new_stats[s, 1] = stat_decay * stats[s, 1] + (1.0 - stat_decay) * exact(grad, grad, ((0,), (0,)))
        shaped = exact(roots[s, 0], grad, ((1,), (0,)))
        shaped = exact(shaped, roots[s, 1], ((1,), (0,)))
        old = master[s]
        shaped_rms = jnp.sqrt(jnp.mean(shaped * shaped) + 1e-06)
        weight_rms = jnp.sqrt(jnp.mean(old * old) + 1e-06)
        new_master[s] = old - block_rate * weight_rms * shaped / shaped_rms


def update_blocks(has, sums, master, kron_stats, inverse_roots):
    count = master.shape[0]
    slots = min(4, count)
    one = pl.BlockSpec((slots, BLK, BLK), lambda p, *_: (p, 0, 0))
    two = pl.BlockSpec((slots, 2, BLK, BLK), lambda p, *_: (p, 0, 0, 0))
    return pl.pallas_call(
        functools.partial(update_kernel, slots),
        grid_spec=pltpu.PrefetchScalarGridSpec(
            num_scalar_prefetch=1,
            grid=(count // slots,),
            in_specs=[pl.BlockSpec((slots * BLK, BLK), lambda p, *_: (p, 0)), one, two, two],
            out_specs=[one, two, one],
        ),
        out_shape=[
            jax.ShapeDtypeStruct(master.shape, f32),
            jax.ShapeDtypeStruct(kron_stats.shape, f32),
            jax.ShapeDtypeStruct(master.shape, f32),
        ],
        name="update_blocks",
    )(has, sums, master, kron_stats, inverse_roots)


def gather_all(shard, dp_count):
    if dp_count == 16:
        return gather_rows(shard, dp_count, 0)
    return lax.all_gather(shard, ("dp", "opt"), axis=0, tiled=True)


def scatter_all(terms, dp_count):
    if dp_count == 16:
        return scatter_rows(terms, dp_count, 1)
    return lax.psum_scatter(terms, ("dp", "opt"), scatter_dimension=0, tiled=True).astype(f32)


def pad_rows(array, rows):
    return jnp.pad(array, ((0, rows - array.shape[0]),) + ((0, 0),) * (array.ndim - 1))


def per_device(
    enc_in,
    enc_cot,
    dec_in,
    dec_cot,
    passage_lengths,
    passage_example,
    answer_tokens,
    owner_slot,
    master,
    kron_stats,
    inverse_roots,
    small_params,
    small_moment,
):
    dp_count = lax.axis_size("dp")
    pair_count = lax.axis_size("opt")
    devices = dp_count * pair_count
    slot_dev = master.shape[0]
    small_dev = small_params.shape[0]
    dev_rows = slot_dev * BLK + EXTRA
    total_rows = devices * dev_rows
    table_size = NB * H

    padded = jnp.pad(to_low(small_params), (0, EXTRA * BLK - small_dev)).reshape(EXTRA, BLK)
    gathered = gather_all(
        jnp.concatenate([to_low(master).reshape(slot_dev * BLK, BLK), padded], axis=0), dp_count
    )
    small_all = gathered.reshape(devices, dev_rows, BLK)[:, slot_dev * BLK :]
    small_all = small_all.reshape(devices, EXTRA * BLK)[:, :small_dev].reshape(-1).astype(f32)
    gains = pad_rows(small_all[: 6 * D].reshape(6, D), 8)
    rows = (owner_slot // slot_dev * dev_rows + owner_slot % slot_dev * BLK).astype(jnp.int32)
    strips = bias_strips(small_all[6 * D : 6 * D + table_size])
    answer_at = np.arange(AROWS)
    dec_buckets = bucket_of(np.minimum(answer_at, ALEN - 1)[None, :] - np.minimum(answer_at, ALEN - 1)[:, None], False)
    dec_onehot = jnp.asarray((dec_buckets[..., None] == np.arange(NB)).reshape(-1, NB).astype(np.float32))
    dec_bias = jnp.dot(
        small_all[6 * D + table_size :].reshape(NB, H).T, dec_onehot.T, precision=exact_prec, preferred_element_type=f32
    ).reshape(HROWS, AROWS)

    dec_rows = pad_rows(dec_in, AROWS)
    dec_qkv, dec_mixed, first, dec_normed, dec_normed_two, cross_queries = decoder_self(
        rows, dec_rows, gathered, gains, dec_bias
    )
    from_one, from_two = shifted(cross_queries, cross_queries, 1, 2)
    queries = jnp.stack([cross_queries, from_one, from_two])

    owner_dp = passage_example // EX_DEV // pair_count
    offsets = ((lax.axis_index("dp") - owner_dp) % dp_count).astype(jnp.int32)
    qkv, log_total, mixed, hidden = encoder_attend(rows, passage_lengths, enc_in, gathered, gains, strips)
    inner, output, encoded, memory = encoder_feed(rows, hidden, gathered, gains)

    parts = cross_attend(passage_lengths, offsets, queries, memory)
    part_one, part_two = shifted(parts[1], parts[2], -1, 3)
    valid = (pad_rows(answer_tokens.reshape(ALEN, 1), AROWS) != 0).astype(f32)
    dec_out, cross_mixed, dec_normed_three, dec_act, dec_inner_grad, dec_branch, cross_out_grad, back, second_grad, gain_six = (
        decoder_feed(
            rows, jnp.stack([parts[0], part_one, part_two]), first, pad_rows(dec_cot, AROWS),
            jnp.broadcast_to(valid, (AROWS, BLK)), gathered, gains,
        )
    )
    back_one, back_two = shifted(back, back, 1, 4)
    memory_grad, query_parts, upstream = cross_back(
        rows, passage_lengths, offsets, queries, jnp.stack([back, back_one, back_two]), memory, enc_cot, gathered
    )
    query_one, query_two = shifted(query_parts[1], query_parts[2], -1, 5)
    dec_in_grad, cross_query_grad, dec_out_grad, dec_qkv_grad, dec_scores, gain_four = decoder_self_back(
        rows, jnp.stack([query_parts[0], query_one, query_two]), second_grad, first, dec_rows, dec_qkv, gathered, gains, dec_bias
    )

    act, inner_grad, branch, normed_two, hidden_grad, attn_grad, mixed_grad, gain_two = feed_back(
        rows, output, hidden, inner, upstream, gathered, gains
    )
    grad_query, grad_key, grad_value, bias_sums = attend_back(passage_lengths, qkv, mixed_grad, log_total, strips)
    enc_in_grad, normed, gain_one = input_back(
        rows, enc_in, grad_query, grad_key, grad_value, hidden_grad, gathered, gains
    )

    slots = None
    for left, right, at in (
        (act, branch, ENC_DOWN),
        (normed_two, inner_grad, ENC_UP),
        (mixed, attn_grad, ENC_OUT),
        (encoded, memory_grad[:, :D], CROSS_KV),
        (encoded, memory_grad[:, D:], CROSS_KV + 36),
        (normed, grad_query, ENC_QKV),
        (normed, grad_key, ENC_QKV + 36),
        (normed, grad_value, ENC_QKV + 72),
        (dec_normed, dec_qkv_grad[:, :D], DEC_QKV),
        (dec_normed, dec_qkv_grad[:, D : 2 * D], DEC_QKV + 36),
        (dec_normed, dec_qkv_grad[:, 2 * D :], DEC_QKV + 72),
        (dec_mixed, dec_out_grad, DEC_OUT),
        (dec_normed_two, cross_query_grad, CROSS_Q),
        (cross_mixed, cross_out_grad, CROSS_OUT),
        (dec_normed_three, dec_inner_grad, DEC_UP),
        (dec_act, dec_branch, DEC_DOWN),
    ):
        slots = weight_slots(rows, left, right, at, slots, total_rows)

    middle = bias_sums[:, 2 * BLK : 5 * BLK].reshape(H, -1)
    strip_onehot = jnp.asarray(strip_buckets().reshape(-1, 1) == np.arange(NB)[None, :]).astype(f32)
    enc_table = jnp.dot(middle, strip_onehot, precision=exact_prec, preferred_element_type=f32).T
    enc_table = enc_table.at[NB // 2 - 1].add(jnp.sum(bias_sums[:, : 2 * BLK], axis=(1, 2)))
    enc_table = enc_table.at[NB - 1].add(jnp.sum(bias_sums[:, 5 * BLK :], axis=(1, 2)))
    dec_table = jnp.dot(
        dec_scores.reshape(H, AROWS * AROWS), dec_onehot, precision=exact_prec, preferred_element_type=f32
    ).T
    small_terms = jnp.concatenate(
        [gain_one[0], gain_two[0], gain_two[1], gain_four[0], gain_four[1], gain_six[0], enc_table.reshape(-1), dec_table.reshape(-1)]
    )
    small_rows = jnp.pad(
        to_low(small_terms).reshape(devices, small_dev), ((0, 0), (0, EXTRA * BLK - small_dev))
    ).reshape(devices, EXTRA, BLK)
    slots = slots.reshape(devices, dev_rows, BLK).at[:, slot_dev * BLK :].set(small_rows).reshape(total_rows, BLK)

    sums = scatter_all(slots, dp_count)
    small_grads = sums[slot_dev * BLK :].reshape(-1)[:small_dev]
    here = (lax.axis_index("dp") * pair_count + lax.axis_index("opt")) * slot_dev + jnp.arange(slot_dev)
    has = jnp.any(owner_slot[None, :] == here[:, None], axis=1).astype(jnp.int32)
    block_grads, new_stats, new_master = update_blocks(has, sums, master, kron_stats, inverse_roots)
    new_moment = moment_decay * small_moment + small_grads
    new_small = small_params - small_rate * new_moment
    return (
        dec_out[:ALEN],
        encoded,
        enc_in_grad,
        dec_in_grad[:ALEN],
        block_grads,
        new_stats,
        new_master,
        small_grads,
        new_moment,
        new_small,
    )


def solution(mesh):
    placed = (
        P(("dp", "opt"), None),
        P(("dp", "opt"), None),
        P(("dp", "opt"), None),
        P(("dp", "opt"), None),
        P(("dp", "opt")),
        P(("dp", "opt")),
        P(("dp", "opt"), None),
        P(),
        P(("dp", "opt"), None, None),
        P(("dp", "opt"), None, None, None),
        P(("dp", "opt"), None, None, None),
        P(("dp", "opt")),
        P(("dp", "opt")),
    )
    return jax.shard_map(
        per_device,
        mesh=mesh,
        in_specs=placed,
        out_specs=(
            P(("dp", "opt"), None),
            P(("dp", "opt"), None),
            P(("dp", "opt"), None),
            P(("dp", "opt"), None),
            P(("dp", "opt"), None, None),
            P(("dp", "opt"), None, None, None),
            P(("dp", "opt"), None, None),
            P(("dp", "opt")),
            P(("dp", "opt")),
            P(("dp", "opt")),
        ),
        check_vma=False,
    )
```

time: 2090 us -> 865 us (0.41); the launches traced: 2060 us -> 860 us
  local copies, waits for them, and re-layouts: 1050 us -> 30.2 us
  Pallas kernels: 0 us -> 805 us
  waiting for transfers between devices: 447 us -> 0 us
  matrix products: 341 us -> 3.68 us
  other arithmetic: 109 us -> 19.5 us
  blocking collectives: 82.3 us -> 0 us
    pallas_call x0 -> x34, Pallas kernels: none -> 805 us  [the longest x1 201 us: scatter_rows(): pl.pallas_call(functools.partial(scatter_kernel, plan, nbits, rows), out_...]
    reduce_scatter x1 -> x0, waiting for transfers between devices: 380 us -> none  [per_device(): lax.psum_scatter(grad_slots, ('dp', 'opt'), scatter_dimension=0, tiled=True)]
    dot_general x92 -> x3, matrix products: 341 us -> 3.68 us  [the longest x1 2.94 us: per_device(): jnp.dot(middle, strip_onehot, precision=exact_prec, preferred_element_typ...]
    unnamed x427 -> x24, local copies, waits for them, and re-layouts: 213 us -> 4.76 us
    rev x4 -> x0, local copies, waits for them, and re-layouts: 197 us -> none  [the longest x2 101 us: collapse_offsets(): flipped = bias_total[:, ::-1, :]]
    scatter x1, local copies, waits for them, and re-layouts: 182 us -> 0.7 us  [per_device(): slots.reshape(devices, dev_rows, BLK).at[:, slot_dev * BLK:].set(small_rows)]
    reshape x40 -> x6, local copies, waits for them, and re-layouts: 181 us -> 2.81 us  [the longest x1 1.05 us: per_device(): dec_scores.reshape(H, AROWS * AROWS)]
    unnamed x2 -> x0, blocking collectives: 82.3 us -> none
  transfers between devices with their start and end apart: 8 -> 0, of which waited for: 5 -> 0; matrix products, arithmetic and copies ran while one was open for 28% -> 0% of each run, Pallas kernels for 0% -> 0%
where the time goes in v1:
time: 865 us; the launch traced here: 860 us
  Pallas kernels  805 us (93%)
  local copies, waits for them, and re-layouts  30.2 us (3%)
  other arithmetic  19.5 us (2%)
    pallas_call x1, Pallas kernels, scatter_rows(): pl.pallas_call(functools.partial(scatter_kernel, plan, nbits, rows), out_...  201 us
    pallas_call x1, Pallas kernels, gather_rows(): pl.pallas_call(functools.partial(gather_kernel, plan, nbits, rows), out_s...  149 us
    pallas_call x16, Pallas kernels, weight_slots(): pl.pallas_call(functools.partial(weight_kernel, first, tile, chunk, cols,...  133 us
    pallas_call x1, Pallas kernels, encoder_attend(): pl.pallas_call(attend_kernel, grid_spec=pltpu.PrefetchScalarGridSpec(num_...  58.6 us
    pallas_call x1, Pallas kernels, attend_back(): pl.pallas_call(attend_back_kernel, grid_spec=pltpu.PrefetchScalarGridSpec...  43.8 us
    pallas_call x1, Pallas kernels, feed_back(): pl.pallas_call(feed_back_kernel, grid_spec=pltpu.PrefetchScalarGridSpec(n...  41.5 us
    pallas_call x1, Pallas kernels, encoder_feed(): pl.pallas_call(feed_kernel, grid_spec=pltpu.PrefetchScalarGridSpec(num_sc...  38.5 us
    pallas_call x4, Pallas kernels, shifted(): pl.pallas_call(functools.partial(shift_kernel, way), in_specs=[vmem, vmem...  38.2 us

profile of v1, /device:TPU:0, one launch (start us, length us, event | category | flops | bytes accessed | tf_op | source)
XLA Modules:
  0.0 859.9 jit_solution(8746845470783530072)
XLA Ops:
  12.2 149.3 %gather_rows.1.gathered = bf16[131584,128]{1,0:T(8,128)(2,1)} custom-call(bf16[4112,128]{1,0:T(8,128)(2,1)} %pad_maximum_fusion.x_ref), custom_call_target="tpu_custom_call" | custom-call | tf_op jit(solution)/shard_map/gather_rows/pallas_call | solution.py:211
  165.3 8.4 decoder_self.1
  173.6 9.8 %shift_rows.4 = (bf16[32,768]{1,0:T(8,128)(2,1)}, bf16[32,768]{1,0:T(8,128)(2,1)}) custom-call(bf16[32,768]{1,0:T(8,128)(2,1)} %get-tuple-element.105.one.two, bf16[32,768]{1,0:T(8,128)(2,1)} %get-tuple-element.105.one.two), custom_call_target="tpu_custom_call" | custom-call | tf_op jit(solution)/shard_map/shift_rows/pallas_call | solution.py:1045
  184.9 8.6 bias_strips.1.strips
  193.5 58.6 %encoder_attend.1 = (bf16[1536,2304]{1,0:T(8,128)(2,1)}, f32[3,16,512]{2,1,0:T(8,128)}, bf16[1536,768]{1,0:T(8,128)(2,1)}, f32[1536,768]{1,0:T(8,128)}) custom-call(s32[1008]{0:T(1024)} %fusion.4.rows_ref, s32[3]{0:T(128)} %lengths.7, bf16[1536,768]{1,0:T(8,128)(2,1)} %x_ref.3, bf16[131584,128]{1,0:T(8,128)(2,1)} %gather_rows.1.gathered, ...), custom_call_target="tpu_custom_call" | custom-call | tf_op jit(solution)/shard_map/encoder_attend/pallas_call | solution.py:378
  252.2 38.5 %encoder_feed.1 = (bf16[1536,3072]{1,0:T(8,128)(2,1)}, f32[1536,768]{1,0:T(8,128)}, bf16[1536,768]{1,0:T(8,128)(2,1)}, bf16[1536,1536]{1,0:T(8,128)(2,1)}) custom-call(s32[1008]{0:T(1024)} %fusion.4.rows_ref, f32[1536,768]{1,0:T(8,128)} %get-tuple-element.108.hidden, bf16[131584,128]{1,0:T(8,128)(2,1)} %gather_rows.1.gathered, f32[8,768]{1,0:T(8,128)} %pad_convert_fusion.gains), custom_call_target="tpu_custom_call" | custom-call | tf_op jit(solution)/shard_map/encoder_feed/pallas_call | solution.py:454
  299.1 7.7 shift_rows.5
  308.5 14.1 %decoder_feed.1 = (bf16[32,768]{1,0:T(8,128)(2,1)}, bf16[32,768]{1,0:T(8,128)(2,1)}, bf16[32,768]{1,0:T(8,128)(2,1)}, bf16[32,3072]{1,0:T(8,128)(2,1)}, bf16[32,...) custom-call(s32[1008]{0:T(1024)} %fusion.4.rows_ref, ...), custom_call_target="tpu_custom_call" | custom-call | tf_op jit(solution)/shard_map/decoder_feed/pallas_call | solution.py:773
  324.7 13.1 %shift_rows.6 = (f32[32,1024]{1,0:T(8,128)}, f32[32,1024]{1,0:T(8,128)}) custom-call(f32[32,1024]{1,0:T(8,128)} %get-tuple-element.118.one.two, f32[32,1024]{1,0:T(8,128)} %get-tuple-element.118.one.two), custom_call_target="tpu_custom_call" | custom-call | tf_op jit(solution)/shard_map/shift_rows/pallas_call | solution.py:1045
  339.7 17.2 %cross_back.1 = (bf16[1536,1536]{1,0:T(8,128)(2,1)}, f32[3,32,768]{2,1,0:T(8,128)}, f32[1536,768]{1,0:T(8,128)}) custom-call(s32[1008]{0:T(1024)} %fusion.4.rows_ref, s32[3]{0:T(128)} %lengths.7, s32[3]{0:T(128)} %and_select_fusion.offsets, bf16[3,32,768]{2,1,0:T(8,128)(2,1)} %pad_maximum_fusion.4.queries, f32[3,32,1024]{2,1,0:T(8,128)} %pad_maximum_fusion.2.back, ...), custom_call_target="tpu_custom_call" | custom-call | tf_op jit(solution)/shard_map/cross_back/pallas_call | solution.py:937
  367.9 9.2 %decoder_self_back.1 = (f32[32,768]{1,0:T(8,128)}, bf16[32,768]{1,0:T(8,128)(2,1)}, bf16[32,768]{1,0:T(8,128)(2,1)}, bf16[32,2304]{1,0:T(8,128)(2,1)}, f32[384,32]{1,0:T(8,128)}, /*index=5*/f32[8,768]{1,0:T(8,128)}) custom-call(s32[1008]{0:T(1024)} %fusion.4.rows_ref, f32[3,32,768]{2,1,0:T(8,128)} %pad_maximum_fusion.3.parts, ...), custom_call_target="tpu_custom_call" | custom-call | tf_op jit(solution)/shard_map/decoder_self_back/pallas_call | solution.py:773
  387.5 41.5 %feed_back.1 = (bf16[1536,3072]{1,0:T(8,128)(2,1)}, bf16[1536,3072]{1,0:T(8,128)(2,1)}, bf16[1536,768]{1,0:T(8,128)(2,1)}, bf16[1536,768]{1,0:T(8,128)(2,1)}, f3...) custom-call(s32[1008]{0:T(1024)} %fusion.4.rows_ref, ...), custom_call_target="tpu_custom_call" | custom-call | tf_op jit(solution)/shard_map/feed_back/pallas_call | solution.py:543
  429.0 43.8 %attend_back.1 = (bf16[1536,768]{1,0:T(8,128)(2,1)}, bf16[1536,768]{1,0:T(8,128)(2,1)}, bf16[1536,768]{1,0:T(8,128)(2,1)}, f32[12,896,128]{2,1,0:T(8,128)}) custom-call(s32[3]{0:T(128)} %lengths.7, bf16[1536,2304]{1,0:T(8,128)(2,1)} %get-tuple-element.115.q_ref.k_ref.v_ref, bf16[1536,2304]{1,0:T(8,128)(2,1)} %get-tuple-element.115.q_ref.k_ref.v_ref, ...), custom_call_target="tpu_custom_call" | custom-call | tf_op jit(solution)/shard_map/attend_back/pallas_call | solution.py:620
  472.8 16.1 %input_back.1 = (f32[1536,768]{1,0:T(8,128)}, bf16[1536,768]{1,0:T(8,128)(2,1)}, f32[8,768]{1,0:T(8,128)}) custom-call(s32[1008]{0:T(1024)} %fusion.4.rows_ref, bf16[1536,768]{1,0:T(8,128)(2,1)} %x_ref.3, bf16[1536,768]{1,0:T(8,128)(2,1)} %get-tuple-element.124.gq.refs_1_, bf16[1536,768]{1,0:T(8,128)(2,1)} %get-tuple-element.125.gk.refs_1_, ...), custom_call_target="tpu_custom_call" | custom-call | tf_op jit(solution)/shard_map/input_back/pallas_call | solution.py:673
  502.6 20.6 %weight_slots.16.refs_2_ = bf16[131584,128]{1,0:T(8,128)(2,1)} custom-call(s32[1008]{0:T(1024)} %fusion.4.rows_ref, bf16[1536,3072]{1,0:T(8,128)(2,1)} %get-tuple-element.153.refs_0_, bf16[1536,768]{1,0:T(8,128)(2,1)} %get-tuple-element.154.refs_1_), custom_call_target="tpu_custom_call" | custom-call | tf_op jit(solution)/shard_map/weight_slots/pallas_call | solution.py:1100
  523.2 18.2 %weight_slots.17.refs_2_ = bf16[131584,128]{1,0:T(8,128)(2,1)} custom-call(s32[1008]{0:T(1024)} %fusion.4.rows_ref, bf16[1536,768]{1,0:T(8,128)(2,1)} %get-tuple-element.151.refs_0_, bf16[1536,3072]{1,0:T(8,128)(2,1)} %get-tuple-element.152.refs_1_, bf16[131584,128]{1,0:T(8,128)(2,1)} %weight_slots.16.refs_2_), custom_call_target="tpu_custom_call", output_to_operand_aliasing={{}: (3, {})} | custom-call | tf_op jit(solution)/shard_map/weight_slots/pallas_call | solution.py:1100
  541.4 7.7 weight_slots.18.refs_2_
  556.7 7.7 weight_slots.20.refs_2_
  572.1 7.7 weight_slots.22.refs_2_
  579.7 7.8 weight_slots.23.refs_2_
  614.6 8.3 weight_slots.30.refs_2_
  623.0 12.7 %weight_slots.31 = bf16[131584,128]{1,0:T(8,128)(2,1)} custom-call(s32[1008]{0:T(1024)} %fusion.4.rows_ref, bf16[32,3072]{1,0:T(8,128)(2,1)} %get-tuple-element.135.refs_0_, bf16[32,768]{1,0:T(8,128)(2,1)} %get-tuple-element.136.refs_1_, bf16[131584,128]{1,0:T(8,128)(2,1)} %weight_slots.30.refs_2_), custom_call_target="tpu_custom_call", output_to_operand_aliasing={{}: (3, {})} | custom-call | tf_op jit(solution)/shard_map/weight_slots/pallas_call | solution.py:1100
  636.4 201.3 %scatter_rows.1.sums = f32[4112,128]{1,0:T(8,128)} custom-call(bf16[131584,128]{1,0:T(8,128)(2,1)} %bitcast.54), custom_call_target="tpu_custom_call" | custom-call | tf_op jit(solution)/shard_map/scatter_rows/pallas_call | solution.py:280
  839.0 20.7 %update_blocks.1 = (f32[32,128,128]{2,1,0:T(8,128)}, f32[32,2,128,128]{3,2,1,0:T(8,128)}, f32[32,128,128]{2,1,0:T(8,128)}) custom-call(s32[32]{0:T(128)} %convert_element_type.37.has_ref, f32[4112,128]{1,0:T(8,128)} %scatter_rows.1.sums, f32[32,128,128]{2,1,0:T(8,128)} %master.1, f32[32,2,128,128]{3,2,1,0:T(8,128)} %stats.1, f32[32,2,128,128]{3,2,1,0:T(8,128)} %roots.1), custom_call_target="tpu_custom_call" | custom-call | tf_op jit(solution)/shard_map/update_blocks/pallas_call | solution.py:1149
  (95 shorter events, 110.1 us)
Async XLA Ops:
  12.2 151.9 %copy-start = (f32[1024,32]{1,0:T(8,128)S(1)}, f32[1024,32]{1,0:T(8,128)}, u32[]{:S(2)}) copy-start(f32[1024,32]{1,0:T(8,128)} %constant.178.clone) | copy-start | bytes 393220
  491.1 2.9 copy-start.3
  495.3 1.8 copy-start.1
  622.9 12.7 %copy-start.2 = (bf16[4,8,16,128]{3,2,1,0:T(8,128)(2,1)S(1)}, bf16[4,8,16,128]{3,2,1,0:T(8,128)(2,1)}, u32[]{:S(2)}) copy-start(bf16[4,8,16,128]{3,2,1,0:T(8,128)(2,1)} %copy.60) | copy-start | bytes 393220
  636.4 202.0 %copy-start.4 = (f32[168]{0:T(256)S(1)}, f32[168]{0:T(256)}, u32[]{:S(2)}) copy-start(f32[168]{0:T(256)} %param.33) | copy-start | bytes 2020
  636.4 202.0 %copy-start.5 = (f32[168]{0:T(256)S(1)}, f32[168]{0:T(256)}, u32[]{:S(2)}) copy-start(f32[168]{0:T(256)} %param.34) | copy-start | bytes 2020

commit v2 on v1

--- a/solution.py
+++ b/solution.py
@@ -23,6 +23,7 @@
 PAIRS = H // 2
 STRIP = 7 * BLK
 EXTRA = 16
+SURE = 248
 
 exact_prec = lax.Precision.HIGHEST
 neg_fill = -1000000000.0
@@ -137,153 +138,240 @@
     return (lane < HD) if head == 0 else (lane >= HD)
 
 
-def chunk_plan(rows, nbits):
+ORDERS = {"A": (3, 2, 0, 1), "B": (3, 2, 1, 0), "C": (0, 1, 3, 2), "D": (1, 0, 3, 2)}
+
+
+def chunk_plan(rows, nbits, names, shares):
     if nbits != 4:
-        return [(0, rows, list(range(nbits - 1, -1, -1)))]
-    A = [3, 2, 0, 1]; B = [3, 2, 1, 0]; C = [0, 1, 3, 2]; D = [1, 0, 3, 2]
-    orders = [A, B, C, D, A, B]
-    unit = rows // 16
-    sizes = [768, 768, 512, 512, 768]
-    sizes.append(rows - sum(sizes))
-    out = []; s = 0
-    for z, o in zip(sizes, orders):
-        out.append((s, z, o)); s += z
-    return out
-
-def tree_info(order):
-    n = len(order)
-    stage = {b: t for t, b in enumerate(order)}
-    def last(m):
-        return max([stage[b] for b in range(n) if m >> b & 1], default=-1)
-    return stage, last
-
-def gather_kernel(plan, nbits, rows, x_ref, out_ref, ssem, rsem, ssib, rsib, lsem):
-    me = lax.axis_index("dp"); core = lax.axis_index("opt")
-    bar = pltpu.get_barrier_semaphore()
+        return [(0, rows, tuple(range(nbits - 1, -1, -1)))]
+    total = sum(shares)
+    plan, first = [], 0
+    for k, name in enumerate(names):
+        size = rows - first if k == len(names) - 1 else rows * shares[k] // total // 16 * 16
+        plan.append((first, size, ORDERS[name]))
+        first += size
+    return plan
+
+
+class Tree:
+    def __init__(self, order):
+        self.order, self.nbits = order, len(order)
+
+    def last(self, m):
+        return max([t for t, b in enumerate(self.order) if m >> b & 1], default=-1)
+
+    def rank(self, m):
+        t = self.last(m)
+        peers = [x for x in range(1 << self.nbits) if self.last(x) == t]
+        return (peers.index(m) + 0.5) / len(peers)
+
+    def children(self, m):
+        return [m | 1 << self.order[t] for t in range(self.last(m) + 1, self.nbits)]
+
+    def bit(self, m):
+        return 1 << self.order[self.last(m)]
+
+
+def enter_tree(nbits):
+    me, core = lax.axis_index("dp"), lax.axis_index("opt")
+    barrier = pltpu.get_barrier_semaphore()
     for b in range(nbits):
-        pl.semaphore_signal(bar, inc=1, device_id=(me ^ (1 << b), core), device_id_type=MESH)
-    pl.semaphore_signal(bar, inc=1, device_id=(me, 1 - core), device_id_type=MESH)
-    pl.semaphore_wait(bar, nbits + 1)
-    nm = 1 << nbits
-    def region(c, m, o=None):
-        s, z, _ = plan[c]
-        dev = (me ^ m) * 2 + (core if o is None else o)
-        return out_ref.at[pl.ds(pl.multiple_of(dev * rows + s, 16), z)]
-    def own(c):
-        s, z, _ = plan[c]
-        return x_ref.at[pl.ds(s, z)]
-    waits = []
-    events = []
-    for c, (s, z, order) in enumerate(plan):
-        stage, last = tree_info(order)
-        for m in range(nm):
-            events.append((last(m) * 2 + (c if last(m) >= 0 else 0), c, m))
-    events.sort()
-    idx = {c: 0 for c in range(len(plan))}
-    local = []
-    for _, c, m in events:
-        s, z, order = plan[c]
-        stage, last = tree_info(order)
+        pl.semaphore_signal(barrier, inc=1, device_id=(me ^ (1 << b), core), device_id_type=MESH)
+    pl.semaphore_signal(barrier, inc=1, device_id=(me, 1 - core), device_id_type=MESH)
+    pl.semaphore_wait(barrier, nbits + 1)
+
+
+def spread_steps(plan, nbits, rows, source, out_ref, sems):
+    ssem, rsem, ssib, rsib, lsem = sems
+    me, core = lax.axis_index("dp"), lax.axis_index("opt")
+    masks = range(1 << nbits)
+    trees = [Tree(order) for _, _, order in plan]
+
+    def region(c, m, o):
+        first, size, _ = plan[c]
+        return out_ref.at[pl.ds(pl.multiple_of(((me ^ m) * 2 + o) * rows + first, 16), size)]
+
+    def down(c, m):
+        parent = m ^ trees[c].bit(m)
+        return lambda sending: pltpu.make_async_remote_copy(
+            (source(c) if parent == 0 else region(c, parent, core)) if sending else region(c, m, core),
+            region(c, parent, core) if sending else region(c, m, core),
+            ssem.at[c, m], rsem.at[c, m], device_id=(me ^ trees[c].bit(m), core), device_id_type=MESH,
+        )
+
+    def across(c, m):
+        return pltpu.make_async_remote_copy(
+            region(c, m, core) if m else source(c), region(c, m, core),
+            ssib.at[c, m], rsib.at[c, m], device_id=(me, 1 - core), device_id_type=MESH,
+        )
+
+    def arrived(c, m):
+        ref = region(c, m, 1 - core)
+        return pltpu.make_async_remote_copy(
+            ref, ref, ssib.at[c, m], rsib.at[c, m], device_id=(me, 1 - core), device_id_type=MESH
+        )
+
+    def keep(c):
+        return pltpu.make_async_copy(source(c), region(c, 0, core), lsem.at[c, 0])
+
+    def step(c, m):
         if m:
-            b = order[last(m)]
-            pltpu.make_async_remote_copy(region(c, m), region(c, m), ssem.at[c, 0], rsem.at[c, m], device_id=(me ^ (1 << b), core), device_id_type=MESH).wait_recv()
-        src = region(c, m) if m else own(c)
-        for t in range(last(m) + 1, nbits):
-            b = order[t]
-            cp = pltpu.make_async_remote_copy(src, region(c, m), ssem.at[c, idx[c]], rsem.at[c, m | (1 << b)], device_id=(me ^ (1 << b), core), device_id_type=MESH)
-            cp.start(); waits.append(cp); idx[c] += 1
-        cp = pltpu.make_async_remote_copy(src, region(c, m), ssib.at[c, m], rsib.at[c, m], device_id=(me, 1 - core), device_id_type=MESH)
-        cp.start(); waits.append(cp)
+            down(c, m)(False).wait_recv()
+        for child in trees[c].children(m):
+            down(c, child)(True).start()
+        across(c, m).start()
         if m == 0:
-            cp = pltpu.make_async_copy(src, region(c, 0), lsem.at[c]); cp.start(); local.append(cp)
-    for c in range(len(plan)):
-        for m in range(nm):
-            r = region(c, m, 1 - core)
-            pltpu.make_async_remote_copy(r, r, ssib.at[c, m], rsib.at[c, m], device_id=(me, 1 - core), device_id_type=MESH).wait_recv()
-    for cp in waits: cp.wait_send()
-    for cp in local: cp.wait()
-
-def gather_rows(x, dp_count, cid):
-    rows = x.shape[0]
+            keep(c).start()
+
+    def end():
+        for c in range(len(plan)):
+            for m in masks:
+                arrived(c, m).wait_recv()
+                across(c, m).wait_send()
+                if m:
+                    down(c, m)(True).wait_send()
+            keep(c).wait()
+
+    keys = sorted((trees[c].last(m) * 100 + trees[c].rank(m) * (trees[c].last(m) + 2), c, m) for c in range(len(plan)) for m in masks)
+    return [functools.partial(step, c, m) for _, c, m in keys], end
+
+
+def sum_steps(plan, nbits, rows, terms_ref, put, own, sib, land, sems):
+    ssem, rsem, ssib, rsib, lsem = sems
+    me, core = lax.axis_index("dp"), lax.axis_index("opt")
+    trees = [Tree(order) for _, _, order in plan]
+
+    def span(c):
+        return pl.ds(plan[c][0], plan[c][1])
+
+    def source(c, m, o):
+        first, size, _ = plan[c]
+        return terms_ref.at[pl.ds(pl.multiple_of(((me ^ m) * 2 + o) * rows + first, 16), size)]
+
+    def load(c, m):
+        return pltpu.make_async_copy(source(c, m, core), own.at[m, span(c)], lsem.at[c, m])
+
+    def across(c, m):
+        return pltpu.make_async_remote_copy(
+            source(c, m, 1 - core), sib.at[m, span(c)], ssib.at[c, m], rsib.at[c, m],
+            device_id=(me, 1 - core), device_id_type=MESH,
+        )
+
+    def up(c, m):
+        return pltpu.make_async_remote_copy(
+            own.at[m, span(c)], land.at[m - 1, span(c)], ssem.at[c, m], rsem.at[c, m],
+            device_id=(me ^ trees[c].bit(m), core), device_id_type=MESH,
+        )
+
+    def step(c, m):
+        first, size, _ = plan[c]
+        load(c, m).wait()
+        across(c, m).wait_recv()
+        arrived = [child - 1 for child in trees[c].children(m)]
+        for child in reversed(trees[c].children(m)):
+            up(c, child).wait_recv()
+
+        def add(i, count):
+            at = pl.ds(pl.multiple_of(first + i * BLK, 16), count)
+            total = own[m, at, :].astype(f32) + sib[m, at, :].astype(f32)
+            for child in arrived:
+                total = total + land[child, at, :].astype(f32)
+            if m:
+                own[m, at, :] = to_low(total)
+            else:
+                put(at, total)
+
+        def body(i, carry):
+            add(i, BLK)
+            return carry
+
+        lax.fori_loop(0, size // BLK, body, 0)
+        if size % BLK:
+            add(size // BLK, size % BLK)
+        if m:
+            up(c, m).start()
+
+    stages = lambda c, m: nbits - 1 - trees[c].last(m)
+    keys = sorted(
+        (stages(c, m) * 8 + trees[c].rank(m) * 8 + 2 * c, c, m) for c in range(len(plan)) for m in range(1 << nbits)
+    )
+
+    def begin():
+        for _, c, m in keys:
+            load(c, m).start()
+            across(c, m).start()
+
+    def end():
+        for _, c, m in keys:
+            across(c, m).wait_send()
+            if m:
+                up(c, m).wait_send()
+
+    return begin, [functools.partial(step, c, m) for _, c, m in keys], end
+
+
+def tree_sems(plan, nbits):
+    return [pltpu.SemaphoreType.DMA((len(plan), 1 << nbits))] * 5
+
+
+def sum_scratch(rows, nbits):
+    many = 1 << nbits
+    return [pltpu.VMEM((count, rows, BLK), bf16) for count in (many, many, many - 1)]
+
+
+def gather_kernel(plan, nbits, rows, shard, out_ref, *sems):
+    enter_tree(nbits)
+    steps, end = spread_steps(plan, nbits, rows, lambda c: shard.at[pl.ds(plan[c][0], plan[c][1])], out_ref, sems)
+    for step in steps:
+        step()
+    end()
+
+
+def gather_rows(shard, dp_count, cid):
+    rows = shard.shape[0]
     nbits = dp_count.bit_length() - 1
-    plan = chunk_plan(rows, nbits)
-    nm = 1 << nbits; nc = len(plan)
-    return pl.pallas_call(functools.partial(gather_kernel, plan, nbits, rows),
-        out_shape=jax.ShapeDtypeStruct((dp_count * 2 * rows, 128), x.dtype),
-        in_specs=[pl.BlockSpec(memory_space=pl.ANY)], out_specs=pl.BlockSpec(memory_space=pl.ANY),
-        scratch_shapes=[pltpu.SemaphoreType.DMA((nc, nm)), pltpu.SemaphoreType.DMA((nc, nm)), pltpu.SemaphoreType.DMA((nc, nm)), pltpu.SemaphoreType.DMA((nc, nm)), pltpu.SemaphoreType.DMA((nc,))],
+    plan = chunk_plan(rows, nbits, "ABABABCD", (1,) * 8)
+    return pl.pallas_call(
+        functools.partial(gather_kernel, plan, nbits, rows),
+        out_shape=jax.ShapeDtypeStruct((dp_count * 2 * rows, BLK), shard.dtype),
+        in_specs=[pl.BlockSpec(memory_space=pl.ANY)],
+        out_specs=pl.BlockSpec(memory_space=pl.ANY),
+        scratch_shapes=tree_sems(plan, nbits),
+        compiler_params=pltpu.CompilerParams(collective_id=cid, has_side_effects=True),
         name="gather_rows",
-        compiler_params=pltpu.CompilerParams(collective_id=cid, has_side_effects=True))(x)
-
-def scatter_kernel(plan, nbits, rows, s_ref, out_ref, own, sib, land, ssem, rsem, ssib, rsib, lsem):
-    me = lax.axis_index("dp"); core = lax.axis_index("opt")
-    bar = pltpu.get_barrier_semaphore()
-    for b in range(nbits):
-        pl.semaphore_signal(bar, inc=1, device_id=(me ^ (1 << b), core), device_id_type=MESH)
-    pl.semaphore_signal(bar, inc=1, device_id=(me, 1 - core), device_id_type=MESH)
-    nm = 1 << nbits
-    def src(c, m, o):
-        s, z, _ = plan[c]
-        dev = (me ^ m) * 2 + o
-        return s_ref.at[pl.ds(pl.multiple_of(dev * rows + s, 16), z)]
-    def send_stage(order, m):
-        rev = order[::-1]
-        return min([t for t in range(nbits) if m >> rev[t] & 1], default=nbits)
-    events = sorted((send_stage(order, m) * 2 + c, c, m) for c, (s, z, order) in enumerate(plan) for m in range(nm))
-    loads = {}
-    for _, c, m in events:
-        s, z, _o = plan[c]
-        cp = pltpu.make_async_copy(src(c, m, core), own.at[m, pl.ds(s, z)], lsem.at[c, m]); cp.start(); loads[c, m] = cp
-    pl.semaphore_wait(bar, nbits + 1)
-    sends = []
-    for _, c, m in events:
-        s, z, _o = plan[c]
-        cp = pltpu.make_async_remote_copy(src(c, m, 1 - core), sib.at[m, pl.ds(s, z)], ssib.at[c, m], rsib.at[c, m], device_id=(me, 1 - core), device_id_type=MESH)
-        cp.start(); sends.append(cp)
-    for _, c, m in events:
-        s, z, order = plan[c]
-        rev = order[::-1]
-        st = send_stage(order, m)
-        loads[c, m].wait()
-        here = own.at[m, pl.ds(s, z)]
-        pltpu.make_async_remote_copy(here, sib.at[m, pl.ds(s, z)], ssib.at[c, m], rsib.at[c, m], device_id=(me, 1 - core), device_id_type=MESH).wait_recv()
-        terms = [own.at[m], sib.at[m]]
-        for t in range(st):
-            mm = m | (1 << rev[t])
-            pltpu.make_async_remote_copy(here, land.at[mm - 1, pl.ds(s, z)], ssem.at[c, mm], rsem.at[c, mm], device_id=(me ^ (1 << rev[t]), core), device_id_type=MESH).wait_recv()
-            terms.append(land.at[mm - 1])
-        step = 128
-        def add(i, k):
-            r = pl.ds(pl.multiple_of(s + i * step, 16), k)
-            total = terms[0][r, :].astype(jnp.float32) + terms[1][r, :].astype(jnp.float32)
-            for x in terms[2:]:
-                total = total + x[r, :].astype(jnp.float32)
-            if m:
-                own[m, r, :] = total.astype(jnp.bfloat16)
-            else:
-                out_ref[r, :] = total
-        def body(i, carry):
-            add(i, step); return carry
-        lax.fori_loop(0, z // step, body, 0)
-        if z % step:
-            add(z // step, z % step)
-        if m:
-            cp = pltpu.make_async_remote_copy(here, land.at[m - 1, pl.ds(s, z)], ssem.at[c, m], rsem.at[c, m], device_id=(me ^ (1 << rev[st]), core), device_id_type=MESH)
-            cp.start(); sends.append(cp)
-    for cp in sends: cp.wait_send()
-
-def scatter_rows(s, dp_count, cid):
-    rows = s.shape[0] // (dp_count * 2)
+    )(shard)
+
+
+def total_kernel(plan, nbits, rows, terms, out_ref, own, sib, land, *sems):
+    enter_tree(nbits)
+
+    def put(at, total):
+        own[0, at, :] = to_low(total)
+
+    begin, steps, end = sum_steps(plan, nbits, rows, terms, put, own, sib, land, sems[:5])
+    begin()
+    for step in steps:
+        step()
+    more, last = spread_steps(plan, nbits, rows, lambda c: own.at[0, pl.ds(plan[c][0], plan[c][1])], out_ref, sems[5:])
+    for step in more:
+        step()
+    end()
+    last()
+
+
+def total_rows_all(terms, dp_count, cid):
+    rows = terms.shape[0] // (dp_count * 2)
     nbits = dp_count.bit_length() - 1
-    plan = chunk_plan(rows, nbits)
-    nm = 1 << nbits; nc = len(plan)
-    return pl.pallas_call(functools.partial(scatter_kernel, plan, nbits, rows),
-        out_shape=jax.ShapeDtypeStruct((rows, 128), jnp.float32),
-        in_specs=[pl.BlockSpec(memory_space=pl.ANY)], out_specs=pl.BlockSpec(memory_space=pltpu.VMEM),
-        scratch_shapes=[pltpu.VMEM((nm, rows, 128), jnp.bfloat16), pltpu.VMEM((nm, rows, 128), jnp.bfloat16), pltpu.VMEM((nm - 1, rows, 128), jnp.bfloat16)]
-          + [pltpu.SemaphoreType.DMA((nc, nm))] * 5,
-        name="scatter_rows",
-        compiler_params=pltpu.CompilerParams(collective_id=cid, has_side_effects=True, vmem_limit_bytes=60 << 20))(s)
+    plan = chunk_plan(rows, nbits, "ABCD", (3, 3, 1, 1))
+    return pl.pallas_call(
+        functools.partial(total_kernel, plan, nbits, rows),
+        out_shape=jax.ShapeDtypeStruct(terms.shape, bf16),
+        in_specs=[pl.BlockSpec(memory_space=pl.ANY)],
+        out_specs=pl.BlockSpec(memory_space=pl.ANY),
+        scratch_shapes=sum_scratch(rows, nbits) + tree_sems(plan, nbits) * 2,
+        compiler_params=pltpu.CompilerParams(collective_id=cid, has_side_effects=True, vmem_limit_bytes=VMEM_CAP),
+        name="total_rows",
+    )(terms)
 
 
 def strip_kernel(table, buckets, out):
@@ -318,7 +406,8 @@
         [strip[(3 - n) * BLK : (3 - n) * BLK + rows, :] for n in (offset, offset + 1)], axis=1
     )
     key_at = lax.broadcasted_iota(jnp.int32, scores.shape, 0)
-    return jnp.where(key_at < length, scores + bias, neg_fill)
+    scores = scores + bias
+    return jnp.concatenate([scores[:SURE], jnp.where(key_at[SURE:] < length, scores[SURE:], neg_fill)], axis=0)
 
 
 def attend_kernel(rows_ref, lengths, x_ref, gathered, gains, strips, qkv, lse, mixed, hidden, wqkv, wout, sems):
@@ -356,7 +445,7 @@
                 expos = jnp.exp(scores - peak)
                 total = jnp.sum(expos, axis=0, keepdims=True)
                 lse[0, pl.ds(2 * pair + head, 1), n * 256 : (n + 1) * 256] = peak + jnp.log(total)
-                outs.append(dot(turned, to_low(expos * (1.0 / total))))
+                outs.append(dot(turned, to_low(expos)) * (1.0 / total))
             lane = lax.broadcasted_iota(jnp.int32, (BLK, 256), 0)
             both = jnp.where(lane < HD, outs[0], outs[1])
             mixed[n * 256 : (n + 1) * 256, pl.ds(at, BLK)] = to_low(both.T)
@@ -409,7 +498,7 @@
     )(rows, lengths, enc_in, gathered, gains, strips)
 
 
-FCHUNK = 512
+FCHUNK = 1024
 
 
 def feed_kernel(rows_ref, hidden, gathered, gains, inner, output, encoded, cross, wup, wdown, wkv, sems):
@@ -449,7 +538,7 @@
 
 def encoder_feed(rows, hidden, gathered, gains):
     total = hidden.shape[0]
-    tile = 256
+    tile = 512
     by_row = lambda p, *_: (p, 0)
     return pl.pallas_call(
         feed_kernel,
@@ -569,9 +658,37 @@
     )(rows, output, hidden, inner, upstream, gathered, gains)
 
 
-def attend_back_kernel(lengths, q_ref, k_ref, v_ref, go_ref, lse, strips, gq_ref, gk_ref, gv_ref, bias_sums):
+def attend_back_kernel(
+    plan, nbits, rows, lengths, q_ref, k_ref, v_ref, go_ref, lse, strips, *refs
+):
+    if plan is None:
+        gq_ref, gk_ref, gv_ref, bias_sums = refs
+    else:
+        terms, gq_ref, gk_ref, gv_ref, bias_sums, reduced, own, sib, land, *sems = refs
     pair = pl.program_id(0)
     step = pl.program_id(1)
+    at = pair * pl.num_programs(1) + step
+    total_steps = PAIRS * PASS_EX
+
+    if plan is not None:
+
+        def put(where, total):
+            reduced[where, :] = to_low(total)
+
+        begin, steps, end = sum_steps(plan, nbits, rows, terms, put, own, sib, land, sems)
+
+        @pl.when(at == 0)
+        def _():
+            enter_tree(nbits)
+            begin()
+
+        for k in range(1, total_steps):
+            some = steps[len(steps) * (k - 1) // (total_steps - 1) : len(steps) * k // (total_steps - 1)]
+
+            @pl.when(at == k)
+            def _(some=some):
+                for one in some:
+                    one()
 
     @pl.when(step == 0)
     def _():
@@ -611,32 +728,59 @@
     gk_ref[...] = to_low(key_grad)
     gv_ref[...] = to_low(value_grad)
 
-
-def attend_back(lengths, qkv, mixed_grad, lse, strips):
+    if plan is not None:
+
+        @pl.when(at == total_steps - 1)
+        def _():
+            end()
+
+
+def attend_back(lengths, qkv, mixed_grad, lse, strips, terms, dp_count, cid):
     count = lengths.shape[0]
     total = count * PASS_SLOT
     block = (PASS_SLOT, BLK)
     place = pl.BlockSpec(block, lambda a, p, *_: (p, a))
-    return pl.pallas_call(
-        attend_back_kernel,
+    strip = pl.BlockSpec((2, STRIP, BLK), lambda a, p, *_: (a, 0, 0))
+    in_specs = [
+        place,
+        pl.BlockSpec(block, lambda a, p, *_: (p, a + PAIRS)),
+        pl.BlockSpec(block, lambda a, p, *_: (p, a + 2 * PAIRS)),
+        place,
+        pl.BlockSpec((1, 16, PASS_SLOT), lambda a, p, *_: (p, 0, 0)),
+        strip,
+    ]
+    out_specs = [place, place, place, strip]
+    out_shape = [jax.ShapeDtypeStruct((total, D), bf16)] * 3 + [jax.ShapeDtypeStruct((H, STRIP, BLK), f32)]
+    operands = [qkv, qkv, qkv, mixed_grad, lse, strips]
+    scratch = []
+    plan, nbits, rows = None, 0, 0
+    params = dict(vmem_limit_bytes=VMEM_CAP)
+    if dp_count == 16:
+        rows = terms.shape[0] // (2 * dp_count)
+        nbits = dp_count.bit_length() - 1
+        plan = chunk_plan(rows, nbits, "ABCDAB", (3, 3, 2, 2, 3, 3))
+        in_specs.append(pl.BlockSpec(memory_space=pl.ANY))
+        out_specs.append(pl.BlockSpec((rows, BLK), lambda a, p, *_: (0, 0)))
+        out_shape.append(jax.ShapeDtypeStruct((rows, BLK), bf16))
+        operands.append(terms)
+        scratch = sum_scratch(rows, nbits) + tree_sems(plan, nbits)
+        params.update(collective_id=cid, has_side_effects=True)
+    results = pl.pallas_call(
+        functools.partial(attend_back_kernel, plan, nbits, rows),
         grid_spec=pltpu.PrefetchScalarGridSpec(
             num_scalar_prefetch=1,
             grid=(PAIRS, count),
-            in_specs=[
-                place,
-                pl.BlockSpec(block, lambda a, p, *_: (p, a + PAIRS)),
-                pl.BlockSpec(block, lambda a, p, *_: (p, a + 2 * PAIRS)),
-                place,
-                pl.BlockSpec((1, 16, PASS_SLOT), lambda a, p, *_: (p, 0, 0)),
-                pl.BlockSpec((2, STRIP, BLK), lambda a, p, *_: (a, 0, 0)),
-            ],
-            out_specs=[place, place, place, pl.BlockSpec((2, STRIP, BLK), lambda a, p, *_: (a, 0, 0))],
+            in_specs=in_specs,
+            out_specs=out_specs,
+            scratch_shapes=scratch,
         ),
-        out_shape=[jax.ShapeDtypeStruct((total, D), bf16)] * 3
-        + [jax.ShapeDtypeStruct((H, STRIP, BLK), f32)],
-        compiler_params=pltpu.CompilerParams(vmem_limit_bytes=VMEM_CAP),
+        out_shape=out_shape,
+        compiler_params=pltpu.CompilerParams(**params),
         name="attend_back",
-    )(lengths, qkv, qkv, qkv, mixed_grad, lse, strips)
+    )(lengths, *operands)
+    if plan is None:
+        return *results, lax.psum_scatter(terms, ("dp", "opt"), scatter_dimension=0, tiled=True)
+    return results
 
 
 def input_back_kernel(
@@ -1053,114 +1197,252 @@
     )(one, two)
 
 
-def weight_kernel(first, tile, chunk, cols, has_into, rows_ref, *refs):
-    if has_into:
-        left, right, into, slots, turned, held, sems = refs
-    else:
-        left, right, slots, turned, held, sems = refs
+SQUARE = D * D // BLK
+GROUP_ONE = 2 * D * FF // BLK + 3 * SQUARE
+SMALL_ROWS = 512
+GROUP_TWO = 3 * SQUARE + SMALL_ROWS
+
+
+def put_blocks(out_ref, values, at=0):
+    down, across = values.shape[0] // BLK, values.shape[1] // BLK
+    for i in range(down):
+        for j in range(across):
+            out_ref[pl.ds(at + (i * across + j) * BLK, BLK), :] = to_low(
+                values[i * BLK : (i + 1) * BLK, j * BLK : (j + 1) * BLK]
+            )
+
+
+def up_weight_kernel(left, right, out_ref):
+    put_blocks(out_ref, dot_tn(left[...], right[...]))
+
+
+def up_weight(left, right):
+    count = left.shape[0]
+    tile = 256
+    return pl.pallas_call(
+        up_weight_kernel,
+        grid=(D // tile,),
+        in_specs=[pl.BlockSpec((count, tile), lambda p: (0, p)), pl.BlockSpec((count, FF), lambda p: (0, 0))],
+        out_specs=pl.BlockSpec((tile * FF // BLK, BLK), lambda p: (p, 0)),
+        out_shape=jax.ShapeDtypeStruct((GROUP_ONE, BLK), bf16),
+        compiler_params=pltpu.CompilerParams(vmem_limit_bytes=VMEM_CAP),
+        name="up_weight",
+    )(left, right)
+
+
+def down_weight_kernel(left, right, into, out_ref):
+    put_blocks(out_ref, dot_tn(left[...], right[...]))
+
+
+def down_weight(left, right, into):
+    count = left.shape[0]
+    first = D * FF // BLK // SQUARE
+    return pl.pallas_call(
+        down_weight_kernel,
+        grid=(FF // D,),
+        in_specs=[
+            pl.BlockSpec((count, D), lambda p: (0, p)),
+            pl.BlockSpec((count, D), lambda p: (0, 0)),
+            pl.BlockSpec(memory_space=pl.ANY),
+        ],
+        out_specs=pl.BlockSpec((SQUARE, BLK), lambda p: (first + p, 0)),
+        out_shape=jax.ShapeDtypeStruct(into.shape, bf16),
+        input_output_aliases={2: 0},
+        compiler_params=pltpu.CompilerParams(vmem_limit_bytes=VMEM_CAP),
+        name="down_weight",
+    )(left, right, into)
+
+
+def square_weight_kernel(pairs, has_into, *refs):
+    sources, refs = refs[: len(pairs[0])], refs[len(pairs[0]) + has_into :]
+    out_ref, held, sems = refs
+    step = pl.program_id(0)
+    columns, products = pairs
+
+    def fetch(k):
+        source, col = columns[k]
+        return pltpu.make_async_copy(sources[k].at[:, pl.ds(col, D)], held.at[k], sems.at[k])
+
+    @pl.when(step == 0)
+    def _():
+        for k in range(len(columns)):
+            fetch(k).start()
+
+    seen = set()
+    for m, (a, b) in enumerate(products):
+        fresh = [k for k in (a, b) if k not in seen]
+        seen.update(fresh)
+
+        @pl.when(step == m)
+        def _(a=a, b=b, fresh=fresh):
+            for k in fresh:
+                fetch(k).wait()
+            put_blocks(out_ref, dot_tn(held[a], held[b]))
+
+
+def square_weight(operands, products, into, first, total):
+    any_space = pl.BlockSpec(memory_space=pl.ANY)
+    arrays = [array for array, _ in operands]
+    columns = [(k, col) for k, (_, col) in enumerate(operands)]
+    count = arrays[0].shape[0]
+    extra = [] if into is None else [into]
+    return pl.pallas_call(
+        functools.partial(square_weight_kernel, (columns, products), len(extra)),
+        grid=(len(products),),
+        in_specs=[any_space] * (len(arrays) + len(extra)),
+        out_specs=pl.BlockSpec((SQUARE, BLK), lambda p: (first + p, 0)),
+        scratch_shapes=[pltpu.VMEM((len(arrays), count, D), bf16), pltpu.SemaphoreType.DMA((len(arrays),))],
+        out_shape=jax.ShapeDtypeStruct((total, BLK), bf16),
+        input_output_aliases={len(arrays): 0} if extra else {},
+        compiler_params=pltpu.CompilerParams(vmem_limit_bytes=VMEM_CAP),
+        name="square_weight",
+    )(*arrays, *extra)
+
+
+HELD = 16
+REST = ALEN - HELD
+
+
+def pack_rows(groups):
+    sides = [jnp.concatenate(group, axis=1) if len(group) > 1 else group[0] for group in groups]
+    main = jnp.concatenate([side[:HELD] for side in sides], axis=1)
+    width = max(side.shape[1] for side in sides)
+    rest = jnp.concatenate([jnp.pad(side[HELD:ALEN], ((0, 0), (0, width - side.shape[1]))) for side in sides], axis=0)
+    return jnp.concatenate([main, pad_rows(rest, HELD)], axis=1)
+
+
+def block_table():
+    table = np.zeros((1009, 8), np.int32)
+    wide = D // BLK
+    early, late = 3 * wide, 5 * wide
+    rows = (
+        (DEC_QKV, 108, 1, 0, 0, early, late, 0),
+        (DEC_OUT, 36, 1, wide, 3 * wide, early, late, 1),
+        (CROSS_Q, 36, 1, 2 * wide, 4 * wide, early, late, 2),
+        (DEC_UP, 144, 4, 0, wide, 12 * wide, 13 * wide, 0),
+        (DEC_DOWN, 144, 4, 5 * wide, 9 * wide, 12 * wide, 16 * wide, 1),
+        (CROSS_OUT, 36, 4, 10 * wide, 11 * wide, 12 * wide, 13 * wide, 2),
+    )
+    for first, count, kind, left, right, rest_left, rest_right, group in rows:
+        for b in range(count):
+            if first == DEC_QKV:
+                m, k = divmod(b, 36)
+                i, j = divmod(k, wide)
+                j = j + wide * m
+            else:
+                i, j = divmod(b, 4 * wide if first == DEC_UP else wide)
+            table[first + b] = (kind, 0, left + i, right + j, rest_left + i, rest_right + j, group, 0)
+    for first, count, at in ((ENC_UP, 144, 0), (ENC_DOWN, 144, 144), (CROSS_KV, 72, 288), (ENC_OUT, 36, 360)):
+        for b in range(count):
+            table[first + b, :2] = (2, at + b)
+    for b in range(108):
+        table[b, :2] = (3, b)
+    return table
+
+
+def update_kernel(
+    slots, info, early, middle, late, one, two, master, stats, roots,
+    grads, new_stats, new_master, sides, held, summed, sems,
+):
     step = pl.program_id(0)
     steps = pl.num_programs(0)
-    across = cols // BLK
-    down = tile // BLK
-    turned[...] = left[...].T
-    parts = cols // chunk
-    for c in range(parts):
-        slot = c % 2
-        buffer = held.at[slot]
-
-        def drain():
-            wait_whole(held.at[slot], sems.at[slot])
-
-        if c >= 2:
-            drain()
-        else:
-            pl.when(step > 0)(drain)
-        held[slot] = to_low(dot(turned[...], right[:, c * chunk : (c + 1) * chunk]))
-        for i in range(down):
-            for j in range(chunk // BLK):
-                row = pl.multiple_of(rows_ref[first + (step * down + i) * across + c * (chunk // BLK) + j], 16)
-                pltpu.make_async_copy(
-                    buffer.at[pl.ds(i * BLK, BLK), pl.ds(j * BLK, BLK)], slots.at[pl.ds(row, BLK)], sems.at[slot]
-                ).start()
-
-    @pl.when(step == steps - 1)
+
+    def each(step, action):
+        buffer = lax.rem(step, 2)
+        for s in range(slots):
+            at = (step * slots + s) * 8
+            kind = info[at]
+
+            def copy(source, dest, k, s=s):
+                return pltpu.make_async_copy(source, dest, sems.at[buffer, s, k])
+
+            def rows_of(left, right, s=s, at=at, copy=copy):
+                for k, source in enumerate((left, right, left, right)):
+                    col = pl.multiple_of(info[at + 2 + k] * BLK, BLK)
+                    action(copy(source.at[:, pl.ds(col, BLK)], sides.at[buffer, s, k], k))
+
+            def block_of(source, s=s, at=at, copy=copy):
+                row = pl.multiple_of(info[at + 1] * BLK, BLK)
+                action(copy(source.at[pl.ds(row, BLK)], held.at[buffer, s], 4))
+
+            pl.when(kind == 1)(functools.partial(rows_of, early, late))
+            pl.when(kind == 4)(functools.partial(rows_of, middle, middle))
+            pl.when(kind == 2)(functools.partial(block_of, one))
+            pl.when(kind == 3)(functools.partial(block_of, two))
+
+    @pl.when(step == 0)
     def _():
-        for slot in range(min(2, parts)):
-            wait_whole(held.at[slot], sems.at[slot])
-
-
-def weight_slots(rows, left, right, first, into, total_rows, chunk=D, tile=256):
-    count, down = left.shape
-    cols = right.shape[1]
-    assert cols // chunk >= 2 or cols == chunk
-    any_space = pl.BlockSpec(memory_space=pl.ANY)
-    operands = (rows, left, right) + (() if into is None else (into,))
-    if cols == chunk:
-        chunk = cols // 2
-    return pl.pallas_call(
-        functools.partial(weight_kernel, first, tile, chunk, cols, into is not None),
-        grid_spec=pltpu.PrefetchScalarGridSpec(
-            num_scalar_prefetch=1,
-            grid=(down // tile,),
-            in_specs=[
-                pl.BlockSpec((count, tile), lambda p, *_: (0, p)),
-                pl.BlockSpec((count, cols), lambda p, *_: (0, 0)),
-            ]
-            + ([] if into is None else [any_space]),
-            out_specs=any_space,
-            scratch_shapes=[
-                pltpu.VMEM((tile, count), bf16),
-                pltpu.VMEM((2, tile, chunk), bf16),
-                pltpu.SemaphoreType.DMA((2,)),
-            ],
-        ),
-        out_shape=jax.ShapeDtypeStruct((total_rows, BLK), bf16),
-        input_output_aliases={} if into is None else {3: 0},
-        compiler_params=pltpu.CompilerParams(vmem_limit_bytes=VMEM_CAP),
-        name="weight_slots",
-    )(*operands)
-
-
-def exact(left, right, dims):
-    return lax.dot_general(left, right, (dims, ((), ())), precision=exact_prec, preferred_element_type=f32)
-
-
-def update_kernel(slots, has_ref, sums, master, stats, roots, grads, new_stats, new_master):
+        each(step, lambda copy: copy.start())
+
+    @pl.when(step + 1 < steps)
+    def _():
+        each(step + 1, lambda copy: copy.start())
+
+    each(step, lambda copy: copy.wait())
+    buffer = lax.rem(step, 2)
     for s in range(slots):
-        has = has_ref[pl.program_id(0) * slots + s]
-        grad = sums[s * BLK : (s + 1) * BLK, :]
-        grad = jnp.where(has > 0, grad, 0.0)
+        at = (step * slots + s) * 8
+        kind = info[at]
+        group = info[at + 6]
+
+        @pl.when((kind == 1) | (kind == 4))
+        def _(s=s, group=group):
+            rest = sides[buffer, s, 2]
+            row = lax.broadcasted_iota(jnp.int32, rest.shape, 0)
+            mine = jnp.where(row % HELD // REST == group, rest, jnp.zeros_like(rest))
+            summed[s] = dot_tn(sides[buffer, s, 0], sides[buffer, s, 1]) + dot_tn(mine, sides[buffer, s, 3])
+
+        @pl.when((kind == 2) | (kind == 3))
+        def _(s=s):
+            summed[s] = held[buffer, s].astype(f32)
+
+        @pl.when(kind == 0)
+        def _(s=s):
+            summed[s] = jnp.zeros((BLK, BLK), f32)
+
+    for s in range(slots):
+        grad = summed[s]
+        low = to_low(grad)
         grads[s] = grad
-        new_stats[s, 0] = stat_decay * stats[s, 0] + (1.0 - stat_decay) * exact(grad, grad, ((1,), (1,)))
-        new_stats[s, 1] = stat_decay * stats[s, 1] + (1.0 - stat_decay) * exact(grad, grad, ((0,), (0,)))
-        shaped = exact(roots[s, 0], grad, ((1,), (0,)))
-        shaped = exact(shaped, roots[s, 1], ((1,), (0,)))
+        new_stats[s, 0] = stat_decay * stats[s, 0] + (1.0 - stat_decay) * dot_nt(low, low)
+        new_stats[s, 1] = stat_decay * stats[s, 1] + (1.0 - stat_decay) * dot_tn(low, low)
+        shaped = dot(to_low(roots[s, 0]), low)
+        shaped = dot(to_low(shaped), to_low(roots[s, 1]))
         old = master[s]
         shaped_rms = jnp.sqrt(jnp.mean(shaped * shaped) + 1e-06)
         weight_rms = jnp.sqrt(jnp.mean(old * old) + 1e-06)
-        new_master[s] = old - block_rate * weight_rms * shaped / shaped_rms
-
-
-def update_blocks(has, sums, master, kron_stats, inverse_roots):
+        new_master[s] = old - (block_rate * weight_rms / shaped_rms) * shaped
+
+
+def update_blocks(info, early, middle, late, one, two, master, kron_stats, inverse_roots):
     count = master.shape[0]
     slots = min(4, count)
-    one = pl.BlockSpec((slots, BLK, BLK), lambda p, *_: (p, 0, 0))
-    two = pl.BlockSpec((slots, 2, BLK, BLK), lambda p, *_: (p, 0, 0, 0))
+    depth = early.shape[0]
+    any_space = pl.BlockSpec(memory_space=pl.ANY)
+    block = pl.BlockSpec((slots, BLK, BLK), lambda p, *_: (p, 0, 0))
+    pair = pl.BlockSpec((slots, 2, BLK, BLK), lambda p, *_: (p, 0, 0, 0))
     return pl.pallas_call(
         functools.partial(update_kernel, slots),
         grid_spec=pltpu.PrefetchScalarGridSpec(
             num_scalar_prefetch=1,
             grid=(count // slots,),
-            in_specs=[pl.BlockSpec((slots * BLK, BLK), lambda p, *_: (p, 0)), one, two, two],
-            out_specs=[one, two, one],
+            in_specs=[any_space] * 5 + [block, pair, pair],
+            out_specs=[block, pair, block],
+            scratch_shapes=[
+                pltpu.VMEM((2, slots, 4, depth, BLK), bf16),
+                pltpu.VMEM((2, slots, BLK, BLK), bf16),
+                pltpu.VMEM((slots, BLK, BLK), f32),
+                pltpu.SemaphoreType.DMA((2, slots, 5)),
+            ],
         ),
         out_shape=[
             jax.ShapeDtypeStruct(master.shape, f32),
             jax.ShapeDtypeStruct(kron_stats.shape, f32),
             jax.ShapeDtypeStruct(master.shape, f32),
         ],
+        compiler_params=pltpu.CompilerParams(vmem_limit_bytes=VMEM_CAP),
         name="update_blocks",
-    )(has, sums, master, kron_stats, inverse_roots)
+    )(info, early, middle, late, one, two, master, kron_stats, inverse_roots)
 
 
 def gather_all(shard, dp_count):
@@ -1169,10 +1451,14 @@
     return lax.all_gather(shard, ("dp", "opt"), axis=0, tiled=True)
 
 
-def scatter_all(terms, dp_count):
+def total_all(terms, dp_count):
     if dp_count == 16:
-        return scatter_rows(terms, dp_count, 1)
-    return lax.psum_scatter(terms, ("dp", "opt"), scatter_dimension=0, tiled=True).astype(f32)
+        return total_rows_all(terms, dp_count, 1)
+    return lax.psum(terms, ("dp", "opt"))
+
+
+def gather_low(rows):
+    return lax.all_gather(rows, ("dp", "opt"), axis=0, tiled=True)
 
 
 def pad_rows(array, rows):
@@ -1224,11 +1510,15 @@
         rows, dec_rows, gathered, gains, dec_bias
     )
     from_one, from_two = shifted(cross_queries, cross_queries, 1, 2)
+    early, enc_rows = lax.optimization_barrier(
+        (pack_rows(((dec_normed,), (dec_mixed,), (dec_normed_two,))), enc_in)
+    )
+    early = gather_low(early)
     queries = jnp.stack([cross_queries, from_one, from_two])
 
     owner_dp = passage_example // EX_DEV // pair_count
     offsets = ((lax.axis_index("dp") - owner_dp) % dp_count).astype(jnp.int32)
-    qkv, log_total, mixed, hidden = encoder_attend(rows, passage_lengths, enc_in, gathered, gains, strips)
+    qkv, log_total, mixed, hidden = encoder_attend(rows, passage_lengths, enc_rows, gathered, gains, strips)
     inner, output, encoded, memory = encoder_feed(rows, hidden, gathered, gains)
 
     parts = cross_attend(passage_lengths, offsets, queries, memory)
@@ -1240,6 +1530,11 @@
             jnp.broadcast_to(valid, (AROWS, BLK)), gathered, gains,
         )
     )
+    middle = pack_rows(
+        ((dec_normed_three, dec_inner_grad), (dec_act, dec_branch), (cross_mixed, cross_out_grad))
+    )
+    middle, back, early = lax.optimization_barrier((middle, back, early))
+    middle = gather_low(middle)
     back_one, back_two = shifted(back, back, 1, 4)
     memory_grad, query_parts, upstream = cross_back(
         rows, passage_lengths, offsets, queries, jnp.stack([back, back_one, back_two]), memory, enc_cot, gathered
@@ -1249,38 +1544,35 @@
         rows, jnp.stack([query_parts[0], query_one, query_two]), second_grad, first, dec_rows, dec_qkv, gathered, gains, dec_bias
     )
 
+    late = pack_rows(((dec_qkv_grad,), (dec_out_grad,), (cross_query_grad,)))
+    late, upstream = lax.optimization_barrier((late, upstream))
+
     act, inner_grad, branch, normed_two, hidden_grad, attn_grad, mixed_grad, gain_two = feed_back(
         rows, output, hidden, inner, upstream, gathered, gains
     )
-    grad_query, grad_key, grad_value, bias_sums = attend_back(passage_lengths, qkv, mixed_grad, log_total, strips)
+    late, middle, inner_grad = lax.optimization_barrier((late, middle, inner_grad))
+    late = gather_low(late)
+    one = up_weight(normed_two, inner_grad)
+    one = down_weight(act, branch, one)
+    one = square_weight(
+        [(encoded, 0), (memory_grad, 0), (memory_grad, D), (mixed, 0), (attn_grad, 0)],
+        [(0, 1), (0, 2), (3, 4)], one, 2 * D * FF // BLK // SQUARE, GROUP_ONE,
+    )
+    grad_query, grad_key, grad_value, bias_sums, one = attend_back(
+        passage_lengths, qkv, mixed_grad, log_total, strips, one, dp_count, 6
+    )
+    one, late = lax.optimization_barrier((one, late))
+    one = gather_low(one)
     enc_in_grad, normed, gain_one = input_back(
         rows, enc_in, grad_query, grad_key, grad_value, hidden_grad, gathered, gains
     )
-
-    slots = None
-    for left, right, at in (
-        (act, branch, ENC_DOWN),
-        (normed_two, inner_grad, ENC_UP),
-        (mixed, attn_grad, ENC_OUT),
-        (encoded, memory_grad[:, :D], CROSS_KV),
-        (encoded, memory_grad[:, D:], CROSS_KV + 36),
-        (normed, grad_query, ENC_QKV),
-        (normed, grad_key, ENC_QKV + 36),
-        (normed, grad_value, ENC_QKV + 72),
-        (dec_normed, dec_qkv_grad[:, :D], DEC_QKV),
-        (dec_normed, dec_qkv_grad[:, D : 2 * D], DEC_QKV + 36),
-        (dec_normed, dec_qkv_grad[:, 2 * D :], DEC_QKV + 72),
-        (dec_mixed, dec_out_grad, DEC_OUT),
-        (dec_normed_two, cross_query_grad, CROSS_Q),
-        (cross_mixed, cross_out_grad, CROSS_OUT),
-        (dec_normed_three, dec_inner_grad, DEC_UP),
-        (dec_act, dec_branch, DEC_DOWN),
-    ):
-        slots = weight_slots(rows, left, right, at, slots, total_rows)
-
-    middle = bias_sums[:, 2 * BLK : 5 * BLK].reshape(H, -1)
+    two = square_weight(
+        [(normed, 0), (grad_query, 0), (grad_key, 0), (grad_value, 0)], [(0, 1), (0, 2), (0, 3)], None, 0, GROUP_TWO
+    )
+
+    inner_strip = bias_sums[:, 2 * BLK : 5 * BLK].reshape(H, -1)
     strip_onehot = jnp.asarray(strip_buckets().reshape(-1, 1) == np.arange(NB)[None, :]).astype(f32)
-    enc_table = jnp.dot(middle, strip_onehot, precision=exact_prec, preferred_element_type=f32).T
+    enc_table = jnp.dot(inner_strip, strip_onehot, precision=exact_prec, preferred_element_type=f32).T
     enc_table = enc_table.at[NB // 2 - 1].add(jnp.sum(bias_sums[:, : 2 * BLK], axis=(1, 2)))
     enc_table = enc_table.at[NB - 1].add(jnp.sum(bias_sums[:, 5 * BLK :], axis=(1, 2)))
     dec_table = jnp.dot(
@@ -1289,16 +1581,16 @@
     small_terms = jnp.concatenate(
         [gain_one[0], gain_two[0], gain_two[1], gain_four[0], gain_four[1], gain_six[0], enc_table.reshape(-1), dec_table.reshape(-1)]
     )
-    small_rows = jnp.pad(
-        to_low(small_terms).reshape(devices, small_dev), ((0, 0), (0, EXTRA * BLK - small_dev))
-    ).reshape(devices, EXTRA, BLK)
-    slots = slots.reshape(devices, dev_rows, BLK).at[:, slot_dev * BLK :].set(small_rows).reshape(total_rows, BLK)
-
-    sums = scatter_all(slots, dp_count)
-    small_grads = sums[slot_dev * BLK :].reshape(-1)[:small_dev]
-    here = (lax.axis_index("dp") * pair_count + lax.axis_index("opt")) * slot_dev + jnp.arange(slot_dev)
-    has = jnp.any(owner_slot[None, :] == here[:, None], axis=1).astype(jnp.int32)
-    block_grads, new_stats, new_master = update_blocks(has, sums, master, kron_stats, inverse_roots)
+    small_rows = pad_rows(to_low(small_terms).reshape(-1, BLK), SMALL_ROWS)
+    two = total_all(lax.dynamic_update_slice(two, small_rows, (3 * SQUARE, 0)), dp_count)
+
+    device = lax.axis_index("dp") * pair_count + lax.axis_index("opt")
+    small_grads = lax.dynamic_slice(two[3 * SQUARE :].reshape(-1), (device * small_dev,), (small_dev,)).astype(f32)
+    here = device * slot_dev + jnp.arange(slot_dev)
+    place = jnp.where(owner_slot[None, :] == here[:, None], jnp.arange(owner_slot.shape[0])[None, :] + 1, 0)
+    block_at = jnp.sum(place, axis=1)
+    info = jnp.asarray(np.roll(block_table(), 1, axis=0))[block_at].reshape(-1)
+    block_grads, new_stats, new_master = update_blocks(info, early, middle, late, one, two, master, kron_stats, inverse_roots)
     new_moment = moment_decay * small_moment + small_grads
     new_small = small_params - small_rate * new_moment
     return (

time: 865 us -> 687 us (0.79)
  Pallas kernels: 805 us -> 608 us
  between operations: 1.25 us -> 14.9 us
    pallas_call x18 -> x6, Pallas kernels: 378 us -> 208 us  [the longest x1 86.8 us: attend_back(): pl.pallas_call(functools.partial(attend_back_kernel, plan, nbits, rows),...]
    pallas_call x1, Pallas kernels: 149 us -> 132 us  [gather_rows(): pl.pallas_call(functools.partial(gather_kernel, plan, nbits, rows), out_s...]
  transfers between devices with their start and end apart: 0 -> 4, of which waited for: 0 -> 1; matrix products, arithmetic and copies ran while one was open for 0% -> 6% of each run, Pallas kernels for 0% -> 66%
where the time goes in v2:
time: 687 us; the launch traced here: 679 us
  Pallas kernels  608 us (89%)
  local copies, waits for them, and re-layouts  34.5 us (5%)
  other arithmetic  15.1 us (2%)
  between operations  14.9 us (2%)
    pallas_call x1, Pallas kernels, gather_rows(): pl.pallas_call(functools.partial(gather_kernel, plan, nbits, rows), out_s...  132 us
    pallas_call x1, Pallas kernels, attend_back(): pl.pallas_call(functools.partial(attend_back_kernel, plan, nbits, rows),...  86.8 us
    pallas_call x1, Pallas kernels, total_rows_all(): pl.pallas_call(functools.partial(total_kernel, plan, nbits, rows), out_sh...  77.1 us
    pallas_call x1, Pallas kernels, encoder_attend(): pl.pallas_call(attend_kernel, grid_spec=pltpu.PrefetchScalarGridSpec(num_...  52.8 us
    pallas_call x4, Pallas kernels, shifted(): pl.pallas_call(functools.partial(shift_kernel, way), in_specs=[vmem, vmem...  40.9 us
    pallas_call x1, Pallas kernels, feed_back(): pl.pallas_call(feed_back_kernel, grid_spec=pltpu.PrefetchScalarGridSpec(n...  40.6 us
    pallas_call x1, Pallas kernels, encoder_feed(): pl.pallas_call(feed_kernel, grid_spec=pltpu.PrefetchScalarGridSpec(num_sc...  34.1 us
    pallas_call x3, Pallas kernels, decoder_call(): pl.pallas_call(body, grid_spec=pltpu.PrefetchScalarGridSpec(num_scalar_pr...  30.6 us
  transfers between devices with their start and end apart: 4, of which 1 were waited for; matrix products, arithmetic and copies ran while one was open for 6% of the time, Pallas kernels for 66%

profile of v2, /device:TPU:0, one launch (start us, length us, event | category | flops | bytes accessed | tf_op | source)
XLA Modules:
  0.0 678.5 jit_solution(3173876120547518066)
XLA Ops:
  10.7 132.4 %gather_rows.1.gathered = bf16[131584,128]{1,0:T(8,128)(2,1)} custom-call(bf16[4112,128]{1,0:T(8,128)(2,1)} %pad_maximum_fusion.shard), custom_call_target="tpu_custom_call" | custom-call | tf_op jit(solution)/shard_map/gather_rows/pallas_call | solution.py:334
  147.4 7.8 %decoder_self.1 = (bf16[32,2304]{1,0:T(8,128)(2,1)}, bf16[32,768]{1,0:T(8,128)(2,1)}, f32[32,768]{1,0:T(8,128)}, bf16[32,768]{1,0:T(8,128)(2,1)}, bf16[32,768]{1,0:T(8,128)(2,1)}, /*index=5*/bf16[32,768]{1,0:T(8,128)(2,1)}) custom-call(s32[1008]{0:T(1024)} %fusion.20.rows_ref, bf16[32,768]{1,0:T(8,128)(2,1)} %pad.52.dec_ref, ...), custom_call_target="tpu_custom_call" | custom-call | tf_op jit(solution)/shard_map/decoder_self/pallas_call | solution.py:917
  160.6 9.7 %shift_rows.4 = (bf16[32,768]{1,0:T(8,128)(2,1)}, bf16[32,768]{1,0:T(8,128)(2,1)}) custom-call(bf16[32,768]{1,0:T(8,128)(2,1)} %get-tuple-element.106.one.two, bf16[32,768]{1,0:T(8,128)(2,1)} %get-tuple-element.106.one.two), custom_call_target="tpu_custom_call" | custom-call | tf_op jit(solution)/shard_map/shift_rows/pallas_call | solution.py:1189
  171.0 8.7 %bias_strips.1.strips = f32[12,896,128]{2,1,0:T(8,128)} custom-call(f32[384]{0:T(512)} %slice_convert_fusion.2.table, s32[384,128]{1,0:T(8,128)} %constant.159.clone.buckets), custom_call_target="tpu_custom_call" | custom-call | tf_op jit(solution)/shard_map/bias_strips/pallas_call | solution.py:389
  179.6 52.8 %encoder_attend.1 = (bf16[1536,2304]{1,0:T(8,128)(2,1)}, f32[3,16,512]{2,1,0:T(8,128)}, bf16[1536,768]{1,0:T(8,128)(2,1)}, f32[1536,768]{1,0:T(8,128)}) custom-call(s32[1008]{0:T(1024)} %fusion.20.rows_ref, s32[3]{0:T(128)} %lengths.7, bf16[1536,768]{1,0:T(8,128)(2,1)} %x_ref.2, bf16[131584,128]{1,0:T(8,128)(2,1)} %gather_rows.1.gathered, ...), custom_call_target="tpu_custom_call" | custom-call | tf_op jit(solution)/shard_map/encoder_attend/pallas_call | solution.py:467
  232.5 34.1 %encoder_feed.1 = (bf16[1536,3072]{1,0:T(8,128)(2,1)}, f32[1536,768]{1,0:T(8,128)}, bf16[1536,768]{1,0:T(8,128)(2,1)}, bf16[1536,1536]{1,0:T(8,128)(2,1)}) custom-call(s32[1008]{0:T(1024)} %fusion.20.rows_ref, f32[1536,768]{1,0:T(8,128)} %get-tuple-element.113.hidden, bf16[131584,128]{1,0:T(8,128)(2,1)} %gather_rows.1.gathered, f32[8,768]{1,0:T(8,128)} %pad_convert_fusion.gains), custom_call_target="tpu_custom_call" | custom-call | tf_op jit(solution)/shard_map/encoder_feed/pallas_call | solution.py:543
  268.4 7.2 %cross_attend.1 = f32[3,32,1024]{2,1,0:T(8,128)} custom-call(s32[3]{0:T(128)} %lengths.7, s32[3]{0:T(128)} %and_select_fusion.offsets, bf16[3,32,768]{2,1,0:T(8,128)(2,1)} %pad_maximum_fusion.4.queries, bf16[1536,1536]{1,0:T(8,128)(2,1)} %get-tuple-element.114.memory), custom_call_target="tpu_custom_call" | custom-call | tf_op jit(solution)/shard_map/cross_attend/pallas_call | solution.py:957
  277.4 7.2 %shift_rows.5 = (f32[32,1024]{1,0:T(8,128)}, f32[32,1024]{1,0:T(8,128)}) custom-call(f32[32,1024]{1,0:T(8,128)} %get-tuple-element.189.one, f32[32,1024]{1,0:T(8,128)} %get-tuple-element.188.two), custom_call_target="tpu_custom_call" | custom-call | tf_op jit(solution)/shard_map/shift_rows/pallas_call | solution.py:1189
  287.0 13.6 %decoder_feed.1 = (bf16[32,768]{1,0:T(8,128)(2,1)}, bf16[32,768]{1,0:T(8,128)(2,1)}, bf16[32,768]{1,0:T(8,128)(2,1)}, bf16[32,3072]{1,0:T(8,128)(2,1)}, bf16[32,...) custom-call(s32[1008]{0:T(1024)} %fusion.20.rows_ref, ...), custom_call_target="tpu_custom_call" | custom-call | tf_op jit(solution)/shard_map/decoder_feed/pallas_call | solution.py:917
  305.9 12.8 %shift_rows.6 = (f32[32,1024]{1,0:T(8,128)}, f32[32,1024]{1,0:T(8,128)}) custom-call(f32[32,1024]{1,0:T(8,128)} %get-tuple-element.131.one.two, f32[32,1024]{1,0:T(8,128)} %get-tuple-element.131.one.two), custom_call_target="tpu_custom_call" | custom-call | tf_op jit(solution)/shard_map/shift_rows/pallas_call | solution.py:1189
  320.5 17.2 %cross_back.1 = (bf16[1536,1536]{1,0:T(8,128)(2,1)}, f32[3,32,768]{2,1,0:T(8,128)}, f32[1536,768]{1,0:T(8,128)}) custom-call(s32[1008]{0:T(1024)} %fusion.20.rows_ref, s32[3]{0:T(128)} %lengths.7, s32[3]{0:T(128)} %and_select_fusion.offsets, bf16[3,32,768]{2,1,0:T(8,128)(2,1)} %pad_maximum_fusion.4.queries, f32[3,32,1024]{2,1,0:T(8,128)} %pad_maximum_fusion.2.back, ...), custom_call_target="tpu_custom_call" | custom-call | tf_op jit(solution)/shard_map/cross_back/pallas_call | solution.py:1081
  339.4 11.2 %shift_rows.7 = (f32[32,768]{1,0:T(8,128)}, f32[32,768]{1,0:T(8,128)}) custom-call(f32[32,768]{1,0:T(8,128)} %get-tuple-element.192.one, f32[32,768]{1,0:T(8,128)} %get-tuple-element.191.two), custom_call_target="tpu_custom_call" | custom-call | tf_op jit(solution)/shard_map/shift_rows/pallas_call | solution.py:1189
  352.3 9.2 %decoder_self_back.1 = (f32[32,768]{1,0:T(8,128)}, bf16[32,768]{1,0:T(8,128)(2,1)}, bf16[32,768]{1,0:T(8,128)(2,1)}, bf16[32,2304]{1,0:T(8,128)(2,1)}, f32[384,32]{1,0:T(8,128)}, /*index=5*/f32[8,768]{1,0:T(8,128)}) custom-call(s32[1008]{0:T(1024)} %fusion.20.rows_ref, f32[3,32,768]{2,1,0:T(8,128)} %pad_maximum_fusion.3.parts, ...), custom_call_target="tpu_custom_call" | custom-call | tf_op jit(solution)/shard_map/decoder_self_back/pallas_call | solution.py:917
  366.9 40.6 %feed_back.1 = (bf16[1536,3072]{1,0:T(8,128)(2,1)}, bf16[1536,3072]{1,0:T(8,128)(2,1)}, bf16[1536,768]{1,0:T(8,128)(2,1)}, bf16[1536,768]{1,0:T(8,128)(2,1)}, f3...) custom-call(s32[1008]{0:T(1024)} %fusion.20.rows_ref, ...), custom_call_target="tpu_custom_call" | custom-call | tf_op jit(solution)/shard_map/feed_back/pallas_call | solution.py:632
  407.5 2.2 all-gather.7.cloned.1.call-done.middle
  409.8 13.2 %up_weight.1.into = bf16[50688,128]{1,0:T(8,128)(2,1)} custom-call(bf16[1536,768]{1,0:T(8,128)(2,1)} %get-tuple-element.151.left, bf16[1536,3072]{1,0:T(8,128)(2,1)} %get-tuple-element.155.right), custom_call_target="tpu_custom_call" | custom-call | tf_op jit(solution)/shard_map/up_weight/pallas_call | solution.py:1222
  423.0 11.6 %down_weight.1.refs_5_ = bf16[50688,128]{1,0:T(8,128)(2,1)} custom-call(bf16[1536,3072]{1,0:T(8,128)(2,1)} %get-tuple-element.149.left, bf16[1536,768]{1,0:T(8,128)(2,1)} %get-tuple-element.150.right, bf16[50688,128]{1,0:T(8,128)(2,1)} %up_weight.1.into), custom_call_target="tpu_custom_call", output_to_operand_aliasing={{}: (2, {})} | custom-call | tf_op jit(solution)/shard_map/down_weight/pallas_call | solution.py:1240
  434.6 9.6 %square_weight.2.refs_0_ = bf16[50688,128]{1,0:T(8,128)(2,1)} custom-call(bf16[1536,768]{1,0:T(8,128)(2,1)} %get-tuple-element.97.refs_0_, bf16[1536,1536]{1,0:T(8,128)(2,1)} %get-tuple-element.146.refs_1_.refs_2_, bf16[1536,1536]{1,0:T(8,128)(2,1)} %get-tuple-element.146.refs_1_.refs_2_, ...), custom_call_target="tpu_custom_call", output_to_operand_aliasing={{}: (5, {})} | custom-call | tf_op jit(solution)/shard_map/square_weight/pallas_call | solution.py:1289
  444.3 86.8 %attend_back.1 = (bf16[1536,768]{1,0:T(8,128)(2,1)}, bf16[1536,768]{1,0:T(8,128)(2,1)}, bf16[1536,768]{1,0:T(8,128)(2,1)}, f32[12,896,128]{2,1,0:T(8,128)}, bf16[1584,128]{1,0:T(8,128)(2,1)}) custom-call(s32[3]{0:T(128)} %lengths.7, bf16[1536,2304]{1,0:T(8,128)(2,1)} %get-tuple-element.120.q_ref.k_ref.v_ref, ...), custom_call_target="tpu_custom_call" | custom-call | tf_op jit(solution)/shard_map/attend_back/pallas_call | solution.py:768
  536.5 16.1 %input_back.1 = (f32[1536,768]{1,0:T(8,128)}, bf16[1536,768]{1,0:T(8,128)(2,1)}, f32[8,768]{1,0:T(8,128)}) custom-call(s32[1008]{0:T(1024)} %fusion.20.rows_ref, bf16[1536,768]{1,0:T(8,128)(2,1)} %x_ref.2, bf16[1536,768]{1,0:T(8,128)(2,1)} %get-tuple-element.156.gq.refs_1_, bf16[1536,768]{1,0:T(8,128)(2,1)} %get-tuple-element.157.gk.refs_2_, ...), custom_call_target="tpu_custom_call" | custom-call | tf_op jit(solution)/shard_map/input_back/pallas_call | solution.py:817
  552.6 9.9 %square_weight.3 = bf16[14336,128]{1,0:T(8,128)(2,1)} custom-call(bf16[1536,768]{1,0:T(8,128)(2,1)} %get-tuple-element.168.refs_0_, bf16[1536,768]{1,0:T(8,128)(2,1)} %get-tuple-element.156.gq.refs_1_, bf16[1536,768]{1,0:T(8,128)(2,1)} %get-tuple-element.157.gk.refs_2_, bf16[1536,768]{1,0:T(8,128)(2,1)} %get-tuple-element.158.gv.refs_3_), custom_call_target="tpu_custom_call" | custom-call | tf_op jit(solution)/shard_map/square_weight/pallas_call | solution.py:1289
  566.5 2.9 fusion.33
  574.0 77.1 %total_rows.1.two = bf16[14336,128]{1,0:T(8,128)(2,1)} custom-call(bf16[14336,128]{1,0:T(8,128)(2,1)} %pad_dynamic-update-slice_fusion.terms), custom_call_target="tpu_custom_call" | custom-call | tf_op jit(solution)/shard_map/total_rows/pallas_call | solution.py:366
  652.7 18.8 %update_blocks.1 = (f32[32,128,128]{2,1,0:T(8,128)}, f32[32,2,128,128]{3,2,1,0:T(8,128)}, f32[32,128,128]{2,1,0:T(8,128)}) custom-call(s32[256]{0:T(256)} %reshape.165.info, bf16[512,3072]{1,0:T(8,128)(2,1)} %all-gather.5.cloned.1.call-done.early, bf16[512,13056]{1,0:T(8,128)(2,1)} %all-gather.7.cloned.1.call-done.middle, ...), custom_call_target="tpu_custom_call" | custom-call | tf_op jit(solution)/shard_map/update_blocks/pallas_call | solution.py:1424
  (152 shorter events, 50.8 us)
Async XLA Ops:
  7.2 298.7 %all-gather.5.cloned.1.call-start = ((), (), s32[]{:S(2)}) async-start(), calls=%async_computation | async-start | bytes 3244032 | tf_op jit(solution)/shard_map/all_gather | solution.py:1461
  10.7 133.7 %copy-start.13 = (s32[1008]{0:T(1024)S(1)}, s32[1008]{0:T(1024)}, u32[]{:S(2)}) copy-start(s32[1008]{0:T(1024)} %param.28) | copy-start | bytes 12100
  10.7 134.9 %copy-start = (f32[1024,32]{1,0:T(8,128)S(1)}, f32[1024,32]{1,0:T(8,128)}, u32[]{:S(2)}) copy-start(f32[1024,32]{1,0:T(8,128)} %constant.160.clone) | copy-start | bytes 393220
  10.7 136.1 %copy-start.8 = (bf16[20,768]{1,0:T(8,128)(2,1)S(1)}, bf16[20,768]{1,0:T(8,128)(2,1)}, u32[]{:S(2)}) copy-start(bf16[20,768]{1,0:T(8,128)(2,1)} %param.23) | copy-start | bytes 92164
  160.3 249.4 %all-gather.7.cloned.1.call-start = ((), (), s32[]{:S(2)}) async-start(), calls=%async_computation.1 | async-start | bytes 13787136 | tf_op jit(solution)/shard_map/all_gather | solution.py:1461
  232.5 34.1 %copy-start.9 = (bf16[20,768]{1,0:T(8,128)(2,1)S(1)}, bf16[20,768]{1,0:T(8,128)(2,1)}, u32[]{:S(2)}) copy-start(bf16[20,768]{1,0:T(8,128)(2,1)} %param.24) | copy-start | bytes 92164
  232.5 34.8 %copy-start.3 = (bf16[32,768]{1,0:T(8,128)(2,1)S(1)}, bf16[32,768]{1,0:T(8,128)(2,1)}, u32[]{:S(2)}) copy-start(bf16[32,768]{1,0:T(8,128)(2,1)} %get-tuple-element.106.one.two) | copy-start | bytes 147460
  232.5 34.7 %copy-start.6 = (bf16[32,768]{1,0:T(8,128)(2,1)S(1)}, bf16[32,768]{1,0:T(8,128)(2,1)}, u32[]{:S(2)}) copy-start(bf16[32,768]{1,0:T(8,128)(2,1)} %get-tuple-element.107) | copy-start | bytes 147460
  232.5 34.7 %copy-start.7 = (bf16[32,768]{1,0:T(8,128)(2,1)S(1)}, bf16[32,768]{1,0:T(8,128)(2,1)}, u32[]{:S(2)}) copy-start(bf16[32,768]{1,0:T(8,128)(2,1)} %get-tuple-element.108) | copy-start | bytes 147460
  232.5 35.4 %copy-start.16 = (s32[3]{0:T(128)S(1)}, s32[3]{0:T(128)}, u32[]{:S(2)}) copy-start(s32[3]{0:T(128)} %param.26) | copy-start | bytes 40
  268.4 16.1 %copy-start.17 = (s32[1,20]{1,0:T(1,128)S(1)}, s32[1,20]{1,0:T(1,128)}, u32[]{:S(2)}) copy-start(s32[1,20]{1,0:T(1,128)} %param.27) | copy-start | bytes 244
  300.6 18.1 %copy-start.2 = (f32[32,1024]{1,0:T(8,128)S(1)}, f32[32,1024]{1,0:T(8,128)}, u32[]{:S(2)}) copy-start(f32[32,1024]{1,0:T(8,128)} %get-tuple-element.131.one.two) | copy-start | bytes 393220
  305.9 225.3 %all-gather.9.cloned.1.call-start = ((), (), s32[]{:S(2)}) async-start(), calls=%async_computation.2 | async-start | bytes 6488064 | tf_op jit(solution)/shard_map/all_gather | solution.py:1461
  409.7 243.0 %all-gather.11.cloned.1.call-start = ((), (), s32[]{:S(2)}) async-start(), calls=%async_computation.3 | async-start | bytes 13381632 | tf_op jit(solution)/shard_map/all_gather | solution.py:1461
  444.2 87.0 %copy-start.10 = (bf16[32,768]{1,0:T(8,128)(2,1)S(1)}, bf16[32,768]{1,0:T(8,128)(2,1)}, u32[]{:S(2)}) copy-start(bf16[32,768]{1,0:T(8,128)(2,1)} %get-tuple-element.118) | copy-start | bytes 147460
  444.2 90.8 %copy-start.5 = (f32[32,768]{1,0:T(8,128)S(1)}, f32[32,768]{1,0:T(8,128)}, u32[]{:S(2)}) copy-start(f32[32,768]{1,0:T(8,128)} %get-tuple-element.161) | copy-start | bytes 294916
  444.3 91.5 %copy-start.12 = (f32[8,768]{1,0:T(8,128)S(1)}, f32[8,768]{1,0:T(8,128)}, u32[]{:S(2)}) copy-start(f32[8,768]{1,0:T(8,128)} %get-tuple-element.170) | copy-start | bytes 73732
  444.3 91.5 %copy-start.11 = (f32[8,768]{1,0:T(8,128)S(1)}, f32[8,768]{1,0:T(8,128)}, u32[]{:S(2)}) copy-start(f32[8,768]{1,0:T(8,128)} %get-tuple-element.171) | copy-start | bytes 73732
  444.3 91.5 %copy-start.4 = (f32[384,32]{1,0:T(8,128)S(1)}, f32[384,32]{1,0:T(8,128)}, u32[]{:S(2)}) copy-start(f32[384,32]{1,0:T(8,128)} %get-tuple-element.174) | copy-start | bytes 147460
  564.3 5.3 slice-start
  564.6 1.9 copy-start.1
  564.6 5.0 slice-start.1
  574.0 78.1 %copy-start.14 = (f32[168]{0:T(256)S(1)}, f32[168]{0:T(256)}, u32[]{:S(2)}) copy-start(f32[168]{0:T(256)} %param.32) | copy-start | bytes 2020
  574.0 78.1 %copy-start.15 = (f32[168]{0:T(256)S(1)}, f32[168]{0:T(256)}, u32[]{:S(2)}) copy-start(f32[168]{0:T(256)} %param.33) | copy-start | bytes 2020
Sparse Core Ops, SparseCore 0:
  160.4 58.1 all-gather.4
  306.0 103.6 all-gather.6
  413.1 88.4 all-gather.8
  531.3 117.5 all-gather.10

commit v3 on v2

--- a/solution.py
+++ b/solution.py
@@ -24,6 +24,7 @@
 STRIP = 7 * BLK
 EXTRA = 16
 SURE = 248
+EARLY_SLOTS = 22
 
 exact_prec = lax.Precision.HIGHEST
 neg_fill = -1000000000.0
@@ -118,12 +119,17 @@
     def body(b, carry):
         i = b // across
         j = b - i * across
-        source = pl.multiple_of(rows_ref[first + b], 16)
-        pltpu.make_async_copy(
-            gathered.at[pl.ds(source, BLK)],
-            dest.at[pl.ds(pl.multiple_of(i * BLK, BLK), BLK), pl.ds(pl.multiple_of(j * BLK, BLK), BLK)],
-            sem,
-        ).start()
+        row = rows_ref[first + b]
+        place = dest.at[pl.ds(pl.multiple_of(i * BLK, BLK), BLK), pl.ds(pl.multiple_of(j * BLK, BLK), BLK)]
+
+        @pl.when(row >= 0)
+        def _():
+            pltpu.make_async_copy(gathered[0].at[pl.ds(pl.multiple_of(row, 16), BLK)], place, sem).start()
+
+        @pl.when(row < 0)
+        def _():
+            pltpu.make_async_copy(gathered[1].at[pl.ds(pl.multiple_of(-1 - row, 16), BLK)], place, sem).start()
+
         return carry
 
     lax.fori_loop(0, rows // BLK * across, body, 0)
@@ -319,6 +325,12 @@
     return [pltpu.VMEM((count, rows, BLK), bf16) for count in (many, many, many - 1)]
 
 
+def together(steps, more):
+    placed = [(k / len(steps), 0, k, step) for k, step in enumerate(steps)]
+    placed += [(k / len(more), 1, k, step) for k, step in enumerate(more)]
+    return [step for _, _, _, step in sorted(placed, key=lambda entry: entry[:3])]
+
+
 def gather_kernel(plan, nbits, rows, shard, out_ref, *sems):
     enter_tree(nbits)
     steps, end = spread_steps(plan, nbits, rows, lambda c: shard.at[pl.ds(plan[c][0], plan[c][1])], out_ref, sems)
@@ -327,15 +339,15 @@
     end()
 
 
-def gather_rows(shard, dp_count, cid):
-    rows = shard.shape[0]
+def gather_rows(shard, rows, dp_count, cid):
     nbits = dp_count.bit_length() - 1
     plan = chunk_plan(rows, nbits, "ABABABCD", (1,) * 8)
+    any_space = pl.BlockSpec(memory_space=pl.ANY)
     return pl.pallas_call(
         functools.partial(gather_kernel, plan, nbits, rows),
         out_shape=jax.ShapeDtypeStruct((dp_count * 2 * rows, BLK), shard.dtype),
-        in_specs=[pl.BlockSpec(memory_space=pl.ANY)],
-        out_specs=pl.BlockSpec(memory_space=pl.ANY),
+        in_specs=[any_space],
+        out_specs=any_space,
         scratch_shapes=tree_sems(plan, nbits),
         compiler_params=pltpu.CompilerParams(collective_id=cid, has_side_effects=True),
         name="gather_rows",
@@ -403,21 +415,23 @@
     rows = keys.shape[0]
     scores = dot_nt(keys, queries)
     bias = jnp.concatenate(
-        [strip[(3 - n) * BLK : (3 - n) * BLK + rows, :] for n in (offset, offset + 1)], axis=1
+        [strip[(3 - n) * BLK : (3 - n) * BLK + rows, :] for n in range(offset, offset + queries.shape[0] // BLK)], axis=1
     )
     key_at = lax.broadcasted_iota(jnp.int32, scores.shape, 0)
     scores = scores + bias
     return jnp.concatenate([scores[:SURE], jnp.where(key_at[SURE:] < length, scores[SURE:], neg_fill)], axis=0)
 
 
-def attend_kernel(rows_ref, lengths, x_ref, gathered, gains, strips, qkv, lse, mixed, hidden, wqkv, wout, sems):
+def attend_kernel(
+    rows_ref, lengths, x_ref, near, far, gains, strips, qkv, lse, mixed, hidden, whole, wqkv, sems, out_sem
+):
     step = pl.program_id(0)
+    keep = pltpu.make_async_copy(wqkv, whole, out_sem.at[0])
 
     @pl.when(step == 0)
     def _():
-        for m in range(3):
-            start_blocks(rows_ref, gathered, ENC_QKV + 36 * m, D, D, wqkv.at[m], sems.at[m])
-        start_blocks(rows_ref, gathered, ENC_OUT, D, D, wout, sems.at[3])
+        for m in range(4):
+            start_blocks(rows_ref, (near, far), 36 * m, D, D, wqkv.at[m], sems.at[m])
 
     values = x_ref[...].astype(f32)
     normed = to_low(rms_scale(values, gains[0:1, :]))
@@ -428,6 +442,12 @@
             wait_whole(wqkv.at[m], sems.at[m])
 
         qkv[:, m * D : (m + 1) * D] = to_low(dot(normed, wqkv[m]))
+
+    @pl.when(step == 0)
+    def _():
+        wait_whole(wqkv.at[3], sems.at[3])
+        keep.start()
+
     length = lengths[step]
 
     def one_pair(pair, carry):
@@ -435,35 +455,29 @@
         queries = qkv[:, pl.ds(at, BLK)]
         keys = qkv[:, pl.ds(pl.multiple_of(at + D, BLK), BLK)]
         turned = qkv[:, pl.ds(pl.multiple_of(at + 2 * D, BLK), BLK)].T
-        for n in range(2):
-            part = queries[n * 256 : (n + 1) * 256]
-            outs = []
-            for head in range(2):
-                only = jnp.where(head_lanes(256, head), part, jnp.zeros_like(part))
-                scores = masked_scores(keys, only, strips.at[2 * pair + head], 2 * n, length)
-                peak = jnp.max(scores, axis=0, keepdims=True)
-                expos = jnp.exp(scores - peak)
-                total = jnp.sum(expos, axis=0, keepdims=True)
-                lse[0, pl.ds(2 * pair + head, 1), n * 256 : (n + 1) * 256] = peak + jnp.log(total)
-                outs.append(dot(turned, to_low(expos)) * (1.0 / total))
-            lane = lax.broadcasted_iota(jnp.int32, (BLK, 256), 0)
-            both = jnp.where(lane < HD, outs[0], outs[1])
-            mixed[n * 256 : (n + 1) * 256, pl.ds(at, BLK)] = to_low(both.T)
+        outs = []
+        for head in range(2):
+            only = jnp.where(head_lanes(PASS_SLOT, head), queries, jnp.zeros_like(queries))
+            scores = masked_scores(keys, only, strips.at[2 * pair + head], 0, length)
+            peak = jnp.max(scores, axis=0, keepdims=True)
+            expos = jnp.exp(scores - peak)
+            total = jnp.sum(expos, axis=0, keepdims=True)
+            lse[0, pl.ds(2 * pair + head, 1), :] = peak + jnp.log(total)
+            outs.append(dot(turned, to_low(expos)) * (1.0 / total))
+        lane = lax.broadcasted_iota(jnp.int32, (BLK, PASS_SLOT), 0)
+        mixed[:, pl.ds(at, BLK)] = to_low(jnp.where(lane < HD, outs[0], outs[1]).T)
         return carry
 
     lax.fori_loop(0, PAIRS, one_pair, 0)
-
-    @pl.when(step == 0)
-    def _():
-        wait_whole(wout, sems.at[3])
-
-    hidden[...] = x_ref[...].astype(f32) + dot(mixed[...], wout[...])
+    hidden[...] = x_ref[...].astype(f32) + dot(mixed[...], wqkv[3])
+    pl.when(step == pl.num_programs(0) - 1)(lambda: keep.wait())
 
 
 def encoder_attend(rows, lengths, enc_in, gathered, gains, strips):
     count = lengths.shape[0]
     total = count * PASS_SLOT
     by_row = lambda p, *_: (p, 0)
+    any_space = pl.BlockSpec(memory_space=pl.ANY)
     return pl.pallas_call(
         attend_kernel,
         grid_spec=pltpu.PrefetchScalarGridSpec(
@@ -471,7 +485,8 @@
             grid=(count,),
             in_specs=[
                 pl.BlockSpec((PASS_SLOT, D), by_row),
-                pl.BlockSpec(memory_space=pl.ANY),
+                any_space,
+                any_space,
                 pl.BlockSpec((8, D), lambda p, *_: (0, 0)),
                 pl.BlockSpec((H, STRIP, BLK), lambda p, *_: (0, 0, 0)),
             ],
@@ -480,11 +495,12 @@
                 pl.BlockSpec((1, 16, PASS_SLOT), lambda p, *_: (p, 0, 0)),
                 pl.BlockSpec((PASS_SLOT, D), by_row),
                 pl.BlockSpec((PASS_SLOT, D), by_row),
+                any_space,
             ],
             scratch_shapes=[
-                pltpu.VMEM((3, D, D), bf16),
-                pltpu.VMEM((D, D), bf16),
+                pltpu.VMEM((4, D, D), bf16),
                 pltpu.SemaphoreType.DMA((4,)),
+                pltpu.SemaphoreType.DMA((1,)),
             ],
         ),
         out_shape=[
@@ -492,54 +508,55 @@
             jax.ShapeDtypeStruct((count, 16, PASS_SLOT), f32),
             jax.ShapeDtypeStruct((total, D), bf16),
             jax.ShapeDtypeStruct((total, D), f32),
+            jax.ShapeDtypeStruct((4, D, D), bf16),
         ],
         compiler_params=pltpu.CompilerParams(vmem_limit_bytes=VMEM_CAP),
         name="encoder_attend",
-    )(rows, lengths, enc_in, gathered, gains, strips)
-
-
-FCHUNK = 1024
-
-
-def feed_kernel(rows_ref, hidden, gathered, gains, inner, output, encoded, cross, wup, wdown, wkv, sems):
+    )(rows, lengths, enc_in, *gathered, gains, strips)
+
+
+FEED_CHUNK = 1536
+FCHUNK = 768
+
+
+def feed_kernel(rows_ref, hidden, near, far, gains, inner, output, encoded, up, down, wup, wdown, sems, out_sems):
     step = pl.program_id(0)
+    keeps = [pltpu.make_async_copy(wup, up, out_sems.at[0]), pltpu.make_async_copy(wdown, down, out_sems.at[1])]
 
     @pl.when(step == 0)
     def _():
-        start_blocks(rows_ref, gathered, ENC_UP, D, FF, wup, sems.at[0])
-        start_blocks(rows_ref, gathered, ENC_DOWN, FF, D, wdown, sems.at[1])
-        for m in range(2):
-            start_blocks(rows_ref, gathered, CROSS_KV + 36 * m, D, D, wkv.at[m], sems.at[2 + m])
+        start_blocks(rows_ref, (near, far), ENC_UP, D, FF, wup, sems.at[0])
+        start_blocks(rows_ref, (near, far), ENC_DOWN, FF, D, wdown, sems.at[1])
 
     normed = to_low(rms_scale(hidden[...], gains[1:2, :]))
+    total = hidden[...]
 
     @pl.when(step == 0)
     def _():
         wait_whole(wup, sems.at[0])
         wait_whole(wdown, sems.at[1])
-
-    total = hidden[...]
-    for c in range(FF // FCHUNK):
-        cols = slice(c * FCHUNK, (c + 1) * FCHUNK)
+        for keep in keeps:
+            keep.start()
+
+    for c in range(FF // FEED_CHUNK):
+        cols = slice(c * FEED_CHUNK, (c + 1) * FEED_CHUNK)
         act = dot(normed, wup[:, cols])
         inner[:, cols] = to_low(act)
         total = total + dot(to_low(gate(act)), wdown[cols, :])
     output[...] = total
-    low = to_low(rms_scale(total, gains[2:3, :]))
-    encoded[...] = low
-    for m in range(2):
-
-        @pl.when(step == 0)
-        def _(m=m):
-            wait_whole(wkv.at[m], sems.at[2 + m])
-
-        cross[:, m * D : (m + 1) * D] = to_low(dot(low, wkv[m]))
+    encoded[...] = to_low(rms_scale(total, gains[2:3, :]))
+
+    @pl.when(step == pl.num_programs(0) - 1)
+    def _():
+        for keep in keeps:
+            keep.wait()
 
 
 def encoder_feed(rows, hidden, gathered, gains):
     total = hidden.shape[0]
     tile = 512
     by_row = lambda p, *_: (p, 0)
+    any_space = pl.BlockSpec(memory_space=pl.ANY)
     return pl.pallas_call(
         feed_kernel,
         grid_spec=pltpu.PrefetchScalarGridSpec(
@@ -547,35 +564,38 @@
             grid=(total // tile,),
             in_specs=[
                 pl.BlockSpec((tile, D), by_row),
-                pl.BlockSpec(memory_space=pl.ANY),
+                any_space,
+                any_space,
                 pl.BlockSpec((8, D), lambda p, *_: (0, 0)),
             ],
             out_specs=[
                 pl.BlockSpec((tile, FF), by_row),
                 pl.BlockSpec((tile, D), by_row),
                 pl.BlockSpec((tile, D), by_row),
-                pl.BlockSpec((tile, 2 * D), by_row),
+                any_space,
+                any_space,
             ],
             scratch_shapes=[
                 pltpu.VMEM((D, FF), bf16),
                 pltpu.VMEM((FF, D), bf16),
-                pltpu.VMEM((2, D, D), bf16),
-                pltpu.SemaphoreType.DMA((4,)),
+                pltpu.SemaphoreType.DMA((2,)),
+                pltpu.SemaphoreType.DMA((2,)),
             ],
         ),
         out_shape=[
             jax.ShapeDtypeStruct((total, FF), bf16),
             jax.ShapeDtypeStruct((total, D), f32),
             jax.ShapeDtypeStruct((total, D), bf16),
-            jax.ShapeDtypeStruct((total, 2 * D), bf16),
+            jax.ShapeDtypeStruct((D, FF), bf16),
+            jax.ShapeDtypeStruct((FF, D), bf16),
         ],
         compiler_params=pltpu.CompilerParams(vmem_limit_bytes=VMEM_CAP),
         name="encoder_feed",
-    )(rows, hidden, gathered, gains)
+    )(rows, hidden, *gathered, gains)
 
 
 def feed_back_kernel(
-    rows_ref, output, hidden, inner, upstream, gathered, gains,
+    output, hidden, inner, upstream, down, up, out, gains,
     act_low, inner_grad, branch, normed, hidden_grad, attn_grad, mixed_grad, gain_sums,
     wup, wdown, wout, sems,
 ):
@@ -583,9 +603,9 @@
 
     @pl.when(step == 0)
     def _():
-        start_blocks(rows_ref, gathered, ENC_DOWN, FF, D, wdown, sems.at[0])
-        start_blocks(rows_ref, gathered, ENC_UP, D, FF, wup, sems.at[1])
-        start_blocks(rows_ref, gathered, ENC_OUT, D, D, wout, sems.at[2])
+        pltpu.make_async_copy(down, wdown, sems.at[0]).start()
+        pltpu.make_async_copy(up, wup, sems.at[1]).start()
+        pltpu.make_async_copy(out.at[3], wout, sems.at[2]).start()
         gain_sums[...] = jnp.zeros_like(gain_sums)
 
     output_grad, final_gain = norm_back(output[...], gains[2:3, :], upstream[...])
@@ -622,7 +642,7 @@
     gain_sums[1:2, :] += final_gain
 
 
-def feed_back(rows, output, hidden, inner, upstream, gathered, gains):
+def feed_back(output, hidden, inner, upstream, down, up, out, gains):
     total = hidden.shape[0]
     tile = 256
     by_row = lambda p, *_: (p, 0)
@@ -632,9 +652,9 @@
     return pl.pallas_call(
         feed_back_kernel,
         grid_spec=pltpu.PrefetchScalarGridSpec(
-            num_scalar_prefetch=1,
+            num_scalar_prefetch=0,
             grid=(total // tile,),
-            in_specs=[row, row, wide, row, pl.BlockSpec(memory_space=pl.ANY), pl.BlockSpec((8, D), fixed)],
+            in_specs=[row, row, wide, row, *[pl.BlockSpec(memory_space=pl.ANY)] * 3, pl.BlockSpec((8, D), fixed)],
             out_specs=[wide, wide, row, row, row, row, row, pl.BlockSpec((8, D), fixed)],
             scratch_shapes=[
                 pltpu.VMEM((D, FF), bf16),
@@ -655,16 +675,16 @@
         ],
         compiler_params=pltpu.CompilerParams(vmem_limit_bytes=VMEM_CAP),
         name="feed_back",
-    )(rows, output, hidden, inner, upstream, gathered, gains)
+    )(output, hidden, inner, upstream, down, up, out, gains)
 
 
 def attend_back_kernel(
-    plan, nbits, rows, lengths, q_ref, k_ref, v_ref, go_ref, lse, strips, *refs
+    plan, shard_plan, nbits, rows, lengths, q_ref, k_ref, v_ref, go_ref, lse, strips, buckets, *refs
 ):
     if plan is None:
-        gq_ref, gk_ref, gv_ref, bias_sums = refs
+        gq_ref, gk_ref, gv_ref, table, bias_sums = refs
     else:
-        terms, gq_ref, gk_ref, gv_ref, bias_sums, reduced, own, sib, land, *sems = refs
+        terms, shard, gq_ref, gk_ref, gv_ref, table, reduced, spread, bias_sums, own, sib, land, *sems = refs
     pair = pl.program_id(0)
     step = pl.program_id(1)
     at = pair * pl.num_programs(1) + step
@@ -675,15 +695,20 @@
         def put(where, total):
             reduced[where, :] = to_low(total)
 
-        begin, steps, end = sum_steps(plan, nbits, rows, terms, put, own, sib, land, sems)
+        begin, steps, end = sum_steps(plan, nbits, rows, terms, put, own, sib, land, sems[:5])
+        more, more_end = spread_steps(
+            shard_plan, nbits, shard.shape[0], lambda c: shard.at[pl.ds(shard_plan[c][0], shard_plan[c][1])], spread, sems[5:]
+        )
+        steps = together(steps, more)
 
         @pl.when(at == 0)
         def _():
             enter_tree(nbits)
             begin()
 
+        cuts = [round(len(steps) * (k / (total_steps - 1)) ** 0.8) for k in range(total_steps)]
         for k in range(1, total_steps):
-            some = steps[len(steps) * (k - 1) // (total_steps - 1) : len(steps) * k // (total_steps - 1)]
+            some = steps[cuts[k - 1] : cuts[k]]
 
             @pl.when(at == k)
             def _(some=some):
@@ -705,37 +730,51 @@
     ]
     key_grad = jnp.zeros((PASS_SLOT, BLK), f32)
     value_grad = jnp.zeros((PASS_SLOT, BLK), f32)
-    for n in range(2):
-        span = slice(n * 256, (n + 1) * 256)
-        query_grad = jnp.zeros((BLK, 256), f32)
-        for head in range(2):
-            mask = head_lanes(256, head)
-            queries = jnp.where(mask, q_ref[span, :], jnp.zeros((256, BLK), bf16))
-            grads = jnp.where(mask, go_ref[span, :], jnp.zeros((256, BLK), bf16))
-            scores = masked_scores(keys, queries, strips.at[head], 2 * n, length)
-            probs = jnp.exp(scores - lse[0, pl.ds(2 * pair + head, 1), span])
-            prob_grad = dot_nt(values, grads)
-            inner = jnp.sum(probs * prob_grad, axis=0, keepdims=True)
-            score_grad = to_low(probs * (prob_grad - inner))
-            wide = score_grad.astype(f32)
-            for m in range(2):
-                first = (3 - 2 * n - m) * BLK
-                bias_sums[head, first : first + PASS_SLOT, :] += wide[:, m * BLK : (m + 1) * BLK]
-            value_grad = value_grad + dot(to_low(probs), grads)
-            key_grad = key_grad + dot(score_grad, queries)
-            query_grad = query_grad + dot(halves[head], score_grad)
-        gq_ref[span, :] = to_low(query_grad.T)
+    query_grad = jnp.zeros((BLK, PASS_SLOT), f32)
+    for head in range(2):
+        mask = head_lanes(PASS_SLOT, head)
+        queries = jnp.where(mask, q_ref[...], jnp.zeros((PASS_SLOT, BLK), bf16))
+        grads = jnp.where(mask, go_ref[...], jnp.zeros((PASS_SLOT, BLK), bf16))
+        scores = masked_scores(keys, queries, strips.at[head], 0, length)
+        probs = jnp.exp(scores - lse[0, pl.ds(2 * pair + head, 1), :])
+        prob_grad = dot_nt(values, grads)
+        inner = jnp.sum(probs * prob_grad, axis=0, keepdims=True)
+        score_grad = to_low(probs * (prob_grad - inner))
+        wide = score_grad.astype(f32)
+        for m in range(PASS_SLOT // BLK):
+            first = (3 - m) * BLK
+            bias_sums[head, first : first + PASS_SLOT, :] += wide[:, m * BLK : (m + 1) * BLK]
+        value_grad = value_grad + dot(to_low(probs), grads)
+        key_grad = key_grad + dot(score_grad, queries)
+        query_grad = query_grad + dot(halves[head], score_grad)
+    gq_ref[...] = to_low(query_grad.T)
     gk_ref[...] = to_low(key_grad)
     gv_ref[...] = to_low(value_grad)
+
+    @pl.when(step == pl.num_programs(1) - 1)
+    def _():
+        which = buckets[...]
+        lane = lax.broadcasted_iota(jnp.int32, (1, BLK), 1)
+        for head in range(2):
+            near = bias_sums[head, 2 * BLK : 5 * BLK, :]
+            sums = jnp.zeros((1, BLK), f32)
+            for b in range(NB):
+                part = jnp.sum(jnp.where(which == b, near, 0.0), axis=0, keepdims=True)
+                if b % (NB // 2) == NB // 2 - 1:
+                    ends = slice(0, 2 * BLK) if b < NB // 2 else slice(5 * BLK, STRIP)
+                    part = part + jnp.sum(bias_sums[head, ends, :], axis=0, keepdims=True)
+                sums = jnp.where(lane == b, jnp.sum(part, axis=1, keepdims=True), sums)
+            table[0, head : head + 1, :] = sums
 
     if plan is not None:
 
         @pl.when(at == total_steps - 1)
         def _():
             end()
-
-
-def attend_back(lengths, qkv, mixed_grad, lse, strips, terms, dp_count, cid):
+            more_end()
+
+
+def attend_back(lengths, qkv, mixed_grad, lse, strips, terms, shard, dp_count, cid):
     count = lengths.shape[0]
     total = count * PASS_SLOT
     block = (PASS_SLOT, BLK)
@@ -748,25 +787,31 @@
         place,
         pl.BlockSpec((1, 16, PASS_SLOT), lambda a, p, *_: (p, 0, 0)),
         strip,
+        pl.BlockSpec((3 * BLK, BLK), lambda *_: (0, 0)),
     ]
-    out_specs = [place, place, place, strip]
-    out_shape = [jax.ShapeDtypeStruct((total, D), bf16)] * 3 + [jax.ShapeDtypeStruct((H, STRIP, BLK), f32)]
-    operands = [qkv, qkv, qkv, mixed_grad, lse, strips]
-    scratch = []
-    plan, nbits, rows = None, 0, 0
+    out_specs = [place, place, place, pl.BlockSpec((1, 8, BLK), lambda a, p, *_: (a, 0, 0))]
+    out_shape = [jax.ShapeDtypeStruct((total, D), bf16)] * 3 + [jax.ShapeDtypeStruct((PAIRS, 8, BLK), f32)]
+    operands = [qkv, qkv, qkv, mixed_grad, lse, strips, jnp.asarray(strip_buckets())]
+    scratch = [pltpu.VMEM((2, STRIP, BLK), f32)]
+    plan, shard_plan, nbits, rows = None, None, 0, 0
     params = dict(vmem_limit_bytes=VMEM_CAP)
     if dp_count == 16:
         rows = terms.shape[0] // (2 * dp_count)
         nbits = dp_count.bit_length() - 1
-        plan = chunk_plan(rows, nbits, "ABCDAB", (3, 3, 2, 2, 3, 3))
-        in_specs.append(pl.BlockSpec(memory_space=pl.ANY))
-        out_specs.append(pl.BlockSpec((rows, BLK), lambda a, p, *_: (0, 0)))
-        out_shape.append(jax.ShapeDtypeStruct((rows, BLK), bf16))
-        operands.append(terms)
-        scratch = sum_scratch(rows, nbits) + tree_sems(plan, nbits)
+        plan = chunk_plan(rows, nbits, "ABCDABAB", (2, 2, 2, 2, 3, 3, 1, 1))
+        shard_plan = chunk_plan(shard.shape[0], nbits, "ABCD", (3, 3, 1, 1))
+        any_space = pl.BlockSpec(memory_space=pl.ANY)
+        in_specs += [any_space, any_space]
+        out_specs += [pl.BlockSpec((rows, BLK), lambda a, p, *_: (0, 0)), any_space]
+        out_shape += [
+            jax.ShapeDtypeStruct((rows, BLK), bf16),
+            jax.ShapeDtypeStruct((2 * dp_count * shard.shape[0], BLK), bf16),
+        ]
+        operands += [terms, shard]
+        scratch = scratch + sum_scratch(rows, nbits) + tree_sems(plan, nbits) + tree_sems(shard_plan, nbits)
         params.update(collective_id=cid, has_side_effects=True)
     results = pl.pallas_call(
-        functools.partial(attend_back_kernel, plan, nbits, rows),
+        functools.partial(attend_back_kernel, plan, shard_plan, nbits, rows),
         grid_spec=pltpu.PrefetchScalarGridSpec(
             num_scalar_prefetch=1,
             grid=(PAIRS, count),
@@ -779,19 +824,23 @@
         name="attend_back",
     )(lengths, *operands)
     if plan is None:
-        return *results, lax.psum_scatter(terms, ("dp", "opt"), scatter_dimension=0, tiled=True)
+        return (
+            *results,
+            lax.psum_scatter(terms, ("dp", "opt"), scatter_dimension=0, tiled=True),
+            lax.all_gather(shard, ("dp", "opt"), axis=0, tiled=True),
+        )
     return results
 
 
 def input_back_kernel(
-    rows_ref, x_ref, gq, gk, gv, hidden_grad, gathered, gains, result, normed, gain_sums, wqkv, sems
+    x_ref, gq, gk, gv, hidden_grad, whole, gains, result, normed, gain_sums, wqkv, sems
 ):
     step = pl.program_id(0)
 
     @pl.when(step == 0)
     def _():
         for m in range(3):
-            start_blocks(rows_ref, gathered, ENC_QKV + 36 * m, D, D, wqkv.at[m], sems.at[m])
+            pltpu.make_async_copy(whole.at[m], wqkv.at[m], sems.at[m]).start()
         gain_sums[...] = jnp.zeros_like(gain_sums)
 
     values = x_ref[...].astype(f32)
@@ -809,7 +858,7 @@
     gain_sums[0:1, :] += first_gain
 
 
-def input_back(rows, enc_in, gq, gk, gv, hidden_grad, gathered, gains):
+def input_back(enc_in, gq, gk, gv, hidden_grad, whole, gains):
     total = enc_in.shape[0]
     tile = 256
     fixed = lambda p, *_: (0, 0)
@@ -817,7 +866,7 @@
     return pl.pallas_call(
         input_back_kernel,
         grid_spec=pltpu.PrefetchScalarGridSpec(
-            num_scalar_prefetch=1,
+            num_scalar_prefetch=0,
             grid=(total // tile,),
             in_specs=[row, row, row, row, row, pl.BlockSpec(memory_space=pl.ANY), pl.BlockSpec((8, D), fixed)],
             out_specs=[row, row, pl.BlockSpec((8, D), fixed)],
@@ -830,11 +879,29 @@
         ],
         compiler_params=pltpu.CompilerParams(vmem_limit_bytes=VMEM_CAP),
         name="input_back",
-    )(rows, enc_in, gq, gk, gv, hidden_grad, gathered, gains)
+    )(enc_in, gq, gk, gv, hidden_grad, whole, gains)
 
 
 HROWS = H * AROWS
 SIDE = D + 2 * BLK
+
+
+HELD = 16
+REST = ALEN - HELD
+
+
+def pack_rows(sides):
+    main = jnp.concatenate([side[:HELD] for side in sides], axis=1)
+    width = max(side.shape[1] for side in sides)
+    rest = jnp.zeros((HELD, width), f32)
+    for k, side in enumerate(sides):
+        rows = side[HELD:ALEN].astype(f32)
+        if side.shape[1] < width:
+            rows = jnp.concatenate([rows, jnp.zeros((REST, width - side.shape[1]), f32)], axis=1)
+        above, below = REST * k, HELD - REST * (k + 1)
+        rows = [jnp.zeros((above, width), f32)] * (above > 0) + [rows] + [jnp.zeros((below, width), f32)] * (below > 0)
+        rest = rest + jnp.concatenate(rows, axis=0)
+    return jnp.concatenate([main, to_low(rest)], axis=1)
 
 
 def spread_heads(rows):
@@ -882,14 +949,13 @@
     return jnp.where(key_at <= row % AROWS, scores, neg_fill)
 
 
-def self_kernel(rows_ref, dec_ref, gathered, gains, bias, qkv, mixed, first, normed, normed_two, cross, wqkv, wout, wcq, sems):
+def self_kernel(rows_ref, dec_ref, near, far, gains, bias, qkv, first, cross, early, wqkv, wout, wcq, sems):
     for m in range(3):
-        start_blocks(rows_ref, gathered, DEC_QKV + 36 * m, D, D, wqkv.at[m], sems.at[m])
-    start_blocks(rows_ref, gathered, DEC_OUT, D, D, wout, sems.at[3])
-    start_blocks(rows_ref, gathered, CROSS_Q, D, D, wcq, sems.at[4])
+        start_blocks(rows_ref, (near, far), DEC_QKV + 36 * m, D, D, wqkv.at[m], sems.at[m])
+    start_blocks(rows_ref, (near, far), DEC_OUT, D, D, wout, sems.at[3])
+    start_blocks(rows_ref, (near, far), CROSS_Q, D, D, wcq, sems.at[4])
     values = dec_ref[...].astype(f32)
-    low = to_low(rms_scale(values, gains[3:4, :]))
-    normed[...] = low
+    low = normed = to_low(rms_scale(values, gains[3:4, :]))
     for m in range(3):
         wait_whole(wqkv.at[m], sems.at[m])
         qkv[:, m * D : (m + 1) * D] = to_low(dot(low, wqkv[m]))
@@ -898,14 +964,13 @@
     expos = jnp.exp(scores - peak)
     probs = to_low(expos / jnp.sum(expos, axis=1, keepdims=True))
     heads = to_low(gather_heads(dot(probs, qkv[:, 2 * D : 3 * D])))
-    mixed[...] = heads
     wait_whole(wout, sems.at[3])
     after = values + dot(heads, wout[...])
     first[...] = after
     low = to_low(rms_scale(after, gains[4:5, :]))
-    normed_two[...] = low
     wait_whole(wcq, sems.at[4])
     cross[...] = to_low(dot(low, wcq[...]))
+    early[...] = pack_rows((normed, heads, low))
 
 
 def whole_spec(shape):
@@ -913,7 +978,7 @@
 
 
 def decoder_call(body, name, rows, ins, outs, scratch):
-    specs = [pl.BlockSpec(memory_space=pl.ANY) if x.shape[0] > 65536 else whole_spec(x.shape) for x in ins]
+    specs = [pl.BlockSpec(memory_space=pl.ANY) if x.shape[0] > 8192 else whole_spec(x.shape) for x in ins]
     return pl.pallas_call(
         body,
         grid_spec=pltpu.PrefetchScalarGridSpec(
@@ -933,10 +998,44 @@
     low, full = ((AROWS, D), bf16), ((AROWS, D), f32)
     square = pltpu.VMEM((D, D), bf16)
     return decoder_call(
-        self_kernel, "decoder_self", rows, (dec_rows, gathered, gains, bias),
-        [((AROWS, 3 * D), bf16), low, full, low, low, low],
+        self_kernel, "decoder_self", rows, (dec_rows, *gathered, gains, bias),
+        [((AROWS, 3 * D), bf16), full, low, ((HELD, 4 * D), bf16)],
         [pltpu.VMEM((3, D, D), bf16), square, square, pltpu.SemaphoreType.DMA((5,))],
     )
+
+
+def memory_kernel(rows_ref, encoded, near, far, memory, wkv, sems):
+    step = pl.program_id(0)
+
+    @pl.when(step == 0)
+    def _():
+        for m in range(2):
+            start_blocks(rows_ref, (near, far), CROSS_KV + 36 * m, D, D, wkv.at[m], sems.at[m])
+
+    for m in range(2):
+
+        @pl.when(step == 0)
+        def _(m=m):
+            wait_whole(wkv.at[m], sems.at[m])
+
+        memory[:, m * D : (m + 1) * D] = to_low(dot(encoded[...], wkv[m]))
+
+
+def cross_memory(rows, encoded, gathered):
+    total = encoded.shape[0]
+    return pl.pallas_call(
+        memory_kernel,
+        grid_spec=pltpu.PrefetchScalarGridSpec(
+            num_scalar_prefetch=1,
+            grid=(total // PASS_SLOT,),
+            in_specs=[pl.BlockSpec((PASS_SLOT, D), lambda p, *_: (p, 0)), *[pl.BlockSpec(memory_space=pl.ANY)] * 2],
+            out_specs=pl.BlockSpec((PASS_SLOT, 2 * D), lambda p, *_: (p, 0)),
+            scratch_shapes=[pltpu.VMEM((2, D, D), bf16), pltpu.SemaphoreType.DMA((2,))],
+        ),
+        out_shape=jax.ShapeDtypeStruct((total, 2 * D), bf16),
+        compiler_params=pltpu.CompilerParams(vmem_limit_bytes=VMEM_CAP),
+        name="cross_memory",
+    )(rows, encoded, *gathered)
 
 
 def cross_kernel(lengths, offsets, queries, memory, result):
@@ -972,13 +1071,12 @@
 
 
 def feed_decoder_kernel(
-    rows_ref, parts, first, dec_cot, valid, gathered, gains,
-    result, mixed, normed, act_low, inner_grad, branch, cross_grad, back, second_grad, gain_sums,
-    wout, wup, wdown, sems,
+    rows_ref, parts, first, dec_cot, valid, early, near, far, gains,
+    result, middle, back, second_grad, gain_sums, wout, wup, wdown, sems,
 ):
-    start_blocks(rows_ref, gathered, CROSS_OUT, D, D, wout, sems.at[0])
-    start_blocks(rows_ref, gathered, DEC_UP, D, FF, wup, sems.at[1])
-    start_blocks(rows_ref, gathered, DEC_DOWN, FF, D, wdown, sems.at[2])
+    start_blocks(rows_ref, (near, far), CROSS_OUT, D, D, wout, sems.at[0])
+    start_blocks(rows_ref, (near, far), DEC_UP, D, FF, wup, sems.at[1])
+    start_blocks(rows_ref, (near, far), DEC_DOWN, FF, D, wdown, sems.at[2])
     peaks = [parts[k, :, D : D + BLK] for k in range(PASS_EX)]
     peak = functools.reduce(jnp.maximum, peaks)
     scales = [jnp.exp(one - peak) for one in peaks]
@@ -986,15 +1084,13 @@
     lane = lax.broadcasted_iota(jnp.int32, total.shape, 1)
     total = jnp.where(lane < H, total, 1.0)
     heads = sum(parts[k, :, 0:D] * lanes_over_heads(scales[k] / total) for k in range(PASS_EX))
-    low = to_low(heads)
-    mixed[...] = low
+    low = mixed = to_low(heads)
     wait_whole(wout, sems.at[0])
     second = first[...] + dot(low, wout[...])
     low = to_low(rms_scale(second, gains[5:6, :]))
-    normed[...] = low
     output_grad = dec_cot[...].astype(f32) * valid[:, 0:1]
     grad_low = to_low(output_grad)
-    branch[...] = grad_low
+    acts, inner_grads = [], []
     wait_whole(wup, sems.at[1])
     wait_whole(wdown, sems.at[2])
     after = second
@@ -1003,18 +1099,25 @@
         cols = slice(c * D, (c + 1) * D)
         value, slope = gate_both(dot(low, wup[:, cols]))
         value = to_low(value)
-        act_low[:, cols] = value
+        acts.append(value)
         after = after + dot(value, wdown[cols, :])
         grad = to_low(slope * dot_nt(grad_low, wdown[cols, :]))
-        inner_grad[:, cols] = grad
+        inner_grads.append(grad)
         back_sum = back_sum + dot_nt(grad, wup[:, cols])
     result[...] = to_low(after)
     part, gain_grad = norm_back(second, gains[5:6, :], back_sum)
     grad = output_grad + part
     second_grad[...] = grad
     gain_sums[...] = jnp.broadcast_to(gain_grad, gain_sums.shape)
-    low = to_low(grad)
-    cross_grad[...] = low
+    normed, low = low, to_low(grad)
+    middle[:, : 17 * D] = pack_rows(
+        (
+            jnp.concatenate([normed] + inner_grads, axis=1),
+            jnp.concatenate(acts + [grad_low], axis=1),
+            jnp.concatenate([mixed, low], axis=1),
+        )
+    )
+    middle[:, 17 * D :] = early[...]
     head_grad = to_low(dot_nt(low, wout[...])).astype(f32)
     back[:, 0:D] = head_grad
     back[:, D : D + BLK] = peak + jnp.log(total)
@@ -1027,17 +1130,17 @@
     back[:, D + BLK :] = inner
 
 
-def decoder_feed(rows, parts, first, dec_cot, valid, gathered, gains):
-    low, full, wide = ((AROWS, D), bf16), ((AROWS, D), f32), ((AROWS, FF), bf16)
+def decoder_feed(rows, parts, first, dec_cot, valid, early, gathered, gains):
+    low, full = ((AROWS, D), bf16), ((AROWS, D), f32)
     return decoder_call(
-        feed_decoder_kernel, "decoder_feed", rows, (parts, first, dec_cot, valid, gathered, gains),
-        [low, low, low, wide, wide, low, low, ((AROWS, SIDE), f32), full, ((8, D), f32)],
+        feed_decoder_kernel, "decoder_feed", rows, (parts, first, dec_cot, valid, early, *gathered, gains),
+        [low, ((HELD, 21 * D), bf16), ((AROWS, SIDE), f32), full, ((8, D), f32)],
         [pltpu.VMEM((D, D), bf16), pltpu.VMEM((D, FF), bf16), pltpu.VMEM((FF, D), bf16), pltpu.SemaphoreType.DMA((3,))],
     )
 
 
 def cross_back_kernel(
-    rows_ref, lengths, offsets, queries, back, memory, enc_cot, gathered,
+    rows_ref, lengths, offsets, queries, back, memory, enc_cot, near, far,
     memory_grad, query_grad, upstream, wkv, sems,
 ):
     step = pl.program_id(0)
@@ -1045,7 +1148,7 @@
     @pl.when(step == 0)
     def _():
         for m in range(2):
-            start_blocks(rows_ref, gathered, CROSS_KV + 36 * m, D, D, wkv.at[m], sems.at[m])
+            start_blocks(rows_ref, (near, far), CROSS_KV + 36 * m, D, D, wkv.at[m], sems.at[m])
 
     length = lengths[step]
     spread = spread_heads(queries[0])
@@ -1088,7 +1191,7 @@
                 pl.BlockSpec((1, AROWS, SIDE), at_offset),
                 pl.BlockSpec((PASS_SLOT, 2 * D), by_row),
                 pl.BlockSpec((PASS_SLOT, D), by_row),
-                pl.BlockSpec(memory_space=pl.ANY),
+                *[pl.BlockSpec(memory_space=pl.ANY)] * 2,
             ],
             out_specs=[
                 pl.BlockSpec((PASS_SLOT, 2 * D), by_row),
@@ -1104,24 +1207,22 @@
         ],
         compiler_params=pltpu.CompilerParams(vmem_limit_bytes=VMEM_CAP),
         name="cross_back",
-    )(rows, lengths, offsets, queries, back, memory, enc_cot, gathered)
+    )(rows, lengths, offsets, queries, back, memory, enc_cot, *gathered)
 
 
 def self_back_kernel(
-    rows_ref, parts, second_grad, first, dec_ref, qkv, gathered, gains, bias,
-    result, cross_grad, out_grad, qkv_grad, score_grads, gain_sums, wqkv, wout, wcq, sems,
+    rows_ref, part_zero, part_one, part_two, second_grad, first, dec_ref, qkv, near, far, gains, bias,
+    result, late, score_grads, gain_sums, wqkv, wout, wcq, sems,
 ):
-    start_blocks(rows_ref, gathered, CROSS_Q, D, D, wcq, sems.at[4])
-    start_blocks(rows_ref, gathered, DEC_OUT, D, D, wout, sems.at[3])
+    start_blocks(rows_ref, (near, far), CROSS_Q, D, D, wcq, sems.at[4])
+    start_blocks(rows_ref, (near, far), DEC_OUT, D, D, wout, sems.at[3])
     for m in range(3):
-        start_blocks(rows_ref, gathered, DEC_QKV + 36 * m, D, D, wqkv.at[m], sems.at[m])
-    low = to_low(parts[0] + parts[1] + parts[2])
-    cross_grad[...] = low
+        start_blocks(rows_ref, (near, far), DEC_QKV + 36 * m, D, D, wqkv.at[m], sems.at[m])
+    low = cross_grad = to_low(part_zero[...] + part_one[...] + part_two[...])
     wait_whole(wcq, sems.at[4])
     part, second_gain = norm_back(first[...], gains[4:5, :], dot_nt(low, wcq[...]))
     first_grad = second_grad[...] + part
-    low = to_low(first_grad)
-    out_grad[...] = low
+    low = out_grad = to_low(first_grad)
     wait_whole(wout, sems.at[3])
     heads_grad = spread_heads(to_low(dot_nt(low, wout[...])))
     queries = qkv[:, 0:D]
@@ -1140,9 +1241,12 @@
         dot_tn(to_low(probs), heads_grad),
     )
     total = jnp.zeros((AROWS, D), f32)
+    lows = [to_low(grad) for grad in grads]
+    packed = pack_rows((jnp.concatenate(lows, axis=1), out_grad, cross_grad))
+    for j in range(LATE_COLS):
+        late[j * HELD : (j + 1) * HELD, :] = packed[:, j * BLK : (j + 1) * BLK]
     for m in range(3):
-        low = to_low(grads[m])
-        qkv_grad[:, m * D : (m + 1) * D] = low
+        low = lows[m]
         wait_whole(wqkv.at[m], sems.at[m])
         total = total + dot_nt(low, wqkv[m])
     part, first_gain = norm_back(dec_ref[...].astype(f32), gains[3:4, :], total)
@@ -1151,50 +1255,65 @@
     gain_sums[1:2, :] = second_gain
 
 
+LATE_COLS = 8 * D // BLK
+
+
 def decoder_self_back(rows, parts, second_grad, first, dec_rows, qkv, gathered, gains, bias):
-    low, full = ((AROWS, D), bf16), ((AROWS, D), f32)
+    full = ((AROWS, D), f32)
     square = pltpu.VMEM((D, D), bf16)
     return decoder_call(
         self_back_kernel, "decoder_self_back", rows,
-        (parts, second_grad, first, dec_rows, qkv, gathered, gains, bias),
-        [full, low, low, ((AROWS, 3 * D), bf16), ((HROWS, AROWS), f32), ((8, D), f32)],
+        (*parts, second_grad, first, dec_rows, qkv, *gathered, gains, bias),
+        [full, ((LATE_COLS * HELD, BLK), bf16), ((HROWS, AROWS), f32), ((8, D), f32)],
         [pltpu.VMEM((3, D, D), bf16), square, square, pltpu.SemaphoreType.DMA((5,))],
     )
 
 
-def shift_kernel(way, one, two, got_one, got_two, ssem, rsem):
+def shift_kernel(way, apart, source, got, ssem, rsem, lsem):
     size = lax.axis_size("dp")
     me = lax.axis_index("dp")
     core = lax.axis_index("opt")
     bar = pltpu.get_barrier_semaphore()
     for k in (1, 2):
         pl.semaphore_signal(bar, inc=1, device_id=((me - way * k + size) % size, core), device_id_type=MESH)
+    own = pltpu.make_async_copy(source.at[0] if apart else source, got.at[0], lsem.at[0])
+    own.start()
     pl.semaphore_wait(bar, 2)
-    copies = []
-    for k, source, dest in ((1, one, got_one), (2, two, got_two)):
-        copies.append(
-            pltpu.make_async_remote_copy(
-                src_ref=source, dst_ref=dest, send_sem=ssem.at[k - 1], recv_sem=rsem.at[k - 1],
-                device_id=((me + way * k + size) % size, core), device_id_type=MESH,
-            )
+    copies = [
+        pltpu.make_async_remote_copy(
+            src_ref=source.at[k] if apart else source, dst_ref=got.at[k], send_sem=ssem.at[k - 1], recv_sem=rsem.at[k - 1],
+            device_id=((me + way * k + size) % size, core), device_id_type=MESH,
         )
+        for k in (1, 2)
+    ]
     for copy in copies:
         copy.start()
+    own.wait()
     for copy in copies:
         copy.wait()
 
 
-def shifted(one, two, way, cid):
+def shifted(source, way, apart, cid):
+    shape = source.shape if apart else (PASS_EX,) + source.shape
     vmem = pl.BlockSpec(memory_space=pltpu.VMEM)
     return pl.pallas_call(
-        functools.partial(shift_kernel, way),
-        in_specs=[vmem, vmem],
-        out_specs=[vmem, vmem],
-        out_shape=[jax.ShapeDtypeStruct(one.shape, one.dtype), jax.ShapeDtypeStruct(two.shape, two.dtype)],
-        scratch_shapes=[pltpu.SemaphoreType.DMA((2,)), pltpu.SemaphoreType.DMA((2,))],
+        functools.partial(shift_kernel, way, apart),
+        in_specs=[vmem],
+        out_specs=vmem,
+        out_shape=jax.ShapeDtypeStruct(shape, source.dtype),
+        scratch_shapes=[
+            pltpu.SemaphoreType.DMA((2,)),
+            pltpu.SemaphoreType.DMA((2,)),
+            pltpu.SemaphoreType.DMA((1,)),
+        ],
         compiler_params=pltpu.CompilerParams(collective_id=cid, has_side_effects=True),
         name="shift_rows",
-    )(one, two)
+    )(source)
+
+
+def passed_along(values, by):
+    size = lax.axis_size("dp")
+    return lax.ppermute(values, "dp", [(i, (i + by) % size) for i in range(size)])
 
 
 SQUARE = D * D // BLK
@@ -1212,60 +1331,17 @@
             )
 
 
-def up_weight_kernel(left, right, out_ref):
-    put_blocks(out_ref, dot_tn(left[...], right[...]))
-
-
-def up_weight(left, right):
-    count = left.shape[0]
-    tile = 256
-    return pl.pallas_call(
-        up_weight_kernel,
-        grid=(D // tile,),
-        in_specs=[pl.BlockSpec((count, tile), lambda p: (0, p)), pl.BlockSpec((count, FF), lambda p: (0, 0))],
-        out_specs=pl.BlockSpec((tile * FF // BLK, BLK), lambda p: (p, 0)),
-        out_shape=jax.ShapeDtypeStruct((GROUP_ONE, BLK), bf16),
-        compiler_params=pltpu.CompilerParams(vmem_limit_bytes=VMEM_CAP),
-        name="up_weight",
-    )(left, right)
-
-
-def down_weight_kernel(left, right, into, out_ref):
-    put_blocks(out_ref, dot_tn(left[...], right[...]))
-
-
-def down_weight(left, right, into):
-    count = left.shape[0]
-    first = D * FF // BLK // SQUARE
-    return pl.pallas_call(
-        down_weight_kernel,
-        grid=(FF // D,),
-        in_specs=[
-            pl.BlockSpec((count, D), lambda p: (0, p)),
-            pl.BlockSpec((count, D), lambda p: (0, 0)),
-            pl.BlockSpec(memory_space=pl.ANY),
-        ],
-        out_specs=pl.BlockSpec((SQUARE, BLK), lambda p: (first + p, 0)),
-        out_shape=jax.ShapeDtypeStruct(into.shape, bf16),
-        input_output_aliases={2: 0},
-        compiler_params=pltpu.CompilerParams(vmem_limit_bytes=VMEM_CAP),
-        name="down_weight",
-    )(left, right, into)
-
-
-def square_weight_kernel(pairs, has_into, *refs):
-    sources, refs = refs[: len(pairs[0])], refs[len(pairs[0]) + has_into :]
-    out_ref, held, sems = refs
+def square_weight_kernel(columns, products, *refs):
+    count = len(columns)
+    sources, (out_ref, held, sems) = refs[:count], refs[count:]
     step = pl.program_id(0)
-    columns, products = pairs
 
     def fetch(k):
-        source, col = columns[k]
-        return pltpu.make_async_copy(sources[k].at[:, pl.ds(col, D)], held.at[k], sems.at[k])
+        return pltpu.make_async_copy(sources[k].at[:, pl.ds(columns[k], D)], held.at[k], sems.at[k])
 
     @pl.when(step == 0)
     def _():
-        for k in range(len(columns)):
+        for k in range(count):
             fetch(k).start()
 
     seen = set()
@@ -1280,45 +1356,31 @@
             put_blocks(out_ref, dot_tn(held[a], held[b]))
 
 
-def square_weight(operands, products, into, first, total):
+def square_weight(operands, products, total):
     any_space = pl.BlockSpec(memory_space=pl.ANY)
     arrays = [array for array, _ in operands]
-    columns = [(k, col) for k, (_, col) in enumerate(operands)]
+    columns = [col for _, col in operands]
     count = arrays[0].shape[0]
-    extra = [] if into is None else [into]
     return pl.pallas_call(
-        functools.partial(square_weight_kernel, (columns, products), len(extra)),
+        functools.partial(square_weight_kernel, columns, products),
         grid=(len(products),),
-        in_specs=[any_space] * (len(arrays) + len(extra)),
-        out_specs=pl.BlockSpec((SQUARE, BLK), lambda p: (first + p, 0)),
+        in_specs=[any_space] * len(arrays),
+        out_specs=pl.BlockSpec((SQUARE, BLK), lambda p: (p, 0)),
         scratch_shapes=[pltpu.VMEM((len(arrays), count, D), bf16), pltpu.SemaphoreType.DMA((len(arrays),))],
         out_shape=jax.ShapeDtypeStruct((total, BLK), bf16),
-        input_output_aliases={len(arrays): 0} if extra else {},
         compiler_params=pltpu.CompilerParams(vmem_limit_bytes=VMEM_CAP),
         name="square_weight",
-    )(*arrays, *extra)
-
-
-HELD = 16
-REST = ALEN - HELD
-
-
-def pack_rows(groups):
-    sides = [jnp.concatenate(group, axis=1) if len(group) > 1 else group[0] for group in groups]
-    main = jnp.concatenate([side[:HELD] for side in sides], axis=1)
-    width = max(side.shape[1] for side in sides)
-    rest = jnp.concatenate([jnp.pad(side[HELD:ALEN], ((0, 0), (0, width - side.shape[1]))) for side in sides], axis=0)
-    return jnp.concatenate([main, pad_rows(rest, HELD)], axis=1)
+    )(*arrays)
 
 
 def block_table():
     table = np.zeros((1009, 8), np.int32)
     wide = D // BLK
-    early, late = 3 * wide, 5 * wide
+    early, late = 20 * wide, 5 * wide
     rows = (
-        (DEC_QKV, 108, 1, 0, 0, early, late, 0),
-        (DEC_OUT, 36, 1, wide, 3 * wide, early, late, 1),
-        (CROSS_Q, 36, 1, 2 * wide, 4 * wide, early, late, 2),
+        (DEC_QKV, 108, 1, 17 * wide, 0, early, late, 0),
+        (DEC_OUT, 36, 1, 18 * wide, 3 * wide, early, late, 1),
+        (CROSS_Q, 36, 1, 19 * wide, 4 * wide, early, late, 2),
         (DEC_UP, 144, 4, 0, wide, 12 * wide, 13 * wide, 0),
         (DEC_DOWN, 144, 4, 5 * wide, 9 * wide, 12 * wide, 16 * wide, 1),
         (CROSS_OUT, 36, 4, 10 * wide, 11 * wide, 12 * wide, 13 * wide, 2),
@@ -1332,16 +1394,19 @@
             else:
                 i, j = divmod(b, 4 * wide if first == DEC_UP else wide)
             table[first + b] = (kind, 0, left + i, right + j, rest_left + i, rest_right + j, group, 0)
-    for first, count, at in ((ENC_UP, 144, 0), (ENC_DOWN, 144, 144), (CROSS_KV, 72, 288), (ENC_OUT, 36, 360)):
+    for first, count, at in ((ENC_DOWN, 144, 144), (CROSS_KV, 72, 288), (ENC_OUT, 36, 360)):
         for b in range(count):
             table[first + b, :2] = (2, at + b)
+    for b in range(144):
+        i, j = divmod(b, 4 * wide)
+        table[ENC_UP + b, :2] = (2, j // wide * 36 + i * wide + j % wide)
     for b in range(108):
         table[b, :2] = (3, b)
     return table
 
 
 def update_kernel(
-    slots, info, early, middle, late, one, two, master, stats, roots,
+    slots, info, middle, late, one, two, master, stats, roots,
     grads, new_stats, new_master, sides, held, summed, sems,
 ):
     step = pl.program_id(0)
@@ -1358,14 +1423,18 @@
 
             def rows_of(left, right, s=s, at=at, copy=copy):
                 for k, source in enumerate((left, right, left, right)):
-                    col = pl.multiple_of(info[at + 2 + k] * BLK, BLK)
-                    action(copy(source.at[:, pl.ds(col, BLK)], sides.at[buffer, s, k], k))
+                    col = info[at + 2 + k]
+                    if source is late:
+                        part = source.at[:, pl.ds(pl.multiple_of(col * HELD, HELD), HELD)]
+                    else:
+                        part = source.at[:, :, pl.ds(pl.multiple_of(col * BLK, BLK), BLK)]
+                    action(copy(part, sides.at[buffer, s, k], k))
 
             def block_of(source, s=s, at=at, copy=copy):
                 row = pl.multiple_of(info[at + 1] * BLK, BLK)
                 action(copy(source.at[pl.ds(row, BLK)], held.at[buffer, s], 4))
 
-            pl.when(kind == 1)(functools.partial(rows_of, early, late))
+            pl.when(kind == 1)(functools.partial(rows_of, middle, late))
             pl.when(kind == 4)(functools.partial(rows_of, middle, middle))
             pl.when(kind == 2)(functools.partial(block_of, one))
             pl.when(kind == 3)(functools.partial(block_of, two))
@@ -1387,10 +1456,10 @@
 
         @pl.when((kind == 1) | (kind == 4))
         def _(s=s, group=group):
-            rest = sides[buffer, s, 2]
+            left, right, rest, rest_right = [sides[buffer, s, k].reshape(-1, BLK) for k in range(4)]
             row = lax.broadcasted_iota(jnp.int32, rest.shape, 0)
             mine = jnp.where(row % HELD // REST == group, rest, jnp.zeros_like(rest))
-            summed[s] = dot_tn(sides[buffer, s, 0], sides[buffer, s, 1]) + dot_tn(mine, sides[buffer, s, 3])
+            summed[s] = dot_tn(left, right) + dot_tn(mine, rest_right)
 
         @pl.when((kind == 2) | (kind == 3))
         def _(s=s):
@@ -1414,10 +1483,10 @@
         new_master[s] = old - (block_rate * weight_rms / shaped_rms) * shaped
 
 
-def update_blocks(info, early, middle, late, one, two, master, kron_stats, inverse_roots):
+def update_blocks(info, middle, late, one, two, master, kron_stats, inverse_roots):
     count = master.shape[0]
     slots = min(4, count)
-    depth = early.shape[0]
+    devices = late.shape[0]
     any_space = pl.BlockSpec(memory_space=pl.ANY)
     block = pl.BlockSpec((slots, BLK, BLK), lambda p, *_: (p, 0, 0))
     pair = pl.BlockSpec((slots, 2, BLK, BLK), lambda p, *_: (p, 0, 0, 0))
@@ -1426,10 +1495,10 @@
         grid_spec=pltpu.PrefetchScalarGridSpec(
             num_scalar_prefetch=1,
             grid=(count // slots,),
-            in_specs=[any_space] * 5 + [block, pair, pair],
+            in_specs=[any_space] * 4 + [block, pair, pair],
             out_specs=[block, pair, block],
             scratch_shapes=[
-                pltpu.VMEM((2, slots, 4, depth, BLK), bf16),
+                pltpu.VMEM((2, slots, 4, devices, HELD, BLK), bf16),
                 pltpu.VMEM((2, slots, BLK, BLK), bf16),
                 pltpu.VMEM((slots, BLK, BLK), f32),
                 pltpu.SemaphoreType.DMA((2, slots, 5)),
@@ -1442,13 +1511,39 @@
         ],
         compiler_params=pltpu.CompilerParams(vmem_limit_bytes=VMEM_CAP),
         name="update_blocks",
-    )(info, early, middle, late, one, two, master, kron_stats, inverse_roots)
-
-
-def gather_all(shard, dp_count):
-    if dp_count == 16:
-        return gather_rows(shard, dp_count, 0)
-    return lax.all_gather(shard, ("dp", "opt"), axis=0, tiled=True)
+    )(info, middle, late, one, two, master, kron_stats, inverse_roots)
+
+
+def order_kernel(order, master, small, near, far, held, sems):
+    count = held.shape[0]
+    for s in range(count):
+        pltpu.make_async_copy(master.at[order[s]], held.at[s], sems.at[s]).start()
+    near[0:EXTRA, :] = small[...]
+    first = near.shape[0]
+    for s in range(count):
+        pltpu.make_async_copy(master.at[order[s]], held.at[s], sems.at[s]).wait()
+        at = EXTRA + s * BLK
+        if at < first:
+            near[at : at + BLK, :] = to_low(held[s])
+        else:
+            far[at - first : at - first + BLK, :] = to_low(held[s])
+
+
+def ordered_shards(order, master, small, near_rows):
+    count = master.shape[0]
+    shapes = [(near_rows, BLK), (max(EXTRA + count * BLK - near_rows, EXTRA), BLK)]
+    return pl.pallas_call(
+        order_kernel,
+        grid_spec=pltpu.PrefetchScalarGridSpec(
+            num_scalar_prefetch=1,
+            grid=(1,),
+            in_specs=[pl.BlockSpec(memory_space=pl.ANY), whole_spec(small.shape)],
+            out_specs=[whole_spec(shape) for shape in shapes],
+            scratch_shapes=[pltpu.VMEM((count, BLK, BLK), f32), pltpu.SemaphoreType.DMA((count,))],
+        ),
+        out_shape=[jax.ShapeDtypeStruct(shape, bf16) for shape in shapes],
+        name="ordered_shards",
+    )(order, master, small)
 
 
 def total_all(terms, dp_count):
@@ -1486,18 +1581,66 @@
     slot_dev = master.shape[0]
     small_dev = small_params.shape[0]
     dev_rows = slot_dev * BLK + EXTRA
-    total_rows = devices * dev_rows
     table_size = NB * H
+    device = lax.axis_index("dp") * pair_count + lax.axis_index("opt")
+
+    kinds = jnp.asarray((np.arange(owner_slot.shape[0]) >= DEC_QKV).astype(np.int32))
+    owners, local = owner_slot // slot_dev, owner_slot % slot_dev
+    keys = (owners * 4 + kinds) * slot_dev + local
+    before = (keys[None, :] < keys[:, None]) & (owners[None, :] == owners[:, None])
+    rank = jnp.sum(before.astype(jnp.int32), axis=1)
+    split = dp_count == 16 and slot_dev > EARLY_SLOTS
+    near_slots = EARLY_SLOTS if split else slot_dev
+    near_rows, far_rows = EXTRA + near_slots * BLK, (slot_dev - near_slots) * BLK
+    rows = jnp.where(
+        rank < near_slots,
+        owners * near_rows + EXTRA + rank * BLK,
+        -1 - (owners * far_rows + (rank - near_slots) * BLK),
+    ).astype(jnp.int32)
+    mine = owner_slot[None, :] == (device * slot_dev + jnp.arange(slot_dev))[:, None]
+    block_at = jnp.sum(jnp.where(mine, jnp.arange(owner_slot.shape[0])[None, :] + 1, 0), axis=1)
+    own_kind = 2 - jnp.sum(jnp.where(mine, 2 - kinds[None, :], 0), axis=1)
+    own_keys = own_kind * slot_dev + jnp.arange(slot_dev)
+    own_rank = jnp.sum((own_keys[None, :] < own_keys[:, None]).astype(jnp.int32), axis=1)
+    order = jnp.sum(
+        jnp.where(own_rank[None, :] == jnp.arange(slot_dev)[:, None], jnp.arange(slot_dev)[None, :], 0), axis=1
+    ).astype(jnp.int32)
 
     padded = jnp.pad(to_low(small_params), (0, EXTRA * BLK - small_dev)).reshape(EXTRA, BLK)
-    gathered = gather_all(
-        jnp.concatenate([to_low(master).reshape(slot_dev * BLK, BLK), padded], axis=0), dp_count
-    )
-    small_all = gathered.reshape(devices, dev_rows, BLK)[:, slot_dev * BLK :]
+    near, later = ordered_shards(order, master, padded, near_rows)
+    if split:
+        near = gather_rows(near, near_rows, dp_count, 0)
+        later, near = lax.optimization_barrier((later, near))
+        far = gather_low(later)
+    else:
+        near = far = gather_low(near)
+    small_all = near.reshape(devices, near_rows, BLK)[:, :EXTRA]
     small_all = small_all.reshape(devices, EXTRA * BLK)[:, :small_dev].reshape(-1).astype(f32)
     gains = pad_rows(small_all[: 6 * D].reshape(6, D), 8)
-    rows = (owner_slot // slot_dev * dev_rows + owner_slot % slot_dev * BLK).astype(jnp.int32)
     strips = bias_strips(small_all[6 * D : 6 * D + table_size])
+
+    def encoder(rows, gathered):
+        qkv, log_total, mixed, hidden, whole = encoder_attend(rows, passage_lengths, enc_in, gathered, gains, strips)
+        inner, output, encoded, up, down = encoder_feed(rows, hidden, gathered, gains)
+        return qkv, log_total, mixed, hidden, whole, inner, output, encoded, up, down
+
+    gathered = (near, far)
+    if split:
+        state = encoder(jnp.maximum(rows, 0), (near, near))
+        far, state = lax.optimization_barrier((far, state))
+        gathered = (near, far)
+        late_blocks = jnp.any((kinds == 0) & (rank >= near_slots))
+
+        def again(carry):
+            count, fresh_rows = lax.optimization_barrier((carry[0], rows))
+            return count + 1, encoder(fresh_rows, gathered)
+
+        _, state = lax.while_loop(
+            lambda carry: carry[0] < late_blocks.astype(jnp.int32), again, (jnp.int32(0), state)
+        )
+    else:
+        state = encoder(rows, gathered)
+    qkv, log_total, mixed, hidden, whole, inner, output, encoded, up, down = state
     answer_at = np.arange(AROWS)
     dec_buckets = bucket_of(np.minimum(answer_at, ALEN - 1)[None, :] - np.minimum(answer_at, ALEN - 1)[:, None], False)
     dec_onehot = jnp.asarray((dec_buckets[..., None] == np.arange(NB)).reshape(-1, NB).astype(np.float32))
@@ -1505,76 +1648,55 @@
         small_all[6 * D + table_size :].reshape(NB, H).T, dec_onehot.T, precision=exact_prec, preferred_element_type=f32
     ).reshape(HROWS, AROWS)
 
-    dec_rows = pad_rows(dec_in, AROWS)
-    dec_qkv, dec_mixed, first, dec_normed, dec_normed_two, cross_queries = decoder_self(
-        rows, dec_rows, gathered, gains, dec_bias
-    )
-    from_one, from_two = shifted(cross_queries, cross_queries, 1, 2)
-    early, enc_rows = lax.optimization_barrier(
-        (pack_rows(((dec_normed,), (dec_mixed,), (dec_normed_two,))), enc_in)
-    )
-    early = gather_low(early)
-    queries = jnp.stack([cross_queries, from_one, from_two])
-
+    dec_rows, encoded = lax.optimization_barrier((pad_rows(dec_in, AROWS), encoded))
+    dec_qkv, first, cross_queries, early = decoder_self(rows, dec_rows, gathered, gains, dec_bias)
+    moved = [passed_along(cross_queries, k) for k in (1, 2)]
+    memory = cross_memory(rows, encoded, gathered)
+    moved, memory = lax.optimization_barrier((moved, memory))
+    queries = jnp.stack([cross_queries] + moved)
     owner_dp = passage_example // EX_DEV // pair_count
     offsets = ((lax.axis_index("dp") - owner_dp) % dp_count).astype(jnp.int32)
-    qkv, log_total, mixed, hidden = encoder_attend(rows, passage_lengths, enc_rows, gathered, gains, strips)
-    inner, output, encoded, memory = encoder_feed(rows, hidden, gathered, gains)
 
     parts = cross_attend(passage_lengths, offsets, queries, memory)
-    part_one, part_two = shifted(parts[1], parts[2], -1, 3)
+    parts = shifted(parts, -1, True, 3)
     valid = (pad_rows(answer_tokens.reshape(ALEN, 1), AROWS) != 0).astype(f32)
-    dec_out, cross_mixed, dec_normed_three, dec_act, dec_inner_grad, dec_branch, cross_out_grad, back, second_grad, gain_six = (
-        decoder_feed(
-            rows, jnp.stack([parts[0], part_one, part_two]), first, pad_rows(dec_cot, AROWS),
-            jnp.broadcast_to(valid, (AROWS, BLK)), gathered, gains,
-        )
-    )
-    middle = pack_rows(
-        ((dec_normed_three, dec_inner_grad), (dec_act, dec_branch), (cross_mixed, cross_out_grad))
-    )
-    middle, back, early = lax.optimization_barrier((middle, back, early))
+    dec_out, middle, back, second_grad, gain_six = decoder_feed(
+        rows, parts, first, pad_rows(dec_cot, AROWS), jnp.broadcast_to(valid, (AROWS, BLK)), early, gathered, gains
+    )
+    middle, back = lax.optimization_barrier((middle, back))
     middle = gather_low(middle)
-    back_one, back_two = shifted(back, back, 1, 4)
     memory_grad, query_parts, upstream = cross_back(
-        rows, passage_lengths, offsets, queries, jnp.stack([back, back_one, back_two]), memory, enc_cot, gathered
-    )
-    query_one, query_two = shifted(query_parts[1], query_parts[2], -1, 5)
-    dec_in_grad, cross_query_grad, dec_out_grad, dec_qkv_grad, dec_scores, gain_four = decoder_self_back(
-        rows, jnp.stack([query_parts[0], query_one, query_two]), second_grad, first, dec_rows, dec_qkv, gathered, gains, dec_bias
-    )
-
-    late = pack_rows(((dec_qkv_grad,), (dec_out_grad,), (cross_query_grad,)))
-    late, upstream = lax.optimization_barrier((late, upstream))
+        rows, passage_lengths, offsets, queries, shifted(back, 1, False, 4), memory, enc_cot, gathered
+    )
+    query_parts = [query_parts[0]] + [passed_along(query_parts[k], -k) for k in (1, 2)]
 
     act, inner_grad, branch, normed_two, hidden_grad, attn_grad, mixed_grad, gain_two = feed_back(
-        rows, output, hidden, inner, upstream, gathered, gains
-    )
-    late, middle, inner_grad = lax.optimization_barrier((late, middle, inner_grad))
-    late = gather_low(late)
-    one = up_weight(normed_two, inner_grad)
-    one = down_weight(act, branch, one)
+        output, hidden, inner, upstream, down, up, whole, gains
+    )
+    query_parts, inner_grad = lax.optimization_barrier((query_parts, inner_grad))
+    dec_in_grad, late, dec_scores, gain_four = decoder_self_back(
+        rows, query_parts, second_grad, first, dec_rows, dec_qkv, gathered, gains, dec_bias
+    )
     one = square_weight(
-        [(encoded, 0), (memory_grad, 0), (memory_grad, D), (mixed, 0), (attn_grad, 0)],
-        [(0, 1), (0, 2), (3, 4)], one, 2 * D * FF // BLK // SQUARE, GROUP_ONE,
-    )
-    grad_query, grad_key, grad_value, bias_sums, one = attend_back(
-        passage_lengths, qkv, mixed_grad, log_total, strips, one, dp_count, 6
-    )
-    one, late = lax.optimization_barrier((one, late))
+        [(normed_two, 0)] + [(inner_grad, k * D) for k in range(4)]
+        + [(branch, 0)] + [(act, k * D) for k in range(4)]
+        + [(encoded, 0), (memory_grad, 0), (memory_grad, D), (mixed, 0), (attn_grad, 0)],
+        [(0, 1 + k) for k in range(4)] + [(6 + k, 5) for k in range(4)] + [(10, 11), (10, 12), (13, 14)],
+        GROUP_ONE,
+    )
+    grad_query, grad_key, grad_value, enc_table, one, late = attend_back(
+        passage_lengths, qkv, mixed_grad, log_total, strips, one, late, dp_count, 6
+    )
+    one, middle = lax.optimization_barrier((one, middle))
     one = gather_low(one)
     enc_in_grad, normed, gain_one = input_back(
-        rows, enc_in, grad_query, grad_key, grad_value, hidden_grad, gathered, gains
+        enc_in, grad_query, grad_key, grad_value, hidden_grad, whole, gains
     )
     two = square_weight(
-        [(normed, 0), (grad_query, 0), (grad_key, 0), (grad_value, 0)], [(0, 1), (0, 2), (0, 3)], None, 0, GROUP_TWO
-    )
-
-    inner_strip = bias_sums[:, 2 * BLK : 5 * BLK].reshape(H, -1)
-    strip_onehot = jnp.asarray(strip_buckets().reshape(-1, 1) == np.arange(NB)[None, :]).astype(f32)
-    enc_table = jnp.dot(inner_strip, strip_onehot, precision=exact_prec, preferred_element_type=f32).T
-    enc_table = enc_table.at[NB // 2 - 1].add(jnp.sum(bias_sums[:, : 2 * BLK], axis=(1, 2)))
-    enc_table = enc_table.at[NB - 1].add(jnp.sum(bias_sums[:, 5 * BLK :], axis=(1, 2)))
+        [(normed, 0), (grad_query, 0), (grad_key, 0), (grad_value, 0)], [(0, 1), (0, 2), (0, 3)], GROUP_TWO
+    )
+
+    enc_table = enc_table[:, :2, :NB].reshape(H, NB).T
     dec_table = jnp.dot(
         dec_scores.reshape(H, AROWS * AROWS), dec_onehot, precision=exact_prec, preferred_element_type=f32
     ).T
@@ -1584,13 +1706,10 @@
     small_rows = pad_rows(to_low(small_terms).reshape(-1, BLK), SMALL_ROWS)
     two = total_all(lax.dynamic_update_slice(two, small_rows, (3 * SQUARE, 0)), dp_count)
 
-    device = lax.axis_index("dp") * pair_count + lax.axis_index("opt")
     small_grads = lax.dynamic_slice(two[3 * SQUARE :].reshape(-1), (device * small_dev,), (small_dev,)).astype(f32)
-    here = device * slot_dev + jnp.arange(slot_dev)
-    place = jnp.where(owner_slot[None, :] == here[:, None], jnp.arange(owner_slot.shape[0])[None, :] + 1, 0)
-    block_at = jnp.sum(place, axis=1)
     info = jnp.asarray(np.roll(block_table(), 1, axis=0))[block_at].reshape(-1)
-    block_grads, new_stats, new_master = update_blocks(info, early, middle, late, one, two, master, kron_stats, inverse_roots)
+    middle, late = (part.reshape(devices, -1, part.shape[1]) for part in (middle, late))
+    block_grads, new_stats, new_master = update_blocks(info, middle, late, one, two, master, kron_stats, inverse_roots)
     new_moment = moment_decay * small_moment + small_grads
     new_small = small_params - small_rate * new_moment
     return (

time: 687 us -> 611 us (0.89)
  Pallas kernels: 608 us -> 548 us
  local copies, waits for them, and re-layouts: 34.5 us -> 17 us
  other arithmetic: 15.1 us -> 7.79 us
    pallas_call x1, Pallas kernels: 132 us -> 96 us  [gather_rows(): pl.pallas_call(functools.partial(gather_kernel, plan, nbits, rows), out_s...]
    slice x22 -> x2, local copies, waits for them, and re-layouts: 15.2 us -> 1.81 us  [the longest x1 1.06 us: per_device(): small_all = near.reshape(devices, near_rows, BLK)[:, :EXTRA]]
    pallas_call x1, Pallas kernels: 52.8 us -> 43.2 us  [encoder_attend(): pl.pallas_call(attend_kernel, grid_spec=pltpu.PrefetchScalarGridSpec(num_...]
    pallas_call x9 -> x7, Pallas kernels: 172 us -> 173 us  [the longest x1 96.8 us: attend_back(): pl.pallas_call(functools.partial(attend_back_kernel, plan, shard_plan, nb...]
  transfers between devices with their start and end apart: 4 -> 7, of which waited for: 1 -> 1; matrix products, arithmetic and copies ran while one was open for 6% -> 3% of each run, Pallas kernels for 66% -> 65%
where the time goes in v3:
time: 611 us; the launch traced here: 604 us
  Pallas kernels  548 us (90%)
  local copies, waits for them, and re-layouts  17 us (3%)
  between operations  14.6 us (2%)
  waiting for transfers between devices  7.91 us (1%)
  other arithmetic  7.79 us (1%)
  starting transfers between devices  6.82 us (1%)
    pallas_call x1, Pallas kernels, attend_back(): pl.pallas_call(functools.partial(attend_back_kernel, plan, shard_plan, nb...  96.8 us
    pallas_call x1, Pallas kernels, gather_rows(): pl.pallas_call(functools.partial(gather_kernel, plan, nbits, rows), out_s...  96 us
    pallas_call x1, Pallas kernels, total_rows_all(): pl.pallas_call(functools.partial(total_kernel, plan, nbits, rows), out_sh...  74.6 us
    pallas_call x1, Pallas kernels, encoder_attend(): pl.pallas_call(attend_kernel, grid_spec=pltpu.PrefetchScalarGridSpec(num_...  43.2 us
    pallas_call x2, Pallas kernels, square_weight(): pl.pallas_call(functools.partial(square_weight_kernel, columns, products)...  37.4 us
    pallas_call x1, Pallas kernels, feed_back(): pl.pallas_call(feed_back_kernel, grid_spec=pltpu.PrefetchScalarGridSpec(n...  37.1 us
    pallas_call x3, Pallas kernels, decoder_call(): pl.pallas_call(body, grid_spec=pltpu.PrefetchScalarGridSpec(num_scalar_pr...  31.4 us
    pallas_call x1, Pallas kernels, encoder_feed(): pl.pallas_call(feed_kernel, grid_spec=pltpu.PrefetchScalarGridSpec(num_sc...  27.6 us
  transfers between devices with their start and end apart: 7, of which 1 were waited for; matrix products, arithmetic and copies ran while one was open for 3% of the time, Pallas kernels for 65%

profile of v3, /device:TPU:0, one launch (start us, length us, event | category | flops | bytes accessed | tf_op | source)
XLA Modules:
  0.0 604.4 jit_solution(13318980912516656357)
XLA Ops:
  10.8 4.1 ordered_shards.1
  14.9 96.0 %gather_rows.1.near.far = bf16[90624,128]{1,0:T(8,128)(2,1)} custom-call(bf16[2832,128]{1,0:T(8,128)(2,1)} %get-tuple-element.194.shard), custom_call_target="tpu_custom_call" | custom-call | tf_op jit(solution)/shard_map/gather_rows/pallas_call | solution.py:346
  113.3 8.6 %bias_strips.1.strips = f32[12,896,128]{2,1,0:T(8,128)} custom-call(f32[384]{0:T(512)} %slice_convert_fusion.3.table, s32[384,128]{1,0:T(8,128)} %constant.123.clone.buckets), custom_call_target="tpu_custom_call" | custom-call | tf_op jit(solution)/shard_map/bias_strips/pallas_call | solution.py:401
  123.7 43.2 %encoder_attend.2 = (bf16[1536,2304]{1,0:T(8,128)(2,1)}, f32[3,16,512]{2,1,0:T(8,128)}, bf16[1536,768]{1,0:T(8,128)(2,1)}, f32[1536,768]{1,0:T(8,128)}, bf16[4,768,768]{2,1,0:T(8,128)(2,1)}) custom-call(s32[1008]{0:T(1024)} %get-tuple-element.324.rows_ref, s32[3]{0:T(128)S(1)} %copy-done.9, bf16[1536,768]{1,0:T(8,128)(2,1)S(1)} %copy-done, ...), custom_call_target="tpu_custom_call" | custom-call | tf_op jit(solution)/shard_map/encoder_attend/pallas_call | solution.py:481
  166.9 27.6 %encoder_feed.2 = (bf16[1536,3072]{1,0:T(8,128)(2,1)}, f32[1536,768]{1,0:T(8,128)}, bf16[1536,768]{1,0:T(8,128)(2,1)}, bf16[768,3072]{1,0:T(8,128)(2,1)}, bf16[3072,768]{1,0:T(8,128)(2,1)}) custom-call(s32[1008]{0:T(1024)} %get-tuple-element.324.rows_ref, f32[1536,768]{1,0:T(8,128)} %get-tuple-element.455.hidden, bf16[90624,128]{1,0:T(8,128)(2,1)} %gather_rows.1.near.far, ...), custom_call_target="tpu_custom_call" | custom-call | tf_op jit(solution)/shard_map/encoder_feed/pallas_call | solution.py:560
  198.7 7.9 %decoder_self.1 = (bf16[32,2304]{1,0:T(8,128)(2,1)}, f32[32,768]{1,0:T(8,128)}, bf16[32,768]{1,0:T(8,128)(2,1)}, bf16[16,3072]{1,0:T(8,128)(2,1)}) custom-call(s32[1008]{0:T(1024)S(1)} %get-tuple-element.522, bf16[32,768]{1,0:T(8,128)(2,1)} %pad.25.dec_ref, bf16[90624,128]{1,0:T(8,128)(2,1)} %get-tuple-element.514, bf16[40960,128]{1,0:T(8,128)(2,1)} %get-tuple-element.516, ...), custom_call_target="tpu_custom_call" | custom-call | tf_op jit(solution)/shard_map/decoder_self/pallas_call | solution.py:982
  206.6 1.9 collective-permute-start
  208.5 3.1 collective-permute-start.1
  212.2 10.0 %cross_memory.1.memory = bf16[1536,1536]{1,0:T(8,128)(2,1)} custom-call(s32[1008]{0:T(1024)S(1)} %get-tuple-element.522, bf16[1536,768]{1,0:T(8,128)(2,1)} %get-tuple-element.184.encoded.refs_10_, bf16[90624,128]{1,0:T(8,128)(2,1)} %get-tuple-element.514, bf16[40960,128]{1,0:T(8,128)(2,1)} %get-tuple-element.516), custom_call_target="tpu_custom_call" | custom-call | tf_op jit(solution)/shard_map/cross_memory/pallas_call | solution.py:1026
  222.9 6.6 %cross_attend.1.source = f32[3,32,1024]{2,1,0:T(8,128)} custom-call(s32[3]{0:T(128)S(1)} %get-tuple-element.537, s32[3]{0:T(128)} %and_select_fusion.offsets, bf16[3,32,768]{2,1,0:T(8,128)(2,1)} %pad_maximum_fusion.queries, bf16[1536,1536]{1,0:T(8,128)(2,1)} %cross_memory.1.memory), custom_call_target="tpu_custom_call" | custom-call | tf_op jit(solution)/shard_map/cross_attend/pallas_call | solution.py:1056
  229.6 12.0 %shift_rows.2.parts = f32[3,32,1024]{2,1,0:T(8,128)} custom-call(f32[3,32,1024]{2,1,0:T(8,128)} %cross_attend.1.source), custom_call_target="tpu_custom_call" | custom-call | tf_op jit(solution)/shard_map/shift_rows/pallas_call | solution.py:1299
  242.2 14.0 %decoder_feed.1 = (bf16[32,768]{1,0:T(8,128)(2,1)}, bf16[16,16128]{1,0:T(8,128)(2,1)}, f32[32,1024]{1,0:T(8,128)}, f32[32,768]{1,0:T(8,128)}, f32[8,768]{1,0:T(8,128)}) custom-call(s32[1008]{0:T(1024)S(1)} %get-tuple-element.522, f32[3,32,1024]{2,1,0:T(8,128)} %shift_rows.2.parts, f32[32,768]{1,0:T(8,128)} %get-tuple-element.225.first, ...), custom_call_target="tpu_custom_call" | custom-call | tf_op jit(solution)/shard_map/decoder_feed/pallas_call | solution.py:982
  256.3 12.8 %shift_rows.3.back = f32[3,32,1024]{2,1,0:T(8,128)} custom-call(f32[32,1024]{1,0:T(8,128)} %get-tuple-element.234.source), custom_call_target="tpu_custom_call" | custom-call | tf_op jit(solution)/shard_map/shift_rows/pallas_call | solution.py:1299
  269.2 17.4 %cross_back.1 = (bf16[1536,1536]{1,0:T(8,128)(2,1)}, f32[3,32,768]{2,1,0:T(8,128)}, f32[1536,768]{1,0:T(8,128)}) custom-call(s32[1008]{0:T(1024)S(1)} %get-tuple-element.522, s32[3]{0:T(128)S(1)} %get-tuple-element.537, s32[3]{0:T(128)} %and_select_fusion.offsets, bf16[3,32,768]{2,1,0:T(8,128)(2,1)} %pad_maximum_fusion.queries, ...), custom_call_target="tpu_custom_call" | custom-call | tf_op jit(solution)/shard_map/cross_back/pallas_call | solution.py:1184
  286.5 1.7 slice_bitcast_fusion.1
  289.8 37.1 %feed_back.1 = (bf16[1536,3072]{1,0:T(8,128)(2,1)}, bf16[1536,3072]{1,0:T(8,128)(2,1)}, bf16[1536,768]{1,0:T(8,128)(2,1)}, bf16[1536,768]{1,0:T(8,128)(2,1)}, f3...) custom-call(f32[1536,768]{1,0:T(8,128)} %get-tuple-element.229.output, ...), custom_call_target="tpu_custom_call" | custom-call | tf_op jit(solution)/shard_map/feed_back/pallas_call | solution.py:652
  327.5 9.4 %decoder_self_back.1 = (f32[32,768]{1,0:T(8,128)}, bf16[768,128]{1,0:T(8,128)(2,1)}, f32[384,32]{1,0:T(8,128)}, f32[8,768]{1,0:T(8,128)}) custom-call(s32[1008]{0:T(1024)S(1)} %get-tuple-element.522, f32[32,768]{1,0:T(8,128)} %get-tuple-element.250.part_zero, f32[32,768]{1,0:T(8,128)} %copy-done.5, f32[32,768]{1,0:T(8,128)} %copy-done.6, ...), custom_call_target="tpu_custom_call" | custom-call | tf_op jit(solution)/shard_map/decoder_self_back/pallas_call | solution.py:982
  337.0 27.8 %square_weight.2.refs_0_ = bf16[50688,128]{1,0:T(8,128)(2,1)} custom-call(bf16[1536,768]{1,0:T(8,128)(2,1)} %get-tuple-element.241.refs_0_, bf16[1536,3072]{1,0:T(8,128)(2,1)} %get-tuple-element.244.refs_1_.refs_2_.refs_3_.refs_4_, bf16[1536,3072]{1,0:T(8,128)(2,1)} %get-tuple-element.244.refs_1_.refs_2_.refs_3_.refs_4_, ...), custom_call_target="tpu_custom_call" | custom-call | tf_op jit(solution)/shard_map/square_weight/pallas_call | solution.py:1364
  364.8 96.8 %attend_back.1 = (bf16[1536,768]{1,0:T(8,128)(2,1)}, bf16[1536,768]{1,0:T(8,128)(2,1)}, bf16[1536,768]{1,0:T(8,128)(2,1)}, f32[6,8,128]{2,1,0:T(8,128)}, bf16[15...) custom-call(s32[3]{0:T(128)S(1)} %get-tuple-element.537, bf16[1536,2304]{1,0:T(8,128)(2,1)} %get-tuple-element.228.q_ref.k_ref.v_ref, ...), custom_call_target="tpu_custom_call" | custom-call | tf_op jit(solution)/shard_map/attend_back/pallas_call | solution.py:813
  467.2 15.1 %input_back.1 = (f32[1536,768]{1,0:T(8,128)}, bf16[1536,768]{1,0:T(8,128)(2,1)}, f32[8,768]{1,0:T(8,128)}) custom-call(bf16[1536,768]{1,0:T(8,128)(2,1)S(1)} %get-tuple-element.518, bf16[1536,768]{1,0:T(8,128)(2,1)} %get-tuple-element.256.gq.refs_1_, bf16[1536,768]{1,0:T(8,128)(2,1)} %get-tuple-element.257.gk.refs_2_, ...), custom_call_target="tpu_custom_call" | custom-call | tf_op jit(solution)/shard_map/input_back/pallas_call | solution.py:866
  482.2 9.6 %square_weight.3 = bf16[14336,128]{1,0:T(8,128)(2,1)} custom-call(bf16[1536,768]{1,0:T(8,128)(2,1)} %get-tuple-element.267.refs_0_, bf16[1536,768]{1,0:T(8,128)(2,1)} %get-tuple-element.256.gq.refs_1_, bf16[1536,768]{1,0:T(8,128)(2,1)} %get-tuple-element.257.gk.refs_2_, bf16[1536,768]{1,0:T(8,128)(2,1)} %get-tuple-element.258.gv.refs_3_), custom_call_target="tpu_custom_call" | custom-call | tf_op jit(solution)/shard_map/square_weight/pallas_call | solution.py:1364
  495.1 74.6 %total_rows.1.two = bf16[14336,128]{1,0:T(8,128)(2,1)} custom-call(bf16[14336,128]{1,0:T(8,128)(2,1)} %pad_dynamic-update-slice_fusion.terms), custom_call_target="tpu_custom_call" | custom-call | tf_op jit(solution)/shard_map/total_rows/pallas_call | solution.py:378
  571.9 7.8 %all-gather.8.cloned.1.call-done.one = bf16[50688,128]{1,0:T(8,128)(2,1)} async-done(((bf16[1584,128]{1,0:T(8,128)(2,1)}), bf16[50688,128]{1,0:T(8,128)(2,1)}) %all-gather.8.cloned.1.call-update) | async-done | bytes 12976144 | tf_op jit(solution)/shard_map/all_gather | solution.py:1556
  579.7 17.9 %update_blocks.1 = (f32[32,128,128]{2,1,0:T(8,128)}, f32[32,2,128,128]{3,2,1,0:T(8,128)}, f32[32,128,128]{2,1,0:T(8,128)}) custom-call(s32[256]{0:T(256)} %reshape.127.info, bf16[32,16,16128]{2,1,0:T(8,128)(2,1)} %bitcast.36, bf16[32,768,128]{2,1,0:T(8,128)(2,1)} %bitcast.37, bf16[50688,128]{1,0:T(8,128)(2,1)} %all-gather.8.cloned.1.call-done.one, ...), custom_call_target="tpu_custom_call" | custom-call | tf_op jit(solution)/shard_map/update_blocks/pallas_call | solution.py:1493
  (121 shorter events, 26.8 us)
Async XLA Ops:
  7.2 190.4 %all-gather.4.cloned.1.call-start = ((), (), s32[]{:S(2)}) async-start(), calls=%async_computation | async-start | bytes 10813440 | tf_op jit(solution)/shard_map/all_gather | solution.py:1556
  111.0 12.7 %copy-start = (bf16[1536,768]{1,0:T(8,128)(2,1)S(1)}, bf16[1536,768]{1,0:T(8,128)(2,1)}, u32[]{:S(2)}) copy-start(bf16[1536,768]{1,0:T(8,128)(2,1)} %x_ref.3) | copy-start | bytes 7077892
  111.0 350.6 %all-gather.6.cloned.1.call-start = ((), (), s32[]{:S(2)}) async-start(), calls=%async_computation.1 | async-start | bytes 17031168 | tf_op jit(solution)/shard_map/all_gather | solution.py:1556
  166.9 27.6 %copy-start.1 = (f32[1024,32]{1,0:T(8,128)S(1)}, f32[1024,32]{1,0:T(8,128)}, u32[]{:S(2)}) copy-start(f32[1024,32]{1,0:T(8,128)} %constant.124.clone) | copy-start | bytes 393220
  166.9 28.8 %copy-start.11 = (bf16[20,768]{1,0:T(8,128)(2,1)S(1)}, bf16[20,768]{1,0:T(8,128)(2,1)}, u32[]{:S(2)}) copy-start(bf16[20,768]{1,0:T(8,128)(2,1)} %param.22) | copy-start | bytes 92164
  166.9 29.4 %copy-start.19 = (pred[1008]{0:T(1024)(128)(4,1)S(1)}, pred[1008]{0:T(1024)(128)(4,1)}, u32[]{:S(2)}) copy-start(pred[1008]{0:T(1024)(128)(4,1)} %constant.147) | copy-start | bytes 3028
  166.9 30.0 %copy-start.21 = (s32[3]{0:T(128)S(1)}, s32[3]{0:T(128)}, u32[]{:S(2)}) copy-start(s32[3]{0:T(128)} %param.25) | copy-start | bytes 40
  198.6 12.9 %copy-start.22 = (s32[1,20]{1,0:T(1,128)S(1)}, s32[1,20]{1,0:T(1,128)}, u32[]{:S(2)}) copy-start(s32[1,20]{1,0:T(1,128)} %param.26) | copy-start | bytes 244
  198.7 12.9 %copy-start.12 = (bf16[20,768]{1,0:T(8,128)(2,1)S(1)}, bf16[20,768]{1,0:T(8,128)(2,1)}, u32[]{:S(2)}) copy-start(bf16[20,768]{1,0:T(8,128)(2,1)} %param.23) | copy-start | bytes 92164
  206.6 15.6 %collective-permute-start = (bf16[32,768]{1,0:T(8,128)(2,1)}, bf16[32,768]{1,0:T(8,128)(2,1)S(1)}, u32[]{:S(2)}, u32[]{:S(2)}) collective-permute-start(bf16[32,768]{1,0:T(8,128)(2,1)} %get-tuple-element.220), channel_id=1, source_target_pairs={{0,2},{2,4},{4,6},{6,8},{8,10},{10,12},{12,14},{14,16},{16,18},{18... | collective-permute-start | bytes 147464 | tf_op jit(solution)/shard_map/ppermute | solution.py:1316
  208.5 13.7 %collective-permute-start.1 = (bf16[32,768]{1,0:T(8,128)(2,1)}, bf16[32,768]{1,0:T(8,128)(2,1)S(1)}, u32[]{:S(2)}, u32[]{:S(2)}) collective-permute-start(bf16[32,768]{1,0:T(8,128)(2,1)} %get-tuple-element.220), channel_id=1, source_target_pairs={{0,4},{2,6},{4,8},{6,10},{8,12},{10,14},{12,16},{14,18},{16,20},{1... | collective-permute-start | bytes 147464 | tf_op jit(solution)/shard_map/ppermute | solution.py:1316
  256.3 323.4 %all-gather.8.cloned.1.call-start = ((), (), s32[]{:S(2)}) async-start(), calls=%async_computation.2 | async-start | bytes 13381632 | tf_op jit(solution)/shard_map/all_gather | solution.py:1556
  288.2 38.6 %collective-permute-start.2 = (f32[32,768]{1,0:T(8,128)S(1)}, f32[32,768]{1,0:T(8,128)S(1)}, u32[]{:S(2)}, u32[]{:S(2)}) collective-permute-start(f32[32,768]{1,0:T(8,128)S(1)} %get-tuple-element.327), channel_id=1, source_target_pairs={{0,30},{2,0},{4,2},{6,4},{8,6},{10,8},{12,10},{14,12},{16,14},{18,... | collective-permute-start | bytes 294920 | tf_op jit(solution)/shard_map/ppermute | solution.py:1316
  288.3 38.6 %collective-permute-start.3 = (f32[32,768]{1,0:T(8,128)S(1)}, f32[32,768]{1,0:T(8,128)S(1)}, u32[]{:S(2)}, u32[]{:S(2)}) collective-permute-start(f32[32,768]{1,0:T(8,128)S(1)} %get-tuple-element.326), channel_id=1, source_target_pairs={{0,28},{2,30},{4,0},{6,2},{8,4},{10,6},{12,8},{14,10},{16,12},{18,... | collective-permute-start | bytes 294920 | tf_op jit(solution)/shard_map/ppermute | solution.py:1316
  337.0 27.8 %copy-start.4 = (f32[3,16,512]{2,1,0:T(8,128)S(1)}, f32[3,16,512]{2,1,0:T(8,128)}, u32[]{:S(2)}) copy-start(f32[3,16,512]{2,1,0:T(8,128)} %get-tuple-element.240.lse) | copy-start | bytes 294916
  364.8 96.9 %copy-start.20 = (s32[32]{0:T(128)S(1)}, s32[32]{0:T(128)}, u32[]{:S(2)}) copy-start(s32[32]{0:T(128)} %get-tuple-element.281) | copy-start | bytes 388
  364.8 99.2 %copy-start.14 = (f32[8,768]{1,0:T(8,128)S(1)}, f32[8,768]{1,0:T(8,128)}, u32[]{:S(2)}) copy-start(f32[8,768]{1,0:T(8,128)} %get-tuple-element.269) | copy-start | bytes 73732
  364.8 99.2 %copy-start.13 = (bf16[32,768]{1,0:T(8,128)(2,1)S(1)}, bf16[32,768]{1,0:T(8,128)(2,1)}, u32[]{:S(2)}) copy-start(bf16[32,768]{1,0:T(8,128)(2,1)} %get-tuple-element.227) | copy-start | bytes 147460
  364.8 100.6 %copy-start.15 = (f32[8,768]{1,0:T(8,128)S(1)}, f32[8,768]{1,0:T(8,128)}, u32[]{:S(2)}) copy-start(f32[8,768]{1,0:T(8,128)} %get-tuple-element.270) | copy-start | bytes 73732
  364.8 101.6 %copy-start.3 = (f32[384,32]{1,0:T(8,128)S(1)}, f32[384,32]{1,0:T(8,128)}, u32[]{:S(2)}) copy-start(f32[384,32]{1,0:T(8,128)} %get-tuple-element.273) | copy-start | bytes 147460
  364.8 101.7 %copy-start.2 = (f32[1024,32]{1,0:T(8,128)S(1)}, f32[1024,32]{1,0:T(8,128)}, u32[]{:S(2)}) copy-start(f32[1024,32]{1,0:T(8,128)} %constant.124.clone) | copy-start | bytes 393220
  491.8 77.8 %copy-start.7 = (f32[32,768]{1,0:T(8,128)S(1)}, f32[32,768]{1,0:T(8,128)}, u32[]{:S(2)}) copy-start(f32[32,768]{1,0:T(8,128)} %get-tuple-element.261) | copy-start | bytes 294916
  491.8 79.4 %copy-start.17 = (f32[168]{0:T(256)S(1)}, f32[168]{0:T(256)}, u32[]{:S(2)}) copy-start(f32[168]{0:T(256)} %param.31) | copy-start | bytes 2020
  491.9 79.4 %copy-start.18 = (f32[168]{0:T(256)S(1)}, f32[168]{0:T(256)}, u32[]{:S(2)}) copy-start(f32[168]{0:T(256)} %param.32) | copy-start | bytes 2020
  (6 other events, 46.0 us)
Sparse Core Ops, SparseCore 0:
  111.2 85.6 all-gather.3
  256.4 117.2 all-gather.5
  461.8 117.8 all-gather.7

commit v4 on v3

--- a/solution.py
+++ b/solution.py
@@ -468,7 +468,7 @@
         mixed[:, pl.ds(at, BLK)] = to_low(jnp.where(lane < HD, outs[0], outs[1]).T)
         return carry
 
-    lax.fori_loop(0, PAIRS, one_pair, 0)
+    lax.fori_loop(0, PAIRS, one_pair, 0, unroll=2)
     hidden[...] = x_ref[...].astype(f32) + dot(mixed[...], wqkv[3])
     pl.when(step == pl.num_programs(0) - 1)(lambda: keep.wait())
 

time: 611 us -> 609 us (level)
  transfers between devices with their start and end apart: 7 -> 7, of which waited for: 1 -> 2; matrix products, arithmetic and copies ran while one was open for 3% -> 3% of each run, Pallas kernels for 65% -> 64%
where the time goes in v4:
time: 609 us; the launch traced here: 605 us
  Pallas kernels  545 us (89%)
  local copies, waits for them, and re-layouts  17 us (3%)
  between operations  14.6 us (2%)
  waiting for transfers between devices  11.6 us (2%)
  other arithmetic  7.79 us (1%)
  starting transfers between devices  6.57 us (1%)
    pallas_call x1, Pallas kernels, attend_back(): pl.pallas_call(functools.partial(attend_back_kernel, plan, shard_plan, nb...  96.4 us
    pallas_call x1, Pallas kernels, gather_rows(): pl.pallas_call(functools.partial(gather_kernel, plan, nbits, rows), out_s...  96 us
    pallas_call x1, Pallas kernels, total_rows_all(): pl.pallas_call(functools.partial(total_kernel, plan, nbits, rows), out_sh...  73.6 us
    pallas_call x1, Pallas kernels, encoder_attend(): pl.pallas_call(attend_kernel, grid_spec=pltpu.PrefetchScalarGridSpec(num_...  40.2 us
    pallas_call x2, Pallas kernels, square_weight(): pl.pallas_call(functools.partial(square_weight_kernel, columns, products)...  37.4 us
    pallas_call x1, Pallas kernels, feed_back(): pl.pallas_call(feed_back_kernel, grid_spec=pltpu.PrefetchScalarGridSpec(n...  37.1 us
    pallas_call x3, Pallas kernels, decoder_call(): pl.pallas_call(body, grid_spec=pltpu.PrefetchScalarGridSpec(num_scalar_pr...  31.4 us
    pallas_call x1, Pallas kernels, encoder_feed(): pl.pallas_call(feed_kernel, grid_spec=pltpu.PrefetchScalarGridSpec(num_sc...  27.6 us
  transfers between devices with their start and end apart: 7, of which 2 were waited for; matrix products, arithmetic and copies ran while one was open for 3% of the time, Pallas kernels for 64%

profile of v4, /device:TPU:0, one launch (start us, length us, event | category | flops | bytes accessed | tf_op | source)
XLA Modules:
  0.0 604.7 jit_solution(10837413721894146785)
XLA Ops:
  10.8 4.1 ordered_shards.1
  14.9 96.0 %gather_rows.1.near.far = bf16[90624,128]{1,0:T(8,128)(2,1)} custom-call(bf16[2832,128]{1,0:T(8,128)(2,1)} %get-tuple-element.194.shard), custom_call_target="tpu_custom_call" | custom-call | tf_op jit(solution)/shard_map/gather_rows/pallas_call | solution.py:346
  113.3 8.6 %bias_strips.1.strips = f32[12,896,128]{2,1,0:T(8,128)} custom-call(f32[384]{0:T(512)} %slice_convert_fusion.3.table, s32[384,128]{1,0:T(8,128)} %constant.123.clone.buckets), custom_call_target="tpu_custom_call" | custom-call | tf_op jit(solution)/shard_map/bias_strips/pallas_call | solution.py:401
  123.7 40.2 %encoder_attend.2 = (bf16[1536,2304]{1,0:T(8,128)(2,1)}, f32[3,16,512]{2,1,0:T(8,128)}, bf16[1536,768]{1,0:T(8,128)(2,1)}, f32[1536,768]{1,0:T(8,128)}, bf16[4,768,768]{2,1,0:T(8,128)(2,1)}) custom-call(s32[1008]{0:T(1024)} %get-tuple-element.324.rows_ref, s32[3]{0:T(128)S(1)} %copy-done.9, bf16[1536,768]{1,0:T(8,128)(2,1)S(1)} %copy-done, ...), custom_call_target="tpu_custom_call" | custom-call | tf_op jit(solution)/shard_map/encoder_attend/pallas_call | solution.py:481
  164.0 27.6 %encoder_feed.2 = (bf16[1536,3072]{1,0:T(8,128)(2,1)}, f32[1536,768]{1,0:T(8,128)}, bf16[1536,768]{1,0:T(8,128)(2,1)}, bf16[768,3072]{1,0:T(8,128)(2,1)}, bf16[3072,768]{1,0:T(8,128)(2,1)}) custom-call(s32[1008]{0:T(1024)} %get-tuple-element.324.rows_ref, f32[1536,768]{1,0:T(8,128)} %get-tuple-element.455.hidden, bf16[90624,128]{1,0:T(8,128)(2,1)} %gather_rows.1.near.far, ...), custom_call_target="tpu_custom_call" | custom-call | tf_op jit(solution)/shard_map/encoder_feed/pallas_call | solution.py:560
  194.6 2.1 all-gather.4.cloned.1.call-done.far
  197.8 7.9 %decoder_self.1 = (bf16[32,2304]{1,0:T(8,128)(2,1)}, f32[32,768]{1,0:T(8,128)}, bf16[32,768]{1,0:T(8,128)(2,1)}, bf16[16,3072]{1,0:T(8,128)(2,1)}) custom-call(s32[1008]{0:T(1024)S(1)} %get-tuple-element.522, bf16[32,768]{1,0:T(8,128)(2,1)} %pad.25.dec_ref, bf16[90624,128]{1,0:T(8,128)(2,1)} %get-tuple-element.514, bf16[40960,128]{1,0:T(8,128)(2,1)} %get-tuple-element.516, ...), custom_call_target="tpu_custom_call" | custom-call | tf_op jit(solution)/shard_map/decoder_self/pallas_call | solution.py:982
  207.0 3.4 collective-permute-start.1
  211.1 10.0 %cross_memory.1.memory = bf16[1536,1536]{1,0:T(8,128)(2,1)} custom-call(s32[1008]{0:T(1024)S(1)} %get-tuple-element.522, bf16[1536,768]{1,0:T(8,128)(2,1)} %get-tuple-element.184.encoded.refs_10_, bf16[90624,128]{1,0:T(8,128)(2,1)} %get-tuple-element.514, bf16[40960,128]{1,0:T(8,128)(2,1)} %get-tuple-element.516), custom_call_target="tpu_custom_call" | custom-call | tf_op jit(solution)/shard_map/cross_memory/pallas_call | solution.py:1026
  221.8 6.6 %cross_attend.1.source = f32[3,32,1024]{2,1,0:T(8,128)} custom-call(s32[3]{0:T(128)S(1)} %get-tuple-element.537, s32[3]{0:T(128)} %and_select_fusion.offsets, bf16[3,32,768]{2,1,0:T(8,128)(2,1)} %pad_maximum_fusion.queries, bf16[1536,1536]{1,0:T(8,128)(2,1)} %cross_memory.1.memory), custom_call_target="tpu_custom_call" | custom-call | tf_op jit(solution)/shard_map/cross_attend/pallas_call | solution.py:1056
  228.4 11.5 %shift_rows.2.parts = f32[3,32,1024]{2,1,0:T(8,128)} custom-call(f32[3,32,1024]{2,1,0:T(8,128)} %cross_attend.1.source), custom_call_target="tpu_custom_call" | custom-call | tf_op jit(solution)/shard_map/shift_rows/pallas_call | solution.py:1299
  240.6 14.0 %decoder_feed.1 = (bf16[32,768]{1,0:T(8,128)(2,1)}, bf16[16,16128]{1,0:T(8,128)(2,1)}, f32[32,1024]{1,0:T(8,128)}, f32[32,768]{1,0:T(8,128)}, f32[8,768]{1,0:T(8,128)}) custom-call(s32[1008]{0:T(1024)S(1)} %get-tuple-element.522, f32[3,32,1024]{2,1,0:T(8,128)} %shift_rows.2.parts, f32[32,768]{1,0:T(8,128)} %get-tuple-element.225.first, ...), custom_call_target="tpu_custom_call" | custom-call | tf_op jit(solution)/shard_map/decoder_feed/pallas_call | solution.py:982
  254.7 12.6 %shift_rows.3.back = f32[3,32,1024]{2,1,0:T(8,128)} custom-call(f32[32,1024]{1,0:T(8,128)} %get-tuple-element.234.source), custom_call_target="tpu_custom_call" | custom-call | tf_op jit(solution)/shard_map/shift_rows/pallas_call | solution.py:1299
  267.3 17.4 %cross_back.1 = (bf16[1536,1536]{1,0:T(8,128)(2,1)}, f32[3,32,768]{2,1,0:T(8,128)}, f32[1536,768]{1,0:T(8,128)}) custom-call(s32[1008]{0:T(1024)S(1)} %get-tuple-element.522, s32[3]{0:T(128)S(1)} %get-tuple-element.537, s32[3]{0:T(128)} %and_select_fusion.offsets, bf16[3,32,768]{2,1,0:T(8,128)(2,1)} %pad_maximum_fusion.queries, ...), custom_call_target="tpu_custom_call" | custom-call | tf_op jit(solution)/shard_map/cross_back/pallas_call | solution.py:1184
  284.7 1.7 slice_bitcast_fusion.1
  288.0 37.1 %feed_back.1 = (bf16[1536,3072]{1,0:T(8,128)(2,1)}, bf16[1536,3072]{1,0:T(8,128)(2,1)}, bf16[1536,768]{1,0:T(8,128)(2,1)}, bf16[1536,768]{1,0:T(8,128)(2,1)}, f3...) custom-call(f32[1536,768]{1,0:T(8,128)} %get-tuple-element.229.output, ...), custom_call_target="tpu_custom_call" | custom-call | tf_op jit(solution)/shard_map/feed_back/pallas_call | solution.py:652
  325.8 9.4 %decoder_self_back.1 = (f32[32,768]{1,0:T(8,128)}, bf16[768,128]{1,0:T(8,128)(2,1)}, f32[384,32]{1,0:T(8,128)}, f32[8,768]{1,0:T(8,128)}) custom-call(s32[1008]{0:T(1024)S(1)} %get-tuple-element.522, f32[32,768]{1,0:T(8,128)} %get-tuple-element.250.part_zero, f32[32,768]{1,0:T(8,128)} %copy-done.5, f32[32,768]{1,0:T(8,128)} %copy-done.6, ...), custom_call_target="tpu_custom_call" | custom-call | tf_op jit(solution)/shard_map/decoder_self_back/pallas_call | solution.py:982
  335.2 27.8 %square_weight.2.refs_0_ = bf16[50688,128]{1,0:T(8,128)(2,1)} custom-call(bf16[1536,768]{1,0:T(8,128)(2,1)} %get-tuple-element.241.refs_0_, bf16[1536,3072]{1,0:T(8,128)(2,1)} %get-tuple-element.244.refs_1_.refs_2_.refs_3_.refs_4_, bf16[1536,3072]{1,0:T(8,128)(2,1)} %get-tuple-element.244.refs_1_.refs_2_.refs_3_.refs_4_, ...), custom_call_target="tpu_custom_call" | custom-call | tf_op jit(solution)/shard_map/square_weight/pallas_call | solution.py:1364
  363.1 96.4 %attend_back.1 = (bf16[1536,768]{1,0:T(8,128)(2,1)}, bf16[1536,768]{1,0:T(8,128)(2,1)}, bf16[1536,768]{1,0:T(8,128)(2,1)}, f32[6,8,128]{2,1,0:T(8,128)}, bf16[15...) custom-call(s32[3]{0:T(128)S(1)} %get-tuple-element.537, bf16[1536,2304]{1,0:T(8,128)(2,1)} %get-tuple-element.228.q_ref.k_ref.v_ref, ...), custom_call_target="tpu_custom_call" | custom-call | tf_op jit(solution)/shard_map/attend_back/pallas_call | solution.py:813
  465.0 15.0 %input_back.1 = (f32[1536,768]{1,0:T(8,128)}, bf16[1536,768]{1,0:T(8,128)(2,1)}, f32[8,768]{1,0:T(8,128)}) custom-call(bf16[1536,768]{1,0:T(8,128)(2,1)S(1)} %get-tuple-element.518, bf16[1536,768]{1,0:T(8,128)(2,1)} %get-tuple-element.256.gq.refs_1_, bf16[1536,768]{1,0:T(8,128)(2,1)} %get-tuple-element.257.gk.refs_2_, ...), custom_call_target="tpu_custom_call" | custom-call | tf_op jit(solution)/shard_map/input_back/pallas_call | solution.py:866
  480.1 9.6 %square_weight.3 = bf16[14336,128]{1,0:T(8,128)(2,1)} custom-call(bf16[1536,768]{1,0:T(8,128)(2,1)} %get-tuple-element.267.refs_0_, bf16[1536,768]{1,0:T(8,128)(2,1)} %get-tuple-element.256.gq.refs_1_, bf16[1536,768]{1,0:T(8,128)(2,1)} %get-tuple-element.257.gk.refs_2_, bf16[1536,768]{1,0:T(8,128)(2,1)} %get-tuple-element.258.gv.refs_3_), custom_call_target="tpu_custom_call" | custom-call | tf_op jit(solution)/shard_map/square_weight/pallas_call | solution.py:1364
  492.9 73.6 %total_rows.1.two = bf16[14336,128]{1,0:T(8,128)(2,1)} custom-call(bf16[14336,128]{1,0:T(8,128)(2,1)} %pad_dynamic-update-slice_fusion.terms), custom_call_target="tpu_custom_call" | custom-call | tf_op jit(solution)/shard_map/total_rows/pallas_call | solution.py:378
  568.8 9.3 %all-gather.8.cloned.1.call-done.one = bf16[50688,128]{1,0:T(8,128)(2,1)} async-done(((bf16[1584,128]{1,0:T(8,128)(2,1)}), bf16[50688,128]{1,0:T(8,128)(2,1)}) %all-gather.8.cloned.1.call-update) | async-done | bytes 12976144 | tf_op jit(solution)/shard_map/all_gather | solution.py:1556
  578.1 19.8 %update_blocks.1 = (f32[32,128,128]{2,1,0:T(8,128)}, f32[32,2,128,128]{3,2,1,0:T(8,128)}, f32[32,128,128]{2,1,0:T(8,128)}) custom-call(s32[256]{0:T(256)} %reshape.127.info, bf16[32,16,16128]{2,1,0:T(8,128)(2,1)} %bitcast.36, bf16[32,768,128]{2,1,0:T(8,128)(2,1)} %bitcast.37, bf16[50688,128]{1,0:T(8,128)(2,1)} %all-gather.8.cloned.1.call-done.one, ...), custom_call_target="tpu_custom_call" | custom-call | tf_op jit(solution)/shard_map/update_blocks/pallas_call | solution.py:1493
  (121 shorter events, 28.2 us)
Async XLA Ops:
  7.2 189.6 %all-gather.4.cloned.1.call-start = ((), (), s32[]{:S(2)}) async-start(), calls=%async_computation | async-start | bytes 10813440 | tf_op jit(solution)/shard_map/all_gather | solution.py:1556
  111.0 12.7 %copy-start = (bf16[1536,768]{1,0:T(8,128)(2,1)S(1)}, bf16[1536,768]{1,0:T(8,128)(2,1)}, u32[]{:S(2)}) copy-start(bf16[1536,768]{1,0:T(8,128)(2,1)} %x_ref.3) | copy-start | bytes 7077892
  111.0 12.7 %copy-start.9 = (s32[3]{0:T(128)S(1)}, s32[3]{0:T(128)}, u32[]{:S(2)}) copy-start(s32[3]{0:T(128)} %lengths.7) | copy-start | bytes 40
  111.0 348.4 %all-gather.6.cloned.1.call-start = ((), (), s32[]{:S(2)}) async-start(), calls=%async_computation.1 | async-start | bytes 17031168 | tf_op jit(solution)/shard_map/all_gather | solution.py:1556
  163.9 27.6 %copy-start.1 = (f32[1024,32]{1,0:T(8,128)S(1)}, f32[1024,32]{1,0:T(8,128)}, u32[]{:S(2)}) copy-start(f32[1024,32]{1,0:T(8,128)} %constant.124.clone) | copy-start | bytes 393220
  163.9 28.8 %copy-start.11 = (bf16[20,768]{1,0:T(8,128)(2,1)S(1)}, bf16[20,768]{1,0:T(8,128)(2,1)}, u32[]{:S(2)}) copy-start(bf16[20,768]{1,0:T(8,128)(2,1)} %param.22) | copy-start | bytes 92164
  163.9 29.4 %copy-start.19 = (pred[1008]{0:T(1024)(128)(4,1)S(1)}, pred[1008]{0:T(1024)(128)(4,1)}, u32[]{:S(2)}) copy-start(pred[1008]{0:T(1024)(128)(4,1)} %constant.147) | copy-start | bytes 3028
  163.9 30.0 %copy-start.21 = (s32[3]{0:T(128)S(1)}, s32[3]{0:T(128)}, u32[]{:S(2)}) copy-start(s32[3]{0:T(128)} %param.25) | copy-start | bytes 40
  197.8 12.6 %copy-start.22 = (s32[1,20]{1,0:T(1,128)S(1)}, s32[1,20]{1,0:T(1,128)}, u32[]{:S(2)}) copy-start(s32[1,20]{1,0:T(1,128)} %param.26) | copy-start | bytes 244
  205.7 15.4 %collective-permute-start = (bf16[32,768]{1,0:T(8,128)(2,1)}, bf16[32,768]{1,0:T(8,128)(2,1)S(1)}, u32[]{:S(2)}, u32[]{:S(2)}) collective-permute-start(bf16[32,768]{1,0:T(8,128)(2,1)} %get-tuple-element.220), channel_id=1, source_target_pairs={{0,2},{2,4},{4,6},{6,8},{8,10},{10,12},{12,14},{14,16},{16,18},{18... | collective-permute-start | bytes 147464 | tf_op jit(solution)/shard_map/ppermute | solution.py:1316
  207.0 14.1 %collective-permute-start.1 = (bf16[32,768]{1,0:T(8,128)(2,1)}, bf16[32,768]{1,0:T(8,128)(2,1)S(1)}, u32[]{:S(2)}, u32[]{:S(2)}) collective-permute-start(bf16[32,768]{1,0:T(8,128)(2,1)} %get-tuple-element.220), channel_id=1, source_target_pairs={{0,4},{2,6},{4,8},{6,10},{8,12},{10,14},{12,16},{14,18},{16,20},{1... | collective-permute-start | bytes 147464 | tf_op jit(solution)/shard_map/ppermute | solution.py:1316
  254.6 323.5 %all-gather.8.cloned.1.call-start = ((), (), s32[]{:S(2)}) async-start(), calls=%async_computation.2 | async-start | bytes 13381632 | tf_op jit(solution)/shard_map/all_gather | solution.py:1556
  286.4 38.7 %collective-permute-start.2 = (f32[32,768]{1,0:T(8,128)S(1)}, f32[32,768]{1,0:T(8,128)S(1)}, u32[]{:S(2)}, u32[]{:S(2)}) collective-permute-start(f32[32,768]{1,0:T(8,128)S(1)} %get-tuple-element.327), channel_id=1, source_target_pairs={{0,30},{2,0},{4,2},{6,4},{8,6},{10,8},{12,10},{14,12},{16,14},{18,... | collective-permute-start | bytes 294920 | tf_op jit(solution)/shard_map/ppermute | solution.py:1316
  286.7 38.4 %collective-permute-start.3 = (f32[32,768]{1,0:T(8,128)S(1)}, f32[32,768]{1,0:T(8,128)S(1)}, u32[]{:S(2)}, u32[]{:S(2)}) collective-permute-start(f32[32,768]{1,0:T(8,128)S(1)} %get-tuple-element.326), channel_id=1, source_target_pairs={{0,28},{2,30},{4,0},{6,2},{8,4},{10,6},{12,8},{14,10},{16,12},{18,... | collective-permute-start | bytes 294920 | tf_op jit(solution)/shard_map/ppermute | solution.py:1316
  335.2 27.8 %copy-start.4 = (f32[3,16,512]{2,1,0:T(8,128)S(1)}, f32[3,16,512]{2,1,0:T(8,128)}, u32[]{:S(2)}) copy-start(f32[3,16,512]{2,1,0:T(8,128)} %get-tuple-element.240.lse) | copy-start | bytes 294916
  363.0 96.5 %copy-start.20 = (s32[32]{0:T(128)S(1)}, s32[32]{0:T(128)}, u32[]{:S(2)}) copy-start(s32[32]{0:T(128)} %get-tuple-element.281) | copy-start | bytes 388
  363.0 98.8 %copy-start.14 = (f32[8,768]{1,0:T(8,128)S(1)}, f32[8,768]{1,0:T(8,128)}, u32[]{:S(2)}) copy-start(f32[8,768]{1,0:T(8,128)} %get-tuple-element.269) | copy-start | bytes 73732
  363.0 98.8 %copy-start.13 = (bf16[32,768]{1,0:T(8,128)(2,1)S(1)}, bf16[32,768]{1,0:T(8,128)(2,1)}, u32[]{:S(2)}) copy-start(bf16[32,768]{1,0:T(8,128)(2,1)} %get-tuple-element.227) | copy-start | bytes 147460
  363.0 100.2 %copy-start.15 = (f32[8,768]{1,0:T(8,128)S(1)}, f32[8,768]{1,0:T(8,128)}, u32[]{:S(2)}) copy-start(f32[8,768]{1,0:T(8,128)} %get-tuple-element.270) | copy-start | bytes 73732
  363.0 101.2 %copy-start.3 = (f32[384,32]{1,0:T(8,128)S(1)}, f32[384,32]{1,0:T(8,128)}, u32[]{:S(2)}) copy-start(f32[384,32]{1,0:T(8,128)} %get-tuple-element.273) | copy-start | bytes 147460
  363.1 101.4 %copy-start.2 = (f32[1024,32]{1,0:T(8,128)S(1)}, f32[1024,32]{1,0:T(8,128)}, u32[]{:S(2)}) copy-start(f32[1024,32]{1,0:T(8,128)} %constant.124.clone) | copy-start | bytes 393220
  489.7 76.8 %copy-start.7 = (f32[32,768]{1,0:T(8,128)S(1)}, f32[32,768]{1,0:T(8,128)}, u32[]{:S(2)}) copy-start(f32[32,768]{1,0:T(8,128)} %get-tuple-element.261) | copy-start | bytes 294916
  489.7 78.4 %copy-start.17 = (f32[168]{0:T(256)S(1)}, f32[168]{0:T(256)}, u32[]{:S(2)}) copy-start(f32[168]{0:T(256)} %param.31) | copy-start | bytes 2020
  489.7 78.4 %copy-start.18 = (f32[168]{0:T(256)S(1)}, f32[168]{0:T(256)}, u32[]{:S(2)}) copy-start(f32[168]{0:T(256)} %param.32) | copy-start | bytes 2020
  (6 other events, 45.9 us)
Sparse Core Ops, SparseCore 0:
  111.2 85.5 all-gather.3
  254.8 117.0 all-gather.5
  459.6 118.4 all-gather.7
